TPU v7x, 256 devices: a whole 4x4x8 slice. The times are simulated.
256 devices in a mesh: chan: 64 (over y_hi, x, z), win: 4 (over y_lo, core).
Axes of the slice: x: 4, y: 4 (y_hi: 2, y_lo: 2; y = y_hi * 2 + y_lo), z: 8, core: 2. Of those that a mesh axis runs over, the one named last changes fastest.
Arguments:
- spectra: bfloat16 [64, 128, 128, 2, 128], P('chan', None, 'win'), may hold values from -6 to 6
- counts: int32 [128, 64], P('win'), may hold values from 1 to 256
- partner: int32 [2, 64], replicated, may hold values from 0 to 63, as said below
Outputs:
- cross: bfloat16 [64, 2, 128, 128, 256], P('win', None, 'chan')
Inputs may be any that keep to these rules, and one draw needn't show every extreme that they name: Each row of partner is one cycle through all 64 blocks: a permutation with no block its own partner and no two blocks each other's partners.
All inputs are finite; a program needn't handle non-finite values.
Results may differ from a plain program's by a relative error of at most 0.015.
Values may be sent and summed in bfloat16 or wider, within the bound.
No kernel may reach another device: no remote copies, remote signals or barrier semaphores. Data moves between devices by JAX's collectives and lax.ppermute only.
A program may use at most 128 MiB of HBM per device.

v0:
```python
import jax
import jax.numpy as jnp
from jax import lax
from jax.sharding import PartitionSpec as P

W_DEV = 32
NSAMP = 256


EPS = 1e-06


def stack_blocks(blocks, scale, mate_index, first, count):
    own = lax.dynamic_slice_in_dim(blocks, first, count, 0)
    mates = jnp.take(blocks, mate_index, axis=0)
    weighted = (scale[:, :, None, :, :, None, None] * own[:, None]).astype(jnp.bfloat16)
    rotated = jnp.stack([-mates[..., 1, :], mates[..., 0, :]], axis=-2)
    paired = jnp.stack([mates, rotated], axis=-2)
    return jnp.einsum(
        "nrfgwkc,nrfgwkod->nrfgcod", weighted, paired, preferred_element_type=jnp.float32
    )


def weights_of(tallies, partner):
    columns = tallies.astype(jnp.float32).T
    return jnp.minimum(columns[None], jnp.take(columns, partner, axis=0)) / NSAMP


def per_device(spectra, counts, partner):
    values = spectra.astype(jnp.float32)
    power = jnp.mean(jnp.sum(values * values, axis=3), axis=1)
    whitened = (values * lax.rsqrt(power + EPS)[:, None, :, None, :]).astype(jnp.bfloat16)
    mixed = lax.all_to_all(whitened, "chan", split_axis=1, concat_axis=0, tiled=True)
    nblocks = partner.shape[1]
    width = mixed.shape[4]
    local_bins = mixed.shape[1]
    rounds = partner.shape[0]
    groups = lax.axis_size("win")
    chosen = nblocks // groups
    first = lax.axis_index("win") * chosen
    gathered = lax.all_gather(mixed, "win", axis=2, tiled=True)
    tallies = lax.all_gather(counts, "win", axis=0, tiled=True)
    weight = weights_of(tallies, partner)
    norm = jnp.sqrt(jnp.sum(weight * weight, axis=2))
    blocks = gathered.reshape(nblocks, local_bins, groups, W_DEV, 2, width)
    own_scales = jnp.transpose(lax.dynamic_slice_in_dim(weight, first, chosen, 1), (1, 0, 2))
    scale = own_scales.reshape(chosen, rounds, groups, W_DEV)
    mate_index = jnp.transpose(lax.dynamic_slice_in_dim(partner, first, chosen, 1))
    partial_value = stack_blocks(blocks, scale, mate_index, first, chosen)
    partial_value = lax.optimization_barrier(partial_value.astype(jnp.bfloat16))
    total = jnp.sum(partial_value.astype(jnp.float32), axis=3)
    norm_rows = jnp.transpose(lax.dynamic_slice_in_dim(norm, first, chosen, 1))
    shaped = total.reshape(chosen, rounds, local_bins, width, 2 * width)
    result = shaped / norm_rows[:, :, None, None, None]
    return result.astype(jnp.bfloat16)


def solution(mesh):
    placed = (P("chan", None, "win", None, None), P("win", None), P())
    return jax.shard_map(
        per_device,
        mesh=mesh,
        in_specs=placed,
        out_specs=P("win", None, "chan", None, None),
        check_vma=False,
    )
```

profile of v0, /device:TPU:1, one launch (start us, length us, event | category | flops | bytes accessed | tf_op | source)
XLA Modules:
  0.0 240.4 jit_solution(3108517690756288380)
XLA Ops:
  6.5 3.8 %fusion.4 = f32[32,128]{1,0:T(8,128)S(1)} fusion(bf16[1,128,32,2,128]{4,3,2,1,0:T(2,128)(2,1)} %param.3), kind=kLoop, calls=%fused_computation.12 | loop fusion | flops 3141632 | bytes 2113536 | tf_op jit(solution)/shard_map/reduce_sum | solution.py:31
  10.4 3.8 %fusion.5 = bf16[1,128,32,2,128]{4,3,2,0,1:T(2,128)(2,1)S(1)} fusion(bf16[1,128,32,2,128]{4,3,2,1,0:T(2,128)(2,1)} %param.3, f32[32,128]{1,0:T(8,128)S(1)} %add_rsqrt_fusion), kind=kLoop, calls=%fused_computation.13 | loop fusion | flops 3145728 | bytes 4210688 | tf_op jit(solution)/shard_map/convert_element_type | solution.py:32
  14.2 63.5 %all_to_all.12 = bf16[1,128,32,2,128]{4,3,2,0,1:T(2,128)(2,1)S(1)} all-to-all(bf16[1,128,32,2,128]{4,3,2,0,1:T(2,128)(2,1)S(1)} %fusion.5), channel_id=1, replica_groups=mesh['chan'=64,'win'=4] {'chan'}, dimensions={1} | all-to-all | bytes 4194304 | tf_op jit(solution)/shard_map/all_to_all | solution.py:33
  77.7 1.9 copy.36
  79.8 0.1 reshape.56
  79.9 0.1 copy.38
  80.0 9.0 %all_gather.6 = s32[128,64]{1,0:T(8,128)S(1)} all-gather(s32[32,64]{1,0:T(8,128)S(1)} %copy-done.1), channel_id=1, replica_groups=mesh['chan'=64,'win'=4] {'win'}, dimensions={0}, use_global_device_ids=true | all-gather | bytes 40960 | tf_op jit(solution)/shard_map/all_gather | solution.py:42
  89.1 0.1 reshape.48
  89.2 0.6 gather_fusion
  89.9 0.2 multiply_reduce_fusion
  90.1 0.1 mul.33
  90.3 72.9 %all-gather.2.cloned.1.call-done = bf16[64,2,128,2,128]{4,2,3,1,0:T(8,128)(2,1)} async-done(((bf16[64,2,32,2,128]{4,2,3,1,0:T(8,128)(2,1)}), bf16[64,2,128,2,128]{4,2,3,1,0:T(8,128)(2,1)}) %all-gather.2.cloned.1.call-update) | async-done | bytes 8388624 | tf_op jit(solution)/shard_map/all_gather | solution.py:41
  163.2 9.2 %copy.40 = bf16[64,2,4,32,2,128]{5,3,4,2,1,0:T(8,128)(2,1)} copy(bf16[64,2,4,32,2,128]{5,3,2,4,1,0:T(8,128)(2,1)} %bitcast.35) | data formatting | bytes 16777216 | tf_op jit(solution)/shard_map/reshape | solution.py:45
  172.4 6.5 %gather_fusion.1 = bf16[32,2,4,32,2,128]{5,3,4,2,1,0:T(8,128)(2,1)} fusion(bf16[64,2,4,32,2,128]{5,3,4,2,1,0:T(8,128)(2,1)} %copy.40, s32[1024]{0:T(1024)S(1)} %pad_clamp_fusion), kind=kCustom, calls=%fused_computation.1 | custom fusion | bytes 8388736 | tf_op jit(solution)/shard_map/jit(_take)/gather | solution.py:15
  178.8 2.6 %broadcast_select_fusion = bf16[16,2,2,4,32,2,128]{6,4,5,3,2,1,0:T(8,128)(2,1)S(1)} fusion(bf16[16,2,2,4,32,2,128]{6,4,5,3,2,1,0:T(8,128)(2,1)} %bitcast.33, pred[16,2]{1,0:T(8,128)(4,1)S(1)} %copy.38), kind=kLoop, calls=%fused_computation.18 | loop fusion | flops 2097152 | bytes 8388640 | tf_op jit(solution)/shard_map/jit(_take)/select_n | solution.py:15
  181.5 0.4 slice_negate_fusion
  181.9 1.8 copy-done
  183.7 0.5 broadcast_select_fusion.1
  184.2 2.4 maximum_bitcast_fusion
  186.5 11.9 %bitcast_convert_fusion = bf16[16,2,2,4,128,2,128]{6,4,5,3,2,1,0:T(8,128)(2,1)} fusion(bf16[16,2,2,4,32,2,1,128]{7,4,5,6,3,2,1,0:T(8,128)(2,1)} %maximum_bitcast_fusion, bf16[16,2,2,4,32,2,1,128]{7,4,5,6,3,2,1,0:T(8,128)(2,1)S(1)} %broadcast_select_fusion.1, f32[16,2,4,32]{3,2,0,1:T(4,128)S(1)} %mul.33, bf16[64,2,4,32,2,128]{5,3,2,4,1,0:T(8,128)(2,1)} %bitcast.36, ...), kind=kOutput, calls=%fused_computation.2 | convolution fusion | flops 1104150528 | bytes 27279364 | tf_op jit(solution)/shard_map/nrfgwkc,nrfgwkod->nrfgcod/dot_general | solution.py:19
  198.4 13.0 %convert_reduce_fusion = f32[16,2,2,128,2,128]{5,3,4,2,1,0:T(8,128)} fusion(bf16[16,2,2,4,128,2,128]{6,4,5,3,2,1,0:T(8,128)(2,1)} %bitcast_convert_fusion), kind=kLoop, calls=%fused_computation.3 | loop fusion | flops 14680064 | bytes 25165824 | tf_op jit(solution)/shard_map/reduce_sum | solution.py:51
  211.4 9.3 %copy.42 = f32[16,2,2,128,2,128]{3,5,4,2,1,0:T(8,128)} copy(f32[16,2,2,128,2,128]{5,3,4,2,1,0:T(8,128)} %convert_reduce_fusion) | data formatting | bytes 16777216 | tf_op jit(solution)/shard_map/reduce_sum | solution.py:51
  220.7 6.5 %fusion.3 = bf16[16,2,2,128,256]{3,4,2,1,0:T(8,128)(2,1)} fusion(f32[16,2,2,128,2,128]{3,5,4,2,1,0:T(8,128)} %copy.42, f32[16,2]{1,0:T(8,128)S(1)} %copy.43), kind=kLoop, calls=%fused_computation.8 | loop fusion | flops 4194304 | bytes 12583040 | tf_op jit(solution)/shard_map/convert_element_type | solution.py:55
  227.2 6.4 %copy.44 = bf16[16,2,2,128,256]{4,3,2,1,0:T(8,128)(2,1)} copy(bf16[16,2,2,128,256]{3,4,2,1,0:T(8,128)(2,1)} %fusion.3) | data formatting | bytes 8388608 | tf_op jit(solution)/shard_map/convert_element_type | solution.py:55
  (20 shorter events, 0.5 us)
Async XLA Ops:
  6.5 156.7 %all-gather.2.cloned.1.call-start = ((), (), s32[]{:S(2)}) async-start(), calls=%async_computation.1 | async-start | bytes 10485760 | tf_op jit(solution)/shard_map/all_gather | solution.py:41
  77.7 1.9 copy-start.2
  77.7 2.3 copy-start.1
  181.5 2.2 copy-start
Sparse Core Ops, SparseCore 0:
  79.7 83.4 all-gather.1
where the time goes:
time: 241 us; the launch traced here: 240 us
  waiting for transfers between devices  72.9 us (30%)
  blocking collectives  72.6 us (30%)
  local copies, waits for them, and re-layouts  36.3 us (15%)
  other arithmetic  33.3 us (14%)
  between operations  13.5 us (6%)
  matrix products  11.9 us (5%)
    all_gather x1, waiting for transfers between devices, per_device(): gathered = lax.all_gather(mixed, 'win', axis=2, tiled=True)  72.9 us
    all_to_all x1, blocking collectives, per_device(): lax.all_to_all(whitened, 'chan', split_axis=1, concat_axis=0, tiled=True)  63.5 us
    reduce_sum x1, other arithmetic, per_device(): total = jnp.sum(partial_value.astype(jnp.float32), axis=3)  13 us
    dot_general x1, matrix products, stack_blocks(): jnp.einsum('nrfgwkc,nrfgwkod->nrfgcod', weighted, paired, preferred_eleme...  11.9 us
    reduce_sum x1, local copies, waits for them, and re-layouts, per_device(): total = jnp.sum(partial_value.astype(jnp.float32), axis=3)  9.27 us
    reshape x1, local copies, waits for them, and re-layouts, per_device(): blocks = gathered.reshape(nblocks, local_bins, groups, W_DEV, 2, width)  9.15 us
    all_gather x1, blocking collectives, per_device(): tallies = lax.all_gather(counts, 'win', axis=0, tiled=True)  9.03 us
    convert_element_type x1, other arithmetic, per_device(): return result.astype(jnp.bfloat16)  6.5 us
  transfers between devices with their start and end apart: 1, of which 1 were waited for; matrix products, arithmetic and copies ran while one was open for 1% of the time, Pallas kernels for 0%

commit v1 on v0

v1 whole, which is shorter than its diff:
```python
import functools

import jax
import jax.numpy as jnp
from jax import lax
from jax.experimental import pallas as pl
from jax.experimental.pallas import tpu as pltpu
from jax.sharding import PartitionSpec as P

NSAMP = 256
EPS = 1e-06


def whiten_kernel(x_ref, first_ref, second_ref):
    bins, rows, width = x_ref.shape
    step = 4

    def add(i, total):
        for j in range(step):
            values = x_ref[i * step + j].astype(jnp.float32)
            total = total + values * values
        return total

    total = lax.fori_loop(0, bins // step, add, jnp.zeros((rows, width), jnp.float32))
    even = lax.broadcasted_iota(jnp.int32, (rows, width), 0) % 2 == 0
    other = jnp.where(even, pltpu.roll(total, rows - 1, 0), pltpu.roll(total, 1, 0))
    scale = lax.rsqrt((total + other) / bins + EPS)

    def put(i, carry):
        for j in range(step):
            first_ref[i * step + j] = (x_ref[(i * step + j) * 2].astype(jnp.float32) * scale).astype(first_ref.dtype)
            second_ref[i * step + j] = (x_ref[(i * step + j) * 2 + 1].astype(jnp.float32) * scale).astype(first_ref.dtype)
        return carry

    lax.fori_loop(0, bins // 2 // step, put, 0)


def whiten(spectra):
    bins, rows, width = spectra.shape
    half = jax.ShapeDtypeStruct((bins // 2, rows, width), spectra.dtype)
    return pl.pallas_call(
        whiten_kernel,
        out_shape=(half, half),
        in_specs=[pl.BlockSpec(memory_space=pltpu.VMEM)],
        out_specs=[pl.BlockSpec(memory_space=pltpu.VMEM)] * 2,
        compiler_params=pltpu.CompilerParams(vmem_limit_bytes=24 << 20),
        name="whiten",
    )(spectra)


def stack_kernel(chosen, mates_ref, first_ref, weight_ref, norm_ref, *refs):
    sources, out_ref = refs[:4], refs[-1]
    n = pl.program_id(0)
    own = jnp.concatenate([s[first_ref[0] + n] for s in sources], axis=0)
    rows, width = own.shape
    real = own.astype(jnp.float32).T
    even = lax.broadcasted_iota(jnp.int32, (width, rows), 1) % 2 == 0
    turned = jnp.where(even, pltpu.roll(real, rows - 1, 1), -pltpu.roll(real, 1, 1))
    both = jnp.concatenate([real, turned], axis=0)
    for r in range(2):
        mate = jnp.concatenate([s[mates_ref[r * chosen + n]] for s in sources], axis=0)
        left = (both * weight_ref[0, r][None, :]).astype(jnp.bfloat16)
        total = lax.dot_general(left, mate, (((1,), (0,)), ((), ())), preferred_element_type=jnp.float32)
        total = (total * (1.0 / norm_ref[r * chosen + n])).astype(out_ref.dtype)
        out_ref[0, r, 0, :, :width] = total[:width]
        out_ref[0, r, 0, :, width:] = total[width:]


def stack(which, sources, mates, first, weight, norm, into):
    chosen, rounds, rows = weight.shape
    width = sources[0].shape[-1]
    out = jax.ShapeDtypeStruct((chosen, rounds, 2, width, 2 * width), jnp.bfloat16)
    smem = pl.BlockSpec(memory_space=pltpu.SMEM)
    vmem = pl.BlockSpec(memory_space=pltpu.VMEM)
    more = () if into is None else (into,)
    return pl.pallas_call(
        functools.partial(stack_kernel, chosen),
        out_shape=out,
        grid=(chosen,),
        in_specs=[smem, smem, pl.BlockSpec((1, rounds, rows), lambda n: (n, 0, 0)), smem]
        + [vmem] * 4
        + [pl.BlockSpec(memory_space=pl.ANY)] * len(more),
        out_specs=pl.BlockSpec((1, rounds, 1, width, 2 * width), lambda n: (n, 0, which, 0, 0)),
        input_output_aliases={8: 0} if more else {},
        compiler_params=pltpu.CompilerParams(vmem_limit_bytes=24 << 20),
        cost_estimate=pl.CostEstimate(flops=2 * chosen * rounds * 2 * width * rows * width, bytes_accessed=8 << 20, transcendentals=0),
        name="stack" + str(which),
    )(mates, first, weight, norm, *sources, *more)


def per_device(spectra, counts, partner):
    bins, windows, parts, width = spectra.shape[1:]
    nblocks = partner.shape[1]
    rounds = partner.shape[0]
    groups = lax.axis_size("win")
    chosen = nblocks // groups
    me = lax.axis_index("win")
    first = me * chosen

    def swap(x, mask):
        return lax.ppermute(x, "win", [(i, i ^ mask) for i in range(groups)])

    halves = whiten(spectra.reshape(bins, windows * parts, width))
    tallies = [counts, swap(counts, 2), swap(counts, 1), swap(counts, 3)]

    mixed = [lax.all_to_all(h, "chan", split_axis=0, concat_axis=0, tiled=True) for h in halves]
    gathered = []
    for m in mixed:
        y = swap(m, 2)
        gathered.append((m, y, swap(m, 1), swap(y, 1)))

    columns = jnp.concatenate(tallies, axis=0).astype(jnp.float32)
    mine = lax.dynamic_slice_in_dim(partner, first, chosen, 1)
    one_hot = (mine.reshape(rounds * chosen, 1) == jnp.arange(nblocks, dtype=jnp.int32)[None]).astype(jnp.float32)
    own_hot = (first + jnp.arange(chosen, dtype=jnp.int32)[:, None] == jnp.arange(nblocks, dtype=jnp.int32)[None]).astype(jnp.float32)
    pick = functools.partial(jnp.einsum, "nb,wb->nw", precision=lax.Precision.HIGHEST)
    theirs = pick(one_hot, columns).reshape(rounds, chosen, -1)
    ours = pick(own_hot, columns)
    weight = jnp.minimum(ours[None], theirs) / NSAMP
    norm = jnp.sqrt(jnp.sum(weight * weight, axis=2)).reshape(rounds * chosen)
    wide = jnp.repeat(jnp.transpose(weight, (1, 0, 2)), parts, axis=2)

    result = None
    for which in range(2):
        result = stack(which, gathered[which], mine.reshape(-1), first.reshape(1).astype(jnp.int32), wide, norm, result)
    return result


def solution(mesh):
    placed = (P("chan", None, "win", None, None), P("win", None), P())
    return jax.shard_map(
        per_device,
        mesh=mesh,
        in_specs=placed,
        out_specs=P("win", None, "chan", None, None),
        check_vma=False,
    )
```

time: 241 us -> 144 us (0.60)
  other arithmetic: 33.3 us -> 0.01 us
  local copies, waits for them, and re-layouts: 36.3 us -> 3.62 us
  blocking collectives: 72.6 us -> 42.9 us
  Pallas kernels: 0 us -> 22.4 us
  starting transfers between devices: 0.01 us -> 20.8 us
  waiting for transfers between devices: 72.9 us -> 53.5 us
  between operations: 13.5 us -> 0.06 us
  matrix products: 11.9 us -> 0.55 us
    all_gather x1 -> x0, waiting for transfers between devices: 72.9 us -> none  [per_device(): gathered = lax.all_gather(mixed, 'win', axis=2, tiled=True)]
    ppermute x0 -> x9, waiting for transfers between devices: none -> 27.7 us  [swap(): return lax.ppermute(x, 'win', [(i, i ^ mask) for i in range(groups)])]
    all_to_all x0 -> x1, waiting for transfers between devices: none -> 25.9 us  [per_device(): lax.all_to_all(h, 'chan', split_axis=0, concat_axis=0, tiled=True)]
    pallas_call x0 -> x3, Pallas kernels: none -> 22.4 us  [the longest x2 20.5 us: stack(): pl.pallas_call(functools.partial(stack_kernel, chosen), out_shape=out, gr...]
    all_to_all x1, blocking collectives: 63.5 us -> 42.9 us  [per_device(): lax.all_to_all(h, 'chan', split_axis=0, concat_axis=0, tiled=True)]
    reduce_sum x3 -> x0, other arithmetic: 17 us -> none  [the longest x1 13 us: per_device(): total = jnp.sum(partial_value.astype(jnp.float32), axis=3)]
    ppermute x0 -> x9, starting transfers between devices: none -> 13.3 us  [swap(): return lax.ppermute(x, 'win', [(i, i ^ mask) for i in range(groups)])]
    dot_general x1 -> x2, matrix products: 11.9 us -> 0.55 us  [the longest x1 0.39 us: per_device(): theirs = pick(one_hot, columns).reshape(rounds, chosen, -1)]
  transfers between devices with their start and end apart: 1 -> 10, of which waited for: 1 -> 6; matrix products, arithmetic and copies ran while one was open for 1% -> 2% of each run, Pallas kernels for 0% -> 7%
where the time goes in v1:
time: 144 us
  waiting for transfers between devices  53.5 us (37%)
  blocking collectives  42.9 us (30%)
  Pallas kernels  22.4 us (16%)
  starting transfers between devices  20.8 us (14%)
  local copies, waits for them, and re-layouts  3.62 us (3%)
    all_to_all x1, blocking collectives, per_device(): lax.all_to_all(h, 'chan', split_axis=0, concat_axis=0, tiled=True)  42.9 us
    ppermute x9, waiting for transfers between devices, swap(): return lax.ppermute(x, 'win', [(i, i ^ mask) for i in range(groups)])  27.7 us
    all_to_all x1, waiting for transfers between devices, per_device(): lax.all_to_all(h, 'chan', split_axis=0, concat_axis=0, tiled=True)  25.9 us
    pallas_call x2, Pallas kernels, stack(): pl.pallas_call(functools.partial(stack_kernel, chosen), out_shape=out, gr...  20.5 us
    ppermute x9, starting transfers between devices, swap(): return lax.ppermute(x, 'win', [(i, i ^ mask) for i in range(groups)])  13.3 us
    all_to_all x1, starting transfers between devices, per_device(): lax.all_to_all(h, 'chan', split_axis=0, concat_axis=0, tiled=True)  7.56 us
  transfers between devices with their start and end apart: 10, of which 6 were waited for; matrix products, arithmetic and copies ran while one was open for 2% of the time, Pallas kernels for 7%

profile of v1, /device:TPU:1, one launch (start us, length us, event | category | flops | bytes accessed | tf_op | source)
XLA Modules:
  0.0 144.0 jit_solution(17108244196495526121)
XLA Ops:
  0.0 1.6 %copy-done.1 = bf16[1,128,32,2,128]{4,3,2,1,0:T(2,128)(2,1)S(1)} copy-done((bf16[1,128,32,2,128]{4,3,2,1,0:T(2,128)(2,1)S(1)}, bf16[1,128,32,2,128]{4,3,2,1,0:T(2,128)(2,1)}, u32[]{:S(2)}) %copy-start.1) | copy-done | bytes 2097176
  1.6 1.9 %whiten.1 = (bf16[64,64,128]{2,1,0:T(8,128)(2,1)S(1)}, bf16[64,64,128]{2,1,0:T(8,128)(2,1)}) custom-call(bf16[128,64,128]{2,1,0:T(8,128)(2,1)S(1)} %bitcast.14), custom_call_target="tpu_custom_call" | custom-call | tf_op jit(solution)/shard_map/whiten/pallas_call | solution.py:41
  3.5 42.9 %all_to_all.10.refs_0_ = bf16[64,64,128]{2,1,0:T(8,128)(2,1)S(1)} all-to-all(bf16[64,64,128]{2,1,0:T(8,128)(2,1)S(1)} %get-tuple-element.8), channel_id=1, replica_groups=mesh['chan'=64,'win'=4] {'chan'}, dimensions={0} | all-to-all | bytes 2097152 | tf_op jit(solution)/shard_map/all_to_all | solution.py:106
  46.5 7.6 %all-to-all-start = ((bf16[64,64,128]{2,1,0:T(8,128)(2,1)}), bf16[64,64,128]{2,1,0:T(8,128)(2,1)S(1)}, u32[]{:S(2)}, u32[]{:S(2)}) async-start(bf16[64,64,128]{2,1,0:T(8,128)(2,1)} %get-tuple-element.7), calls=%async_computation | async-start | bytes 2097152 | tf_op jit(solution)/shard_map/all_to_all | solution.py:106
  54.0 0.5 collective-permute-start.6
  54.5 25.9 %all-to-all-done.refs_0_ = bf16[64,64,128]{2,1,0:T(8,128)(2,1)S(1)} async-done(((bf16[64,64,128]{2,1,0:T(8,128)(2,1)}), bf16[64,64,128]{2,1,0:T(8,128)(2,1)S(1)}, u32[]{:S(2)}, u32[]{:S(2)}) %all-to-all-start) | async-done | bytes 1048608 | tf_op jit(solution)/shard_map/all_to_all | solution.py:106
  80.4 0.1 collective-permute-start.3
  80.5 5.3 %collective-permute-start.7 = (bf16[64,64,128]{2,1,0:T(8,128)(2,1)S(1)}, bf16[64,64,128]{2,1,0:T(8,128)(2,1)}, u32[]{:S(2)}, u32[]{:S(2)}) collective-permute-start(bf16[64,64,128]{2,1,0:T(8,128)(2,1)S(1)} %all_to_all.10.refs_0_), channel_id=1, source_target_pairs={{0,1},{1,0},{2,3},{3,2},{4,5},{5,4},{6,7},{7,6},{8,9},{9,8},{10,11... | collective-permute-start | bytes 3145736 | tf_op jit(solution)/shard_map/ppermute | solution.py:101
  85.8 3.0 %collective-permute-done.6.refs_1_ = bf16[64,64,128]{2,1,0:T(8,128)(2,1)} collective-permute-done((bf16[64,64,128]{2,1,0:T(8,128)(2,1)S(1)}, bf16[64,64,128]{2,1,0:T(8,128)(2,1)}, u32[]{:S(2)}, u32[]{:S(2)}) %collective-permute-start.6) | collective-permute-done | bytes 1048608 | tf_op jit(solution)/shard_map/ppermute | solution.py:101
  88.9 3.2 %collective-permute-start.8 = (bf16[64,64,128]{2,1,0:T(8,128)(2,1)}, bf16[64,64,128]{2,1,0:T(8,128)(2,1)}, u32[]{:S(2)}, u32[]{:S(2)}) collective-permute-start(bf16[64,64,128]{2,1,0:T(8,128)(2,1)} %collective-permute-done.6.refs_1_), channel_id=1, source_target_pairs={{0,1},{1,0},{2,3},{3,2},{4,5},{5,4},{6,7},{7,6},{8,9},{9,8},{10,11... | collective-permute-start | bytes 3145736 | tf_op jit(solution)/shard_map/ppermute | solution.py:101
  92.1 19.2 %collective-permute-done.3.refs_1_ = bf16[64,64,128]{2,1,0:T(8,128)(2,1)S(1)} collective-permute-done((bf16[64,64,128]{2,1,0:T(8,128)(2,1)S(1)}, bf16[64,64,128]{2,1,0:T(8,128)(2,1)S(1)}, u32[]{:S(2)}, u32[]{:S(2)}) %collective-permute-start.3) | collective-permute-done | bytes 1048608 | tf_op jit(solution)/shard_map/ppermute | solution.py:101
  111.3 1.8 %collective-permute-start.5 = (bf16[64,64,128]{2,1,0:T(8,128)(2,1)S(1)}, bf16[64,64,128]{2,1,0:T(8,128)(2,1)}, u32[]{:S(2)}, u32[]{:S(2)}) collective-permute-start(bf16[64,64,128]{2,1,0:T(8,128)(2,1)S(1)} %collective-permute-done.3.refs_1_), channel_id=1, source_target_pairs={{0,1},{1,0},{2,3},{3,2},{4,5},{5,4},{6,7},{7,6},{8,9},{9,8},{10,11... | collective-permute-start | bytes 3145736 | tf_op jit(solution)/shard_map/ppermute | solution.py:101
  113.1 2.2 %collective-permute-done.1 = s32[32,64]{1,0:T(8,128)S(1)} collective-permute-done((s32[32,64]{1,0:T(8,128)S(1)}, s32[32,64]{1,0:T(8,128)S(1)}, u32[]{:S(2)}, u32[]{:S(2)}) %collective-permute-start.1) | collective-permute-done | bytes 8224 | tf_op jit(solution)/shard_map/ppermute | solution.py:101
  115.2 0.6 collective-permute-start
  115.9 1.9 %collective-permute-done = s32[32,64]{1,0:T(8,128)S(1)} collective-permute-done((s32[32,64]{1,0:T(8,128)S(1)}, s32[32,64]{1,0:T(8,128)S(1)}, u32[]{:S(2)}, u32[]{:S(2)}) %collective-permute-start) | collective-permute-done | bytes 8224 | tf_op jit(solution)/shard_map/ppermute | solution.py:101
  117.8 1.8 %collective-permute-start.2 = (s32[32,64]{1,0:T(8,128)S(1)}, s32[32,64]{1,0:T(8,128)S(1)}, u32[]{:S(2)}, u32[]{:S(2)}) collective-permute-start(s32[32,64]{1,0:T(8,128)S(1)} %copy-done.2), channel_id=1, source_target_pairs={{0,3},{1,2},{2,1},{3,0},{4,7},{5,6},{6,5},{7,4},{8,11},{9,10},{10,... | collective-permute-start | bytes 24584 | tf_op jit(solution)/shard_map/ppermute | solution.py:101
  119.7 1.3 collective-permute-done.2
  121.0 0.2 fusion.1
  121.2 0.4 fusion.4
  121.6 0.8 copy.6
  122.4 1.0 broadcast_in_dim.2
  123.4 0.1 copy.8.weight_ref
  123.5 10.4 %stack0.1.refs_4_ = bf16[16,2,2,128,256]{4,3,2,1,0:T(8,128)(2,1)} custom-call(s32[32]{0:T(128)S(1)} %reshape.30.mates_ref, s32[1]{0:T(128)} %bitcast.first_ref, f32[16,2,256]{2,1,0:T(2,128)S(1)} %copy.8.weight_ref, f32[32]{0:T(128)S(1)} %sqrt.4.norm_ref, bf16[64,64,128]{2,1,0:T(8,128)(2,1)S(1)} %all_to_all.10.refs_0_, ...), custom_call_target="tpu_custom_call" | custom-call | flops 536870912 | bytes 8388608 | tf_op jit(solution)/shard_map/stack0/pallas_call | solution.py:76
  133.9 10.1 %stack1.1 = bf16[16,2,2,128,256]{4,3,2,1,0:T(8,128)(2,1)} custom-call(s32[32]{0:T(128)S(1)} %reshape.30.mates_ref, s32[1]{0:T(128)} %bitcast.first_ref, f32[16,2,256]{2,1,0:T(2,128)S(1)} %copy.8.weight_ref, f32[32]{0:T(128)S(1)} %sqrt.4.norm_ref, bf16[64,64,128]{2,1,0:T(8,128)(2,1)S(1)} %all-to-all-done.refs_0_, ...), custom_call_target="tpu_custom_call", output_to_operand_aliasing={{}: (8, {})} | custom-call | flops 536870912 | bytes 8388608 | tf_op jit(solution)/shard_map/stack1/pallas_call | solution.py:76
  (16 shorter events, 0.2 us)
Async XLA Ops:
  0.0 115.8 %copy-start = (s32[2,64]{1,0:T(2,128)S(1)}, s32[2,64]{1,0:T(2,128)}, u32[]{:S(2)}) copy-start(s32[2,64]{1,0:T(2,128)} %param.5) | copy-start | bytes 1540
  0.0 1.6 %copy-start.1 = (bf16[1,128,32,2,128]{4,3,2,1,0:T(2,128)(2,1)S(1)}, bf16[1,128,32,2,128]{4,3,2,1,0:T(2,128)(2,1)}, u32[]{:S(2)}) copy-start(bf16[1,128,32,2,128]{4,3,2,1,0:T(2,128)(2,1)} %param.3) | copy-start | bytes 6291460
  1.6 111.5 %copy-start.2 = (s32[32,64]{1,0:T(8,128)S(1)}, s32[32,64]{1,0:T(8,128)}, u32[]{:S(2)}) copy-start(s32[32,64]{1,0:T(8,128)} %param.4) | copy-start | bytes 24580
  46.5 33.9 %all-to-all-start = ((bf16[64,64,128]{2,1,0:T(8,128)(2,1)}), bf16[64,64,128]{2,1,0:T(8,128)(2,1)S(1)}, u32[]{:S(2)}, u32[]{:S(2)}) async-start(bf16[64,64,128]{2,1,0:T(8,128)(2,1)} %get-tuple-element.7), calls=%async_computation | async-start | bytes 2097152 | tf_op jit(solution)/shard_map/all_to_all | solution.py:106
  54.0 34.8 %collective-permute-start.6 = (bf16[64,64,128]{2,1,0:T(8,128)(2,1)S(1)}, bf16[64,64,128]{2,1,0:T(8,128)(2,1)}, u32[]{:S(2)}, u32[]{:S(2)}) collective-permute-start(bf16[64,64,128]{2,1,0:T(8,128)(2,1)S(1)} %all_to_all.10.refs_0_), channel_id=1, source_target_pairs={{0,2},{1,3},{2,0},{3,1},{4,6},{5,7},{6,4},{7,5},{8,10},{9,11},{10,... | collective-permute-start | bytes 3145736 | tf_op jit(solution)/shard_map/ppermute | solution.py:101
  80.4 30.9 %collective-permute-start.3 = (bf16[64,64,128]{2,1,0:T(8,128)(2,1)S(1)}, bf16[64,64,128]{2,1,0:T(8,128)(2,1)S(1)}, u32[]{:S(2)}, u32[]{:S(2)}) collective-permute-start(bf16[64,64,128]{2,1,0:T(8,128)(2,1)S(1)} %all-to-all-done.refs_0_), channel_id=1, source_target_pairs={{0,2},{1,3},{2,0},{3,1},{4,6},{5,7},{6,4},{7,5},{8,10},{9,11},{10,... | collective-permute-start | bytes 3145736 | tf_op jit(solution)/shard_map/ppermute | solution.py:101
  80.5 42.9 %collective-permute-start.7 = (bf16[64,64,128]{2,1,0:T(8,128)(2,1)S(1)}, bf16[64,64,128]{2,1,0:T(8,128)(2,1)}, u32[]{:S(2)}, u32[]{:S(2)}) collective-permute-start(bf16[64,64,128]{2,1,0:T(8,128)(2,1)S(1)} %all_to_all.10.refs_0_), channel_id=1, source_target_pairs={{0,1},{1,0},{2,3},{3,2},{4,5},{5,4},{6,7},{7,6},{8,9},{9,8},{10,11... | collective-permute-start | bytes 3145736 | tf_op jit(solution)/shard_map/ppermute | solution.py:101
  88.9 34.6 %collective-permute-start.8 = (bf16[64,64,128]{2,1,0:T(8,128)(2,1)}, bf16[64,64,128]{2,1,0:T(8,128)(2,1)}, u32[]{:S(2)}, u32[]{:S(2)}) collective-permute-start(bf16[64,64,128]{2,1,0:T(8,128)(2,1)} %collective-permute-done.6.refs_1_), channel_id=1, source_target_pairs={{0,1},{1,0},{2,3},{3,2},{4,5},{5,4},{6,7},{7,6},{8,9},{9,8},{10,11... | collective-permute-start | bytes 3145736 | tf_op jit(solution)/shard_map/ppermute | solution.py:101
  92.1 41.8 %collective-permute-start.4 = (bf16[64,64,128]{2,1,0:T(8,128)(2,1)S(1)}, bf16[64,64,128]{2,1,0:T(8,128)(2,1)}, u32[]{:S(2)}, u32[]{:S(2)}) collective-permute-start(bf16[64,64,128]{2,1,0:T(8,128)(2,1)S(1)} %all-to-all-done.refs_0_), channel_id=1, source_target_pairs={{0,1},{1,0},{2,3},{3,2},{4,5},{5,4},{6,7},{7,6},{8,9},{9,8},{10,11... | collective-permute-start | bytes 3145736 | tf_op jit(solution)/shard_map/ppermute | solution.py:101
  111.3 22.6 %collective-permute-start.5 = (bf16[64,64,128]{2,1,0:T(8,128)(2,1)S(1)}, bf16[64,64,128]{2,1,0:T(8,128)(2,1)}, u32[]{:S(2)}, u32[]{:S(2)}) collective-permute-start(bf16[64,64,128]{2,1,0:T(8,128)(2,1)S(1)} %collective-permute-done.3.refs_1_), channel_id=1, source_target_pairs={{0,1},{1,0},{2,3},{3,2},{4,5},{5,4},{6,7},{7,6},{8,9},{9,8},{10,11... | collective-permute-start | bytes 3145736 | tf_op jit(solution)/shard_map/ppermute | solution.py:101
  113.1 2.2 %collective-permute-start.1 = (s32[32,64]{1,0:T(8,128)S(1)}, s32[32,64]{1,0:T(8,128)S(1)}, u32[]{:S(2)}, u32[]{:S(2)}) collective-permute-start(s32[32,64]{1,0:T(8,128)S(1)} %copy-done.2), channel_id=1, source_target_pairs={{0,1},{1,0},{2,3},{3,2},{4,5},{5,4},{6,7},{7,6},{8,9},{9,8},{10,11... | collective-permute-start | bytes 24584 | tf_op jit(solution)/shard_map/ppermute | solution.py:101
  115.2 2.6 %collective-permute-start = (s32[32,64]{1,0:T(8,128)S(1)}, s32[32,64]{1,0:T(8,128)S(1)}, u32[]{:S(2)}, u32[]{:S(2)}) collective-permute-start(s32[32,64]{1,0:T(8,128)S(1)} %copy-done.2), channel_id=1, source_target_pairs={{0,2},{1,3},{2,0},{3,1},{4,6},{5,7},{6,4},{7,5},{8,10},{9,11},{10,... | collective-permute-start | bytes 24584 | tf_op jit(solution)/shard_map/ppermute | solution.py:101
  117.8 3.2 %collective-permute-start.2 = (s32[32,64]{1,0:T(8,128)S(1)}, s32[32,64]{1,0:T(8,128)S(1)}, u32[]{:S(2)}, u32[]{:S(2)}) collective-permute-start(s32[32,64]{1,0:T(8,128)S(1)} %copy-done.2), channel_id=1, source_target_pairs={{0,3},{1,2},{2,1},{3,0},{4,7},{5,6},{6,5},{7,4},{8,11},{9,10},{10,... | collective-permute-start | bytes 24584 | tf_op jit(solution)/shard_map/ppermute | solution.py:101

commit v2 on v1

v2 whole, which is shorter than its diff:
```python
import functools

import jax
import jax.numpy as jnp
from jax import lax
from jax.experimental import pallas as pl
from jax.experimental.pallas import tpu as pltpu
from jax.sharding import Mesh, PartitionSpec as P

NSAMP = 256
EPS = 1e-06
UNROLL = 8


def whiten_kernel(side_ref, x_ref, near_ref, early_ref, late_ref):
    bins, rows, width = x_ref.shape
    half = bins // 2
    more = early_ref.shape[1] - rows
    step = 4

    def add(i, total):
        for j in range(step):
            values = x_ref[i * step + j].astype(jnp.float32)
            total = total + values * values
        return total

    total = lax.fori_loop(0, bins // step, add, jnp.zeros((rows, width), jnp.float32))
    first = lax.broadcasted_iota(jnp.int32, (rows, width), 0) % 2 == 0
    other = jnp.where(first, pltpu.roll(total, rows - 1, 0), pltpu.roll(total, 1, 0))
    scale = lax.rsqrt((total + other) / bins + EPS)
    near = side_ref[0] * half
    far = half - near

    def put(i, carry):
        for j in range(step):
            at = i * step + j
            for which in range(2):
                near_ref[at, which] = (x_ref[near + 2 * at + which].astype(jnp.float32) * scale).astype(near_ref.dtype)
            early_ref[at, :rows] = (x_ref[far + 2 * at].astype(jnp.float32) * scale).astype(early_ref.dtype)
            odd = (x_ref[far + 2 * at + 1].astype(jnp.float32) * scale).astype(early_ref.dtype)
            early_ref[at, rows:] = odd[:more]
            late_ref[at] = odd[more:]
        return carry

    lax.fori_loop(0, half // 2 // step, put, 0)


def whiten(side, spectra):
    bins, rows, width = spectra.shape
    places = bins // 4
    vmem = pl.BlockSpec(memory_space=pltpu.VMEM)
    return pl.pallas_call(
        whiten_kernel,
        out_shape=[
            jax.ShapeDtypeStruct(shape, spectra.dtype)
            for shape in ((places, 2, rows, width), (places, rows + rows // 2, width), (places, rows // 2, width))
        ],
        in_specs=[pl.BlockSpec(memory_space=pltpu.SMEM), vmem],
        out_specs=[vmem] * 3,
        compiler_params=pltpu.CompilerParams(vmem_limit_bytes=16 << 20),
        name="whiten",
    )(side, spectra)


def turn_matrix(rows):
    i = lax.broadcasted_iota(jnp.int32, (rows, rows), 0)
    j = lax.broadcasted_iota(jnp.int32, (rows, rows), 1)
    plus = (i == j + 1) & (j % 2 == 0)
    minus = (i == j - 1) & (j % 2 == 1)
    return (plus.astype(jnp.float32) - minus.astype(jnp.float32)).astype(jnp.bfloat16)


def stack_kernel(which, side_ref, first_ref, mates_ref, weight_ref, norm_ref, *refs):
    near, early, late, out_ref = refs[:4], refs[4:8], refs[8:12], refs[-1]
    chosen, rounds = weight_ref.shape[:2]
    half, _, rows, width = near[0].shape
    side = side_ref[0]

    def block(b):
        mine = b // half == side
        at = b % half
        parts = []
        for t in range(4):
            if which == 0:
                far = early[t ^ 2][at, :rows]
            else:
                far = jnp.concatenate([early[t ^ 2][at, rows:], late[t ^ 2][at]], axis=0)
            parts.append(jnp.where(mine, near[t][at, which], far))
        return jnp.concatenate(parts, axis=0)

    turn = turn_matrix(4 * rows)
    for u in range(UNROLL):
        n = pl.program_id(0) * UNROLL + u
        own = block(first_ref[0] + n).T
        turned = jnp.dot(own, turn, preferred_element_type=jnp.float32).astype(own.dtype)
        left = jnp.concatenate([own, turned], axis=0)
        right = jnp.concatenate([block(mates_ref[r * chosen + n]) * weight_ref[n, r] for r in range(rounds)], axis=1)
        both = jnp.dot(left, right, preferred_element_type=jnp.float32)
        for r in range(rounds):
            total = (both[:, r * width : (r + 1) * width] * (1.0 / norm_ref[r * chosen + n])).astype(out_ref.dtype)
            out_ref[u, r, 0, :, :width] = total[:width]
            out_ref[u, r, 0, :, width:] = total[width:]


def stack(which, near, early, late, side, first, mates, weight, norm, into):
    chosen, rounds, rows, width = weight.shape
    out = jax.ShapeDtypeStruct((chosen, rounds, 2, width, 2 * width), jnp.bfloat16)
    smem = pl.BlockSpec(memory_space=pltpu.SMEM)
    vmem = pl.BlockSpec(memory_space=pltpu.VMEM)
    far = [*early, *late] if which else [*early]
    refs = [smem, smem, smem, vmem, smem] + [vmem] * (len(near) + len(far))
    more = () if into is None else (into,)
    return pl.pallas_call(
        functools.partial(stack_kernel, which),
        out_shape=out,
        grid=(chosen // UNROLL,),
        in_specs=refs + [pl.BlockSpec(memory_space=pl.ANY)] * len(more),
        out_specs=pl.BlockSpec((UNROLL, rounds, 1, width, 2 * width), lambda n: (n, 0, which, 0, 0)),
        input_output_aliases={len(refs): 0} if more else {},
        compiler_params=pltpu.CompilerParams(vmem_limit_bytes=24 << 20),
        cost_estimate=pl.CostEstimate(flops=20 * chosen * rounds * 2 * width * rows * width, bytes_accessed=8 << 20, transcendentals=0),
        name="stack" + str(which),
    )(side, first, mates, weight, norm, *near, *far, *more)


def per_device(spectra, counts, partner):
    bins, windows, parts, width = spectra.shape[1:]
    rounds, nblocks = partner.shape
    groups = lax.axis_size("yl") * lax.axis_size("core")
    chosen = nblocks // groups
    me = lax.axis_index(("yl", "core"))
    side = lax.axis_index("yh").reshape(1)
    first = me * chosen
    swap_pairs = [(0, 1), (1, 0)]
    after = lax.optimization_barrier

    def across(x):
        return lax.ppermute(x, "core", swap_pairs)

    def along(x):
        return lax.ppermute(x, "yl", swap_pairs)

    def hand_on(x):
        return lax.ppermute(x, ("yh", "yl"), [(0, 3), (3, 0), (1, 2), (2, 1)])

    shuffle = functools.partial(lax.all_to_all, axis_name=("x", "z"), split_axis=0, concat_axis=0, tiled=True)

    near, early, late = whiten(side, spectra.reshape(bins, windows * parts, width))
    early, late = hand_on(early), hand_on(late)
    beside = along(counts)
    tallies = (counts, across(counts), beside, across(beside))

    columns = jnp.concatenate(tallies, axis=0).astype(jnp.float32)
    mine = lax.dynamic_slice_in_dim(partner, first, chosen, 1)
    every = jnp.arange(nblocks, dtype=jnp.int32)
    theirs_hot = (mine.reshape(rounds * chosen, 1) == every[None]).astype(jnp.float32)
    ours_hot = (first + jnp.arange(chosen, dtype=jnp.int32)[:, None] == every[None]).astype(jnp.float32)
    pick = functools.partial(jnp.einsum, "nb,wb->nw", precision=lax.Precision.HIGHEST)
    theirs = pick(theirs_hot, columns).reshape(rounds, chosen, -1)
    ours = pick(ours_hot, columns)
    weight = jnp.minimum(ours[None], theirs) / NSAMP
    norm = jnp.sqrt(jnp.sum(weight * weight, axis=2)).reshape(rounds * chosen)
    wide = jnp.repeat(jnp.transpose(weight, (1, 0, 2)), parts, axis=2)
    wide = jnp.broadcast_to(wide.astype(jnp.bfloat16)[..., None], wide.shape + (width,))

    near = shuffle(near)
    near, early, late, wide, norm = after((near, early, late, wide, norm))
    near_beside = along(near)
    near = (near, across(near), near_beside, across(near_beside))
    early = shuffle(early)
    late, near = after((late, near))
    early_beside = along(early)
    late = shuffle(late)
    late, early_beside = after((late, early_beside))
    late_beside = along(late)

    operands = (side, first.reshape(1), mine.reshape(-1), wide, norm)
    early = (early, across(early), early_beside, across(early_beside))
    result = stack(0, near, early, None, *operands, None)
    late_beside, result = after((late_beside, result))
    late = (late, across(late), late_beside, across(late_beside))
    return stack(1, near, early, late, *operands, result)


def solution(mesh):
    split = Mesh(mesh.devices.reshape(2, 4, 8, 2, 2), ("yh", "x", "z", "yl", "core"))
    chan, win = ("yh", "x", "z"), ("yl", "core")
    return jax.shard_map(
        per_device,
        mesh=split,
        in_specs=(P(chan, None, win, None, None), P(win, None), P()),
        out_specs=P(win, None, chan, None, None),
        check_vma=False,
    )
```

time: 144 us -> 109 us (0.76)
  blocking collectives: 42.9 us -> 0 us
  starting transfers between devices: 20.8 us -> 52.2 us
  waiting for transfers between devices: 53.5 us -> 39.7 us
  Pallas kernels: 22.4 us -> 13.1 us
    all_to_all x1 -> x0, blocking collectives: 42.9 us -> none  [per_device(): lax.all_to_all(h, 'chan', split_axis=0, concat_axis=0, tiled=True)]
    all_to_all x1 -> x3, starting transfers between devices: 7.56 us -> 29.5 us  [the longest x1 11.9 us: per_device(): near = shuffle(near)]
    all_to_all x1 -> x3, waiting for transfers between devices: 25.9 us -> 7.45 us  [the longest x1 5.46 us: per_device(): late = shuffle(late)]
    ppermute x9 -> x14, starting transfers between devices: 13.3 us -> 22.7 us  [the longest x8 18 us: across(): return lax.ppermute(x, 'core', swap_pairs)]
    pallas_call x3, Pallas kernels: 22.4 us -> 13.1 us  [the longest x2 11.2 us: stack(): pl.pallas_call(functools.partial(stack_kernel, which), out_shape=out, gri...]
    ppermute x9 -> x14, waiting for transfers between devices: 27.7 us -> 32.2 us  [the longest x2 15.7 us: hand_on(): return lax.ppermute(x, ('yh', 'yl'), [(0, 3), (3, 0), (1, 2), (2, 1)])]
  transfers between devices with their start and end apart: 10 -> 17, of which waited for: 6 -> 11; matrix products, arithmetic and copies ran while one was open for 2% -> 1% of each run, Pallas kernels for 7% -> 5%
where the time goes in v2:
time: 109 us
  starting transfers between devices  52.2 us (48%)
  waiting for transfers between devices  39.7 us (36%)
  Pallas kernels  13.1 us (12%)
  local copies, waits for them, and re-layouts  3.29 us (3%)
    ppermute x8, starting transfers between devices, across(): return lax.ppermute(x, 'core', swap_pairs)  18 us
    ppermute x2, waiting for transfers between devices, hand_on(): return lax.ppermute(x, ('yh', 'yl'), [(0, 3), (3, 0), (1, 2), (2, 1)])  15.7 us
    ppermute x4, waiting for transfers between devices, along(): return lax.ppermute(x, 'yl', swap_pairs)  12.7 us
    all_to_all x1, starting transfers between devices, per_device(): near = shuffle(near)  11.9 us
    pallas_call x2, Pallas kernels, stack(): pl.pallas_call(functools.partial(stack_kernel, which), out_shape=out, gri...  11.2 us
    all_to_all x1, starting transfers between devices, per_device(): late = shuffle(late)  8.93 us
    all_to_all x1, starting transfers between devices, per_device(): early = shuffle(early)  8.7 us
    all_to_all x1, waiting for transfers between devices, per_device(): late = shuffle(late)  5.46 us
  transfers between devices with their start and end apart: 17, of which 11 were waited for; matrix products, arithmetic and copies ran while one was open for 1% of the time, Pallas kernels for 5%

profile of v2, /device:TPU:1, one launch (start us, length us, event | category | flops | bytes accessed | tf_op | source)
XLA Modules:
  0.0 108.9 jit_solution(8832979079380424484)
XLA Ops:
  0.0 1.6 %copy-done.1 = bf16[1,128,32,2,128]{4,3,2,1,0:T(2,128)(2,1)S(1)} copy-done((bf16[1,128,32,2,128]{4,3,2,1,0:T(2,128)(2,1)S(1)}, bf16[1,128,32,2,128]{4,3,2,1,0:T(2,128)(2,1)}, u32[]{:S(2)}) %copy-start.1) | copy-done | bytes 2097176
  1.6 1.9 %whiten.1 = (bf16[32,2,64,128]{3,2,1,0:T(8,128)(2,1)}, bf16[32,96,128]{2,1,0:T(8,128)(2,1)S(1)}, bf16[32,32,128]{2,1,0:T(8,128)(2,1)S(1)}) custom-call(s32[1]{0:T(128)} %bitcast.side_ref, bf16[128,64,128]{2,1,0:T(8,128)(2,1)S(1)} %bitcast.15), custom_call_target="tpu_custom_call" | custom-call | tf_op jit(solution)/shard_map/whiten/pallas_call | solution.py:52
  3.5 11.9 %all-to-all-start = ((bf16[32,2,64,128]{3,2,1,0:T(8,128)(2,1)}), bf16[32,2,64,128]{3,2,1,0:T(8,128)(2,1)S(1)}, u32[]{:S(2)}, u32[]{:S(2)}) async-start(bf16[32,2,64,128]{3,2,1,0:T(8,128)(2,1)} %get-tuple-element.22), calls=%async_computation | async-start | bytes 2097152 | tf_op jit(solution)/shard_map/all_to_all | solution.py:166
  15.4 2.8 %collective-permute-start = (bf16[32,96,128]{2,1,0:T(8,128)(2,1)S(1)}, bf16[32,96,128]{2,1,0:T(8,128)(2,1)}, u32[]{:S(2)}, u32[]{:S(2)}) collective-permute-start(bf16[32,96,128]{2,1,0:T(8,128)(2,1)S(1)} %get-tuple-element.23), channel_id=1, source_target_pairs={{0,130},{130,0},{2,128},{128,2},{1,131},{131,1},{3,129},{129,3},{4... | collective-permute-start | bytes 2359304 | tf_op jit(solution)/shard_map/ppermute | solution.py:144
  18.2 1.2 %collective-permute-start.2 = (s32[32,64]{1,0:T(8,128)S(1)}, s32[32,64]{1,0:T(8,128)S(1)}, u32[]{:S(2)}, u32[]{:S(2)}) collective-permute-start(s32[32,64]{1,0:T(8,128)S(1)} %copy-done.2), channel_id=1, source_target_pairs={{0,1},{1,0},{2,3},{3,2},{4,5},{5,4},{6,7},{7,6},{8,9},{9,8},{10,11... | collective-permute-start | bytes 24584 | tf_op jit(solution)/shard_map/ppermute | solution.py:138
  20.1 2.3 %collective-permute-done.3 = s32[32,64]{1,0:T(8,128)S(1)} collective-permute-done((s32[32,64]{1,0:T(8,128)S(1)}, s32[32,64]{1,0:T(8,128)S(1)}, u32[]{:S(2)}, u32[]{:S(2)}) %collective-permute-start.3) | collective-permute-done | bytes 8224 | tf_op jit(solution)/shard_map/ppermute | solution.py:141
  24.9 15.7 %collective-permute-done.1 = bf16[32,32,128]{2,1,0:T(8,128)(2,1)} collective-permute-done((bf16[32,32,128]{2,1,0:T(8,128)(2,1)S(1)}, bf16[32,32,128]{2,1,0:T(8,128)(2,1)}, u32[]{:S(2)}, u32[]{:S(2)}) %collective-permute-start.1) | collective-permute-done | bytes 262176 | tf_op jit(solution)/shard_map/ppermute | solution.py:144
  40.6 1.2 %broadcast_in_dim.5.weight_ref = bf16[16,2,256,128]{3,2,1,0:T(8,128)(2,1)S(1)} broadcast(bf16[16,2,256]{2,1,0:T(2,128)(2,1)S(1)} %copy.7), dimensions={0,1,2} | broadcast | bytes 2113536 | tf_op jit(solution)/shard_map/broadcast_in_dim | solution.py:164
  41.9 0.8 collective-permute-start.6
  42.6 8.7 %all-to-all-start.1 = ((bf16[32,96,128]{2,1,0:T(8,128)(2,1)}), bf16[32,96,128]{2,1,0:T(8,128)(2,1)}, u32[]{:S(2)}, u32[]{:S(2)}) async-start(bf16[32,96,128]{2,1,0:T(8,128)(2,1)} %collective-permute-done), calls=%async_computation.1 | async-start | bytes 1572864 | tf_op jit(solution)/shard_map/all_to_all | solution.py:170
  51.3 2.4 %collective-permute-start.5 = (bf16[32,2,64,128]{3,2,1,0:T(8,128)(2,1)S(1)}, bf16[32,2,64,128]{3,2,1,0:T(8,128)(2,1)}, u32[]{:S(2)}, u32[]{:S(2)}) collective-permute-start(bf16[32,2,64,128]{3,2,1,0:T(8,128)(2,1)S(1)} %all-to-all-done.refs_0_), channel_id=1, source_target_pairs={{0,1},{1,0},{2,3},{3,2},{4,5},{5,4},{6,7},{7,6},{8,9},{9,8},{10,11... | collective-permute-start | bytes 3145736 | tf_op jit(solution)/shard_map/ppermute | solution.py:138
  53.8 8.6 %collective-permute-done.6.refs_2_ = bf16[32,2,64,128]{3,2,1,0:T(8,128)(2,1)} collective-permute-done((bf16[32,2,64,128]{3,2,1,0:T(8,128)(2,1)S(1)}, bf16[32,2,64,128]{3,2,1,0:T(8,128)(2,1)}, u32[]{:S(2)}, u32[]{:S(2)}) %collective-permute-start.6) | collective-permute-done | bytes 1048608 | tf_op jit(solution)/shard_map/ppermute | solution.py:141
  62.4 5.3 %collective-permute-start.7 = (bf16[32,2,64,128]{3,2,1,0:T(8,128)(2,1)}, bf16[32,2,64,128]{3,2,1,0:T(8,128)(2,1)}, u32[]{:S(2)}, u32[]{:S(2)}) collective-permute-start(bf16[32,2,64,128]{3,2,1,0:T(8,128)(2,1)} %collective-permute-done.6.refs_2_), channel_id=1, source_target_pairs={{0,1},{1,0},{2,3},{3,2},{4,5},{5,4},{6,7},{7,6},{8,9},{9,8},{10,11... | collective-permute-start | bytes 3145736 | tf_op jit(solution)/shard_map/ppermute | solution.py:138
  67.6 2.0 %all-to-all-done.1.refs_4_ = bf16[32,96,128]{2,1,0:T(8,128)(2,1)} async-done(((bf16[32,96,128]{2,1,0:T(8,128)(2,1)}), bf16[32,96,128]{2,1,0:T(8,128)(2,1)}, u32[]{:S(2)}, u32[]{:S(2)}) %all-to-all-start.1) | async-done | bytes 786464 | tf_op jit(solution)/shard_map/all_to_all | solution.py:170
  70.3 8.9 %all-to-all-start.2 = ((bf16[32,32,128]{2,1,0:T(8,128)(2,1)}), bf16[32,32,128]{2,1,0:T(8,128)(2,1)S(1)}, u32[]{:S(2)}, u32[]{:S(2)}) async-start(bf16[32,32,128]{2,1,0:T(8,128)(2,1)} %collective-permute-done.1), calls=%async_computation.2 | async-start | bytes 524288 | tf_op jit(solution)/shard_map/all_to_all | solution.py:173
  79.2 2.7 %collective-permute-start.8 = (bf16[32,96,128]{2,1,0:T(8,128)(2,1)}, bf16[32,96,128]{2,1,0:T(8,128)(2,1)}, u32[]{:S(2)}, u32[]{:S(2)}) collective-permute-start(bf16[32,96,128]{2,1,0:T(8,128)(2,1)} %all-to-all-done.1.refs_4_), channel_id=1, source_target_pairs={{0,1},{1,0},{2,3},{3,2},{4,5},{5,4},{6,7},{7,6},{8,9},{9,8},{10,11... | collective-permute-start | bytes 2359304 | tf_op jit(solution)/shard_map/ppermute | solution.py:138
  81.9 1.5 %collective-permute-done.9.refs_6_ = bf16[32,96,128]{2,1,0:T(8,128)(2,1)} collective-permute-done((bf16[32,96,128]{2,1,0:T(8,128)(2,1)}, bf16[32,96,128]{2,1,0:T(8,128)(2,1)}, u32[]{:S(2)}, u32[]{:S(2)}) %collective-permute-start.9) | collective-permute-done | bytes 786464 | tf_op jit(solution)/shard_map/ppermute | solution.py:141
  83.4 5.5 %all-to-all-done.2.refs_8_ = bf16[32,32,128]{2,1,0:T(8,128)(2,1)S(1)} async-done(((bf16[32,32,128]{2,1,0:T(8,128)(2,1)}), bf16[32,32,128]{2,1,0:T(8,128)(2,1)S(1)}, u32[]{:S(2)}, u32[]{:S(2)}) %all-to-all-start.2) | async-done | bytes 262176 | tf_op jit(solution)/shard_map/all_to_all | solution.py:173
  88.9 4.5 %collective-permute-start.10 = (bf16[32,96,128]{2,1,0:T(8,128)(2,1)}, bf16[32,96,128]{2,1,0:T(8,128)(2,1)S(1)}, u32[]{:S(2)}, u32[]{:S(2)}) collective-permute-start(bf16[32,96,128]{2,1,0:T(8,128)(2,1)} %collective-permute-done.9.refs_6_), channel_id=1, source_target_pairs={{0,1},{1,0},{2,3},{3,2},{4,5},{5,4},{6,7},{7,6},{8,9},{9,8},{10,11... | collective-permute-start | bytes 2359304 | tf_op jit(solution)/shard_map/ppermute | solution.py:138
  94.0 1.5 %collective-permute-done.10.refs_7_ = bf16[32,96,128]{2,1,0:T(8,128)(2,1)S(1)} collective-permute-done((bf16[32,96,128]{2,1,0:T(8,128)(2,1)}, bf16[32,96,128]{2,1,0:T(8,128)(2,1)S(1)}, u32[]{:S(2)}, u32[]{:S(2)}) %collective-permute-start.10) | collective-permute-done | bytes 786464 | tf_op jit(solution)/shard_map/ppermute | solution.py:138
  95.5 5.5 %stack0.1.refs_12_ = bf16[16,2,2,128,256]{4,3,2,1,0:T(8,128)(2,1)} custom-call(s32[1]{0:T(128)} %bitcast.side_ref, s32[1]{0:T(128)} %bitcast.1.first_ref, s32[32]{0:T(128)S(1)} %reshape.37.mates_ref, bf16[16,2,256,128]{3,2,1,0:T(8,128)(2,1)S(1)} %broadcast_in_dim.5.weight_ref, f32[32]{0:T(128)S(1)} %sqrt.4.norm_ref, ...), custom_call_target="tpu_custom_call" | custom-call | flops 5368709120 | bytes 8388608 | tf_op jit(solution)/shard_map/stack0/pallas_call | solution.py:113
  101.3 0.8 collective-permute-start.13
  102.1 1.2 %collective-permute-done.13.refs_11_ = bf16[32,32,128]{2,1,0:T(8,128)(2,1)S(1)} collective-permute-done((bf16[32,32,128]{2,1,0:T(8,128)(2,1)S(1)}, bf16[32,32,128]{2,1,0:T(8,128)(2,1)S(1)}, u32[]{:S(2)}, u32[]{:S(2)}) %collective-permute-start.13) | collective-permute-done | bytes 262176 | tf_op jit(solution)/shard_map/ppermute | solution.py:138
  103.3 5.7 %stack1.1 = bf16[16,2,2,128,256]{4,3,2,1,0:T(8,128)(2,1)} custom-call(s32[1]{0:T(128)} %bitcast.side_ref, s32[1]{0:T(128)} %bitcast.1.first_ref, s32[32]{0:T(128)S(1)} %reshape.37.mates_ref, bf16[16,2,256,128]{3,2,1,0:T(8,128)(2,1)S(1)} %broadcast_in_dim.5.weight_ref, f32[32]{0:T(128)S(1)} %sqrt.4.norm_ref, ...), custom_call_target="tpu_custom_call", output_to_operand_aliasing={{}: (17, {})} | custom-call | flops 5368709120 | bytes 8388608 | tf_op jit(solution)/shard_map/stack1/pallas_call | solution.py:113
  (30 shorter events, 4.7 us)
Async XLA Ops:
  0.0 20.1 %copy-start = (s32[2,64]{1,0:T(2,128)S(1)}, s32[2,64]{1,0:T(2,128)}, u32[]{:S(2)}) copy-start(s32[2,64]{1,0:T(2,128)} %param.5) | copy-start | bytes 1540
  0.0 1.6 %copy-start.1 = (bf16[1,128,32,2,128]{4,3,2,1,0:T(2,128)(2,1)S(1)}, bf16[1,128,32,2,128]{4,3,2,1,0:T(2,128)(2,1)}, u32[]{:S(2)}) copy-start(bf16[1,128,32,2,128]{4,3,2,1,0:T(2,128)(2,1)} %param.3) | copy-start | bytes 6291460
  1.6 16.6 %copy-start.2 = (s32[32,64]{1,0:T(8,128)S(1)}, s32[32,64]{1,0:T(8,128)}, u32[]{:S(2)}) copy-start(s32[32,64]{1,0:T(8,128)} %param.4) | copy-start | bytes 24580
  3.5 37.1 %all-to-all-start = ((bf16[32,2,64,128]{3,2,1,0:T(8,128)(2,1)}), bf16[32,2,64,128]{3,2,1,0:T(8,128)(2,1)S(1)}, u32[]{:S(2)}, u32[]{:S(2)}) async-start(bf16[32,2,64,128]{3,2,1,0:T(8,128)(2,1)} %get-tuple-element.22), calls=%async_computation | async-start | bytes 2097152 | tf_op jit(solution)/shard_map/all_to_all | solution.py:166
  15.4 25.2 %collective-permute-start = (bf16[32,96,128]{2,1,0:T(8,128)(2,1)S(1)}, bf16[32,96,128]{2,1,0:T(8,128)(2,1)}, u32[]{:S(2)}, u32[]{:S(2)}) collective-permute-start(bf16[32,96,128]{2,1,0:T(8,128)(2,1)S(1)} %get-tuple-element.23), channel_id=1, source_target_pairs={{0,130},{130,0},{2,128},{128,2},{1,131},{131,1},{3,129},{129,3},{4... | collective-permute-start | bytes 2359304 | tf_op jit(solution)/shard_map/ppermute | solution.py:144
  18.2 5.1 %collective-permute-start.2 = (s32[32,64]{1,0:T(8,128)S(1)}, s32[32,64]{1,0:T(8,128)S(1)}, u32[]{:S(2)}, u32[]{:S(2)}) collective-permute-start(s32[32,64]{1,0:T(8,128)S(1)} %copy-done.2), channel_id=1, source_target_pairs={{0,1},{1,0},{2,3},{3,2},{4,5},{5,4},{6,7},{7,6},{8,9},{9,8},{10,11... | collective-permute-start | bytes 24584 | tf_op jit(solution)/shard_map/ppermute | solution.py:138
  19.4 3.0 %collective-permute-start.3 = (s32[32,64]{1,0:T(8,128)S(1)}, s32[32,64]{1,0:T(8,128)S(1)}, u32[]{:S(2)}, u32[]{:S(2)}) collective-permute-start(s32[32,64]{1,0:T(8,128)S(1)} %copy-done.2), channel_id=1, source_target_pairs={{0,2},{2,0},{1,3},{3,1},{4,6},{6,4},{5,7},{7,5},{8,10},{10,8},{9,1... | collective-permute-start | bytes 24584 | tf_op jit(solution)/shard_map/ppermute | solution.py:141
  19.4 21.2 %collective-permute-start.1 = (bf16[32,32,128]{2,1,0:T(8,128)(2,1)S(1)}, bf16[32,32,128]{2,1,0:T(8,128)(2,1)}, u32[]{:S(2)}, u32[]{:S(2)}) collective-permute-start(bf16[32,32,128]{2,1,0:T(8,128)(2,1)S(1)} %get-tuple-element.24), channel_id=1, source_target_pairs={{0,130},{130,0},{2,128},{128,2},{1,131},{131,1},{3,129},{129,3},{4... | collective-permute-start | bytes 786440 | tf_op jit(solution)/shard_map/ppermute | solution.py:144
  22.4 1.6 %collective-permute-start.4 = (s32[32,64]{1,0:T(8,128)S(1)}, s32[32,64]{1,0:T(8,128)S(1)}, u32[]{:S(2)}, u32[]{:S(2)}) collective-permute-start(s32[32,64]{1,0:T(8,128)S(1)} %collective-permute-done.3), channel_id=1, source_target_pairs={{0,1},{1,0},{2,3},{3,2},{4,5},{5,4},{6,7},{7,6},{8,9},{9,8},{10,11... | collective-permute-start | bytes 24584 | tf_op jit(solution)/shard_map/ppermute | solution.py:138
  41.9 20.5 %collective-permute-start.6 = (bf16[32,2,64,128]{3,2,1,0:T(8,128)(2,1)S(1)}, bf16[32,2,64,128]{3,2,1,0:T(8,128)(2,1)}, u32[]{:S(2)}, u32[]{:S(2)}) collective-permute-start(bf16[32,2,64,128]{3,2,1,0:T(8,128)(2,1)S(1)} %all-to-all-done.refs_0_), channel_id=1, source_target_pairs={{0,2},{2,0},{1,3},{3,1},{4,6},{6,4},{5,7},{7,5},{8,10},{10,8},{9,1... | collective-permute-start | bytes 3145736 | tf_op jit(solution)/shard_map/ppermute | solution.py:141
  42.6 27.0 %all-to-all-start.1 = ((bf16[32,96,128]{2,1,0:T(8,128)(2,1)}), bf16[32,96,128]{2,1,0:T(8,128)(2,1)}, u32[]{:S(2)}, u32[]{:S(2)}) async-start(bf16[32,96,128]{2,1,0:T(8,128)(2,1)} %collective-permute-done), calls=%async_computation.1 | async-start | bytes 1572864 | tf_op jit(solution)/shard_map/all_to_all | solution.py:170
  51.3 18.5 %collective-permute-start.5 = (bf16[32,2,64,128]{3,2,1,0:T(8,128)(2,1)S(1)}, bf16[32,2,64,128]{3,2,1,0:T(8,128)(2,1)}, u32[]{:S(2)}, u32[]{:S(2)}) collective-permute-start(bf16[32,2,64,128]{3,2,1,0:T(8,128)(2,1)S(1)} %all-to-all-done.refs_0_), channel_id=1, source_target_pairs={{0,1},{1,0},{2,3},{3,2},{4,5},{5,4},{6,7},{7,6},{8,9},{9,8},{10,11... | collective-permute-start | bytes 3145736 | tf_op jit(solution)/shard_map/ppermute | solution.py:138
  62.4 7.9 %collective-permute-start.7 = (bf16[32,2,64,128]{3,2,1,0:T(8,128)(2,1)}, bf16[32,2,64,128]{3,2,1,0:T(8,128)(2,1)}, u32[]{:S(2)}, u32[]{:S(2)}) collective-permute-start(bf16[32,2,64,128]{3,2,1,0:T(8,128)(2,1)} %collective-permute-done.6.refs_2_), channel_id=1, source_target_pairs={{0,1},{1,0},{2,3},{3,2},{4,5},{5,4},{6,7},{7,6},{8,9},{9,8},{10,11... | collective-permute-start | bytes 3145736 | tf_op jit(solution)/shard_map/ppermute | solution.py:138
  69.6 13.8 %collective-permute-start.9 = (bf16[32,96,128]{2,1,0:T(8,128)(2,1)}, bf16[32,96,128]{2,1,0:T(8,128)(2,1)}, u32[]{:S(2)}, u32[]{:S(2)}) collective-permute-start(bf16[32,96,128]{2,1,0:T(8,128)(2,1)} %all-to-all-done.1.refs_4_), channel_id=1, source_target_pairs={{0,2},{2,0},{1,3},{3,1},{4,6},{6,4},{5,7},{7,5},{8,10},{10,8},{9,1... | collective-permute-start | bytes 2359304 | tf_op jit(solution)/shard_map/ppermute | solution.py:141
  70.3 18.6 %all-to-all-start.2 = ((bf16[32,32,128]{2,1,0:T(8,128)(2,1)}), bf16[32,32,128]{2,1,0:T(8,128)(2,1)S(1)}, u32[]{:S(2)}, u32[]{:S(2)}) async-start(bf16[32,32,128]{2,1,0:T(8,128)(2,1)} %collective-permute-done.1), calls=%async_computation.2 | async-start | bytes 524288 | tf_op jit(solution)/shard_map/all_to_all | solution.py:173
  79.2 14.8 %collective-permute-start.8 = (bf16[32,96,128]{2,1,0:T(8,128)(2,1)}, bf16[32,96,128]{2,1,0:T(8,128)(2,1)}, u32[]{:S(2)}, u32[]{:S(2)}) collective-permute-start(bf16[32,96,128]{2,1,0:T(8,128)(2,1)} %all-to-all-done.1.refs_4_), channel_id=1, source_target_pairs={{0,1},{1,0},{2,3},{3,2},{4,5},{5,4},{6,7},{7,6},{8,9},{9,8},{10,11... | collective-permute-start | bytes 2359304 | tf_op jit(solution)/shard_map/ppermute | solution.py:138
  88.9 6.6 %collective-permute-start.10 = (bf16[32,96,128]{2,1,0:T(8,128)(2,1)}, bf16[32,96,128]{2,1,0:T(8,128)(2,1)S(1)}, u32[]{:S(2)}, u32[]{:S(2)}) collective-permute-start(bf16[32,96,128]{2,1,0:T(8,128)(2,1)} %collective-permute-done.9.refs_6_), channel_id=1, source_target_pairs={{0,1},{1,0},{2,3},{3,2},{4,5},{5,4},{6,7},{7,6},{8,9},{9,8},{10,11... | collective-permute-start | bytes 2359304 | tf_op jit(solution)/shard_map/ppermute | solution.py:138
  93.4 7.9 %collective-permute-start.12 = (bf16[32,32,128]{2,1,0:T(8,128)(2,1)S(1)}, bf16[32,32,128]{2,1,0:T(8,128)(2,1)S(1)}, u32[]{:S(2)}, u32[]{:S(2)}) collective-permute-start(bf16[32,32,128]{2,1,0:T(8,128)(2,1)S(1)} %all-to-all-done.2.refs_8_), channel_id=1, source_target_pairs={{0,2},{2,0},{1,3},{3,1},{4,6},{6,4},{5,7},{7,5},{8,10},{10,8},{9,1... | collective-permute-start | bytes 786440 | tf_op jit(solution)/shard_map/ppermute | solution.py:141
  93.7 8.4 %collective-permute-start.11 = (bf16[32,32,128]{2,1,0:T(8,128)(2,1)S(1)}, bf16[32,32,128]{2,1,0:T(8,128)(2,1)S(1)}, u32[]{:S(2)}, u32[]{:S(2)}) collective-permute-start(bf16[32,32,128]{2,1,0:T(8,128)(2,1)S(1)} %all-to-all-done.2.refs_8_), channel_id=1, source_target_pairs={{0,1},{1,0},{2,3},{3,2},{4,5},{5,4},{6,7},{7,6},{8,9},{9,8},{10,11... | collective-permute-start | bytes 786440 | tf_op jit(solution)/shard_map/ppermute | solution.py:138
  101.3 1.9 %collective-permute-start.13 = (bf16[32,32,128]{2,1,0:T(8,128)(2,1)S(1)}, bf16[32,32,128]{2,1,0:T(8,128)(2,1)S(1)}, u32[]{:S(2)}, u32[]{:S(2)}) collective-permute-start(bf16[32,32,128]{2,1,0:T(8,128)(2,1)S(1)} %collective-permute-done.12.refs_10_), channel_id=1, source_target_pairs={{0,1},{1,0},{2,3},{3,2},{4,5},{5,4},{6,7},{7,6},{8,9},{9,8},{10,11... | collective-permute-start | bytes 786440 | tf_op jit(solution)/shard_map/ppermute | solution.py:138

commit v3 on v2

--- a/solution.py
+++ b/solution.py
@@ -71,10 +71,22 @@
 
 
 def stack_kernel(which, side_ref, first_ref, mates_ref, weight_ref, norm_ref, *refs):
-    near, early, late, out_ref = refs[:4], refs[4:8], refs[8:12], refs[-1]
-    chosen, rounds = weight_ref.shape[:2]
-    half, _, rows, width = near[0].shape
+    rounds = weight_ref.shape[2] // UNROLL
+    chosen = norm_ref.shape[0] // rounds
     side = side_ref[0]
+    if which == 0:
+        near, early, (out_ref, near_kept, early_kept, sems) = refs[:4], refs[4:8], refs[8:]
+        half, _, rows, width = near[0].shape
+        moves = [(near[t].at[:, 1], near_kept.at[t], sems.at[0, t]) for t in range(4)]
+        moves += [(early[t].at[:, pl.ds(rows, early_kept.shape[2])], early_kept.at[t], sems.at[1, t]) for t in range(4)]
+
+        @pl.when(pl.program_id(0) == 0)
+        def keep():
+            for move in moves:
+                pltpu.make_async_copy(*move).start()
+    else:
+        near_kept, early_kept, late, out_ref = refs[0], refs[1], refs[2:6], refs[-1]
+        half, rows, width = near_kept.shape[1:]
 
     def block(b):
         mine = b // half == side
@@ -82,11 +94,14 @@
         parts = []
         for t in range(4):
             if which == 0:
-                far = early[t ^ 2][at, :rows]
+                parts.append(jnp.where(mine, near[t][at, 0], early[t ^ 2][at, :rows]))
             else:
-                far = jnp.concatenate([early[t ^ 2][at, rows:], late[t ^ 2][at]], axis=0)
-            parts.append(jnp.where(mine, near[t][at, which], far))
+                far = jnp.concatenate([early_kept[t ^ 2, at], late[t ^ 2][at]], axis=0)
+                parts.append(jnp.where(mine, near_kept[t, at], far))
         return jnp.concatenate(parts, axis=0)
+
+    def weighted(x, column):
+        return (x.astype(jnp.float32) * weight_ref[0, :, column : column + 1]).astype(x.dtype)
 
     turn = turn_matrix(4 * rows)
     for u in range(UNROLL):
@@ -94,33 +109,45 @@
         own = block(first_ref[0] + n).T
         turned = jnp.dot(own, turn, preferred_element_type=jnp.float32).astype(own.dtype)
         left = jnp.concatenate([own, turned], axis=0)
-        right = jnp.concatenate([block(mates_ref[r * chosen + n]) * weight_ref[n, r] for r in range(rounds)], axis=1)
+        right = jnp.concatenate([weighted(block(mates_ref[r * chosen + n]), u * rounds + r) for r in range(rounds)], axis=1)
         both = jnp.dot(left, right, preferred_element_type=jnp.float32)
         for r in range(rounds):
-            total = (both[:, r * width : (r + 1) * width] * (1.0 / norm_ref[r * chosen + n])).astype(out_ref.dtype)
+            total = (both[:, r * width : (r + 1) * width] * (1.0 / norm_ref[n * rounds + r])).astype(out_ref.dtype)
             out_ref[u, r, 0, :, :width] = total[:width]
             out_ref[u, r, 0, :, width:] = total[width:]
 
 
-def stack(which, near, early, late, side, first, mates, weight, norm, into):
-    chosen, rounds, rows, width = weight.shape
-    out = jax.ShapeDtypeStruct((chosen, rounds, 2, width, 2 * width), jnp.bfloat16)
+    if which == 0:
+
+        @pl.when(pl.program_id(0) == pl.num_programs(0) - 1)
+        def kept():
+            for move in moves:
+                pltpu.make_async_copy(*move).wait()
+
+
+def stack(which, parts, side, first, mates, weight, norm, into):
+    steps, rows, columns = weight.shape
+    chosen, rounds, width = steps * UNROLL, columns // UNROLL, parts[0].shape[-1]
+    shapes = [(chosen, rounds, 2, width, 2 * width)]
     smem = pl.BlockSpec(memory_space=pltpu.SMEM)
     vmem = pl.BlockSpec(memory_space=pltpu.VMEM)
-    far = [*early, *late] if which else [*early]
-    refs = [smem, smem, smem, vmem, smem] + [vmem] * (len(near) + len(far))
+    specs = [smem, smem, smem, pl.BlockSpec((1, rows, columns), lambda n: (n, 0, 0)), smem] + [vmem] * len(parts)
+    if which == 0:
+        places, _, some = parts[0].shape[:3]
+        shapes += [(4, places, some, width), (4, places, parts[4].shape[1] - some, width)]
     more = () if into is None else (into,)
     return pl.pallas_call(
         functools.partial(stack_kernel, which),
-        out_shape=out,
-        grid=(chosen // UNROLL,),
-        in_specs=refs + [pl.BlockSpec(memory_space=pl.ANY)] * len(more),
-        out_specs=pl.BlockSpec((UNROLL, rounds, 1, width, 2 * width), lambda n: (n, 0, which, 0, 0)),
-        input_output_aliases={len(refs): 0} if more else {},
+        out_shape=[jax.ShapeDtypeStruct(shape, jnp.bfloat16) for shape in shapes],
+        grid=(steps,),
+        in_specs=specs + [pl.BlockSpec(memory_space=pl.ANY)] * len(more),
+        out_specs=[pl.BlockSpec((UNROLL, rounds, 1, width, 2 * width), lambda n: (n, 0, which, 0, 0))] + [vmem] * (len(shapes) - 1),
+        scratch_shapes=[] if which else [pltpu.SemaphoreType.DMA((2, 4))],
+        input_output_aliases={len(specs): 0} if more else {},
         compiler_params=pltpu.CompilerParams(vmem_limit_bytes=24 << 20),
         cost_estimate=pl.CostEstimate(flops=20 * chosen * rounds * 2 * width * rows * width, bytes_accessed=8 << 20, transcendentals=0),
         name="stack" + str(which),
-    )(side, first, mates, weight, norm, *near, *far, *more)
+    )(side, first, mates, weight, norm, *parts, *more)
 
 
 def per_device(spectra, counts, partner):
@@ -146,24 +173,22 @@
     shuffle = functools.partial(lax.all_to_all, axis_name=("x", "z"), split_axis=0, concat_axis=0, tiled=True)
 
     near, early, late = whiten(side, spectra.reshape(bins, windows * parts, width))
-    early, late = hand_on(early), hand_on(late)
     beside = along(counts)
     tallies = (counts, across(counts), beside, across(beside))
 
     columns = jnp.concatenate(tallies, axis=0).astype(jnp.float32)
     mine = lax.dynamic_slice_in_dim(partner, first, chosen, 1)
-    every = jnp.arange(nblocks, dtype=jnp.int32)
-    theirs_hot = (mine.reshape(rounds * chosen, 1) == every[None]).astype(jnp.float32)
-    ours_hot = (first + jnp.arange(chosen, dtype=jnp.int32)[:, None] == every[None]).astype(jnp.float32)
-    pick = functools.partial(jnp.einsum, "nb,wb->nw", precision=lax.Precision.HIGHEST)
-    theirs = pick(theirs_hot, columns).reshape(rounds, chosen, -1)
-    ours = pick(ours_hot, columns)
-    weight = jnp.minimum(ours[None], theirs) / NSAMP
-    norm = jnp.sqrt(jnp.sum(weight * weight, axis=2)).reshape(rounds * chosen)
-    wide = jnp.repeat(jnp.transpose(weight, (1, 0, 2)), parts, axis=2)
-    wide = jnp.broadcast_to(wide.astype(jnp.bfloat16)[..., None], wide.shape + (width,))
+    every = jnp.arange(nblocks, dtype=jnp.int32)[:, None]
+    theirs_hot = (mine.T.reshape(1, chosen * rounds) == every).astype(jnp.float32)
+    ours_hot = (first + jnp.arange(chosen * rounds, dtype=jnp.int32)[None] // rounds == every).astype(jnp.float32)
+    pick = functools.partial(jnp.dot, precision=lax.Precision.HIGHEST)
+    weight = jnp.minimum(pick(columns, ours_hot), pick(columns, theirs_hot)) / NSAMP
+    norm = jnp.sqrt(jnp.sum(weight * weight, axis=0))
+    steps = chosen // UNROLL
+    wide = jnp.repeat(weight, parts, axis=0).reshape(-1, steps, UNROLL * rounds).transpose(1, 0, 2)
 
     near = shuffle(near)
+    early, late = hand_on(early), hand_on(late)
     near, early, late, wide, norm = after((near, early, late, wide, norm))
     near_beside = along(near)
     near = (near, across(near), near_beside, across(near_beside))
@@ -176,10 +201,10 @@
 
     operands = (side, first.reshape(1), mine.reshape(-1), wide, norm)
     early = (early, across(early), early_beside, across(early_beside))
-    result = stack(0, near, early, None, *operands, None)
+    result, near_kept, early_kept = stack(0, (*near, *early), *operands, None)
     late_beside, result = after((late_beside, result))
     late = (late, across(late), late_beside, across(late_beside))
-    return stack(1, near, early, late, *operands, result)
+    return stack(1, (near_kept, early_kept, *late), *operands, result)[0]
 
 
 def solution(mesh):

time: 109 us -> 107 us (0.982)
  waiting for transfers between devices: 39.7 us -> 37.1 us
  Pallas kernels: 13.1 us -> 11.9 us
  starting transfers between devices: 52.2 us -> 53.4 us
    ppermute x4, waiting for transfers between devices: 12.7 us -> 10.1 us  [along(): return lax.ppermute(x, 'yl', swap_pairs)]
    all_to_all x1, waiting for transfers between devices: 5.46 us -> 6.75 us  [per_device(): late = shuffle(late)]
    broadcast_in_dim x2 -> x1, local copies, waits for them, and re-layouts: 1.3 us -> 0.05 us  [per_device(): jnp.repeat(weight, parts, axis=0).reshape(-1, steps, UNROLL * rounds)]
    all_to_all x1, waiting for transfers between devices: 2 us -> 0.76 us  [per_device(): early = shuffle(early)]
    pallas_call x2, Pallas kernels: 11.2 us -> 10 us  [stack(): pl.pallas_call(functools.partial(stack_kernel, which), out_shape=[jax.Sha...]
    unnamed x6 -> x8, local copies, waits for them, and re-layouts: 1.61 us -> 2.49 us
  transfers between devices with their start and end apart: 17 -> 17, of which waited for: 11 -> 9; matrix products, arithmetic and copies ran while one was open for 1% -> 1% of each run, Pallas kernels for 5% -> 6%
where the time goes in v3:
time: 107 us; the launch traced here: 106 us
  starting transfers between devices  53.4 us (50%)
  waiting for transfers between devices  37.1 us (35%)
  Pallas kernels  11.9 us (11%)
  local copies, waits for them, and re-layouts  3.3 us (3%)
    ppermute x8, starting transfers between devices, across(): return lax.ppermute(x, 'core', swap_pairs)  18.6 us
    ppermute x2, waiting for transfers between devices, hand_on(): return lax.ppermute(x, ('yh', 'yl'), [(0, 3), (3, 0), (1, 2), (2, 1)])  15.6 us
    all_to_all x1, starting transfers between devices, per_device(): near = shuffle(near)  11.9 us
    ppermute x4, waiting for transfers between devices, along(): return lax.ppermute(x, 'yl', swap_pairs)  10.1 us
    pallas_call x2, Pallas kernels, stack(): pl.pallas_call(functools.partial(stack_kernel, which), out_shape=[jax.Sha...  10 us
    all_to_all x1, starting transfers between devices, per_device(): early = shuffle(early)  8.93 us
    all_to_all x1, starting transfers between devices, per_device(): late = shuffle(late)  8.93 us
    all_to_all x1, waiting for transfers between devices, per_device(): late = shuffle(late)  6.75 us
  transfers between devices with their start and end apart: 17, of which 9 were waited for; matrix products, arithmetic and copies ran while one was open for 1% of the time, Pallas kernels for 6%

profile of v3, /device:TPU:1, one launch (start us, length us, event | category | flops | bytes accessed | tf_op | source)
XLA Modules:
  0.0 106.4 jit_solution(12250333920733257583)
XLA Ops:
  0.0 1.6 %copy-done.1 = bf16[1,128,32,2,128]{4,3,2,1,0:T(2,128)(2,1)S(1)} copy-done((bf16[1,128,32,2,128]{4,3,2,1,0:T(2,128)(2,1)S(1)}, bf16[1,128,32,2,128]{4,3,2,1,0:T(2,128)(2,1)}, u32[]{:S(2)}) %copy-start.1) | copy-done | bytes 2097176
  1.6 1.9 %whiten.1 = (bf16[32,2,64,128]{3,2,1,0:T(8,128)(2,1)}, bf16[32,96,128]{2,1,0:T(8,128)(2,1)S(1)}, bf16[32,32,128]{2,1,0:T(8,128)(2,1)S(1)}) custom-call(s32[1]{0:T(128)} %bitcast.side_ref, bf16[128,64,128]{2,1,0:T(8,128)(2,1)S(1)} %bitcast.8), custom_call_target="tpu_custom_call" | custom-call | tf_op jit(solution)/shard_map/whiten/pallas_call | solution.py:52
  3.5 11.9 %all-to-all-start = ((bf16[32,2,64,128]{3,2,1,0:T(8,128)(2,1)}), bf16[32,2,64,128]{3,2,1,0:T(8,128)(2,1)S(1)}, u32[]{:S(2)}, u32[]{:S(2)}) async-start(bf16[32,2,64,128]{3,2,1,0:T(8,128)(2,1)} %get-tuple-element.25), calls=%async_computation | async-start | bytes 2097152 | tf_op jit(solution)/shard_map/all_to_all | solution.py:190
  15.4 2.8 %collective-permute-start = (bf16[32,96,128]{2,1,0:T(8,128)(2,1)S(1)}, bf16[32,96,128]{2,1,0:T(8,128)(2,1)S(1)}, u32[]{:S(2)}, u32[]{:S(2)}) collective-permute-start(bf16[32,96,128]{2,1,0:T(8,128)(2,1)S(1)} %get-tuple-element.26), channel_id=1, source_target_pairs={{0,130},{130,0},{2,128},{128,2},{1,131},{131,1},{3,129},{129,3},{4... | collective-permute-start | bytes 2359304 | tf_op jit(solution)/shard_map/ppermute | solution.py:171
  18.2 1.4 %collective-permute-start.2 = (s32[32,64]{1,0:T(8,128)S(1)}, s32[32,64]{1,0:T(8,128)S(1)}, u32[]{:S(2)}, u32[]{:S(2)}) collective-permute-start(s32[32,64]{1,0:T(8,128)S(1)} %copy-done.3), channel_id=1, source_target_pairs={{0,1},{1,0},{2,3},{3,2},{4,5},{5,4},{6,7},{7,6},{8,9},{9,8},{10,11... | collective-permute-start | bytes 24584 | tf_op jit(solution)/shard_map/ppermute | solution.py:165
  19.6 0.8 collective-permute-start.1
  20.4 0.7 collective-permute-done.3
  21.1 2.1 %collective-permute-start.4 = (s32[32,64]{1,0:T(8,128)S(1)}, s32[32,64]{1,0:T(8,128)S(1)}, u32[]{:S(2)}, u32[]{:S(2)}) collective-permute-start(s32[32,64]{1,0:T(8,128)S(1)} %collective-permute-done.3), channel_id=1, source_target_pairs={{0,1},{1,0},{2,3},{3,2},{4,5},{5,4},{6,7},{7,6},{8,9},{9,8},{10,11... | collective-permute-start | bytes 24584 | tf_op jit(solution)/shard_map/ppermute | solution.py:165
  25.0 15.6 %collective-permute-done.1 = bf16[32,32,128]{2,1,0:T(8,128)(2,1)} collective-permute-done((bf16[32,32,128]{2,1,0:T(8,128)(2,1)S(1)}, bf16[32,32,128]{2,1,0:T(8,128)(2,1)}, u32[]{:S(2)}, u32[]{:S(2)}) %collective-permute-start.1) | collective-permute-done | bytes 262176 | tf_op jit(solution)/shard_map/ppermute | solution.py:171
  40.6 0.9 copy-done.2
  41.5 8.9 %all-to-all-start.1 = ((bf16[32,96,128]{2,1,0:T(8,128)(2,1)}), bf16[32,96,128]{2,1,0:T(8,128)(2,1)S(1)}, u32[]{:S(2)}, u32[]{:S(2)}) async-start(bf16[32,96,128]{2,1,0:T(8,128)(2,1)} %copy-done.2), calls=%async_computation.1 | async-start | bytes 1572864 | tf_op jit(solution)/shard_map/all_to_all | solution.py:195
  50.4 2.8 %collective-permute-start.5 = (bf16[32,2,64,128]{3,2,1,0:T(8,128)(2,1)S(1)}, bf16[32,2,64,128]{3,2,1,0:T(8,128)(2,1)}, u32[]{:S(2)}, u32[]{:S(2)}) collective-permute-start(bf16[32,2,64,128]{3,2,1,0:T(8,128)(2,1)S(1)} %all-to-all-done.refs_0_), channel_id=1, source_target_pairs={{0,1},{1,0},{2,3},{3,2},{4,5},{5,4},{6,7},{7,6},{8,9},{9,8},{10,11... | collective-permute-start | bytes 3145736 | tf_op jit(solution)/shard_map/ppermute | solution.py:165
  53.2 9.5 %collective-permute-done.6.refs_2_ = bf16[32,2,64,128]{3,2,1,0:T(8,128)(2,1)S(1)} collective-permute-done((bf16[32,2,64,128]{3,2,1,0:T(8,128)(2,1)S(1)}, bf16[32,2,64,128]{3,2,1,0:T(8,128)(2,1)S(1)}, u32[]{:S(2)}, u32[]{:S(2)}) %collective-permute-start.6) | collective-permute-done | bytes 1048608 | tf_op jit(solution)/shard_map/ppermute | solution.py:168
  62.7 4.4 %collective-permute-start.7 = (bf16[32,2,64,128]{3,2,1,0:T(8,128)(2,1)S(1)}, bf16[32,2,64,128]{3,2,1,0:T(8,128)(2,1)}, u32[]{:S(2)}, u32[]{:S(2)}) collective-permute-start(bf16[32,2,64,128]{3,2,1,0:T(8,128)(2,1)S(1)} %collective-permute-done.6.refs_2_), channel_id=1, source_target_pairs={{0,1},{1,0},{2,3},{3,2},{4,5},{5,4},{6,7},{7,6},{8,9},{9,8},{10,11... | collective-permute-start | bytes 3145736 | tf_op jit(solution)/shard_map/ppermute | solution.py:165
  67.1 0.8 all-to-all-done.1.refs_4_
  67.8 1.5 %collective-permute-start.9 = (bf16[32,96,128]{2,1,0:T(8,128)(2,1)S(1)}, bf16[32,96,128]{2,1,0:T(8,128)(2,1)}, u32[]{:S(2)}, u32[]{:S(2)}) collective-permute-start(bf16[32,96,128]{2,1,0:T(8,128)(2,1)S(1)} %all-to-all-done.1.refs_4_), channel_id=1, source_target_pairs={{0,2},{2,0},{1,3},{3,1},{4,6},{6,4},{5,7},{7,5},{8,10},{10,8},{9,1... | collective-permute-start | bytes 2359304 | tf_op jit(solution)/shard_map/ppermute | solution.py:168
  69.5 8.9 %all-to-all-start.2 = ((bf16[32,32,128]{2,1,0:T(8,128)(2,1)}), bf16[32,32,128]{2,1,0:T(8,128)(2,1)S(1)}, u32[]{:S(2)}, u32[]{:S(2)}) async-start(bf16[32,32,128]{2,1,0:T(8,128)(2,1)} %collective-permute-done.1), calls=%async_computation.2 | async-start | bytes 524288 | tf_op jit(solution)/shard_map/all_to_all | solution.py:198
  78.4 2.9 %collective-permute-start.8 = (bf16[32,96,128]{2,1,0:T(8,128)(2,1)S(1)}, bf16[32,96,128]{2,1,0:T(8,128)(2,1)}, u32[]{:S(2)}, u32[]{:S(2)}) collective-permute-start(bf16[32,96,128]{2,1,0:T(8,128)(2,1)S(1)} %all-to-all-done.1.refs_4_), channel_id=1, source_target_pairs={{0,1},{1,0},{2,3},{3,2},{4,5},{5,4},{6,7},{7,6},{8,9},{9,8},{10,11... | collective-permute-start | bytes 2359304 | tf_op jit(solution)/shard_map/ppermute | solution.py:165
  81.3 6.7 %all-to-all-done.2.refs_2_ = bf16[32,32,128]{2,1,0:T(8,128)(2,1)S(1)} async-done(((bf16[32,32,128]{2,1,0:T(8,128)(2,1)}), bf16[32,32,128]{2,1,0:T(8,128)(2,1)S(1)}, u32[]{:S(2)}, u32[]{:S(2)}) %all-to-all-start.2) | async-done | bytes 262176 | tf_op jit(solution)/shard_map/all_to_all | solution.py:198
  88.1 4.2 %collective-permute-start.10 = (bf16[32,96,128]{2,1,0:T(8,128)(2,1)}, bf16[32,96,128]{2,1,0:T(8,128)(2,1)}, u32[]{:S(2)}, u32[]{:S(2)}) collective-permute-start(bf16[32,96,128]{2,1,0:T(8,128)(2,1)} %collective-permute-done.9.refs_6_), channel_id=1, source_target_pairs={{0,1},{1,0},{2,3},{3,2},{4,5},{5,4},{6,7},{7,6},{8,9},{9,8},{10,11... | collective-permute-start | bytes 2359304 | tf_op jit(solution)/shard_map/ppermute | solution.py:165
  92.8 1.8 %collective-permute-done.10.refs_7_ = bf16[32,96,128]{2,1,0:T(8,128)(2,1)} collective-permute-done((bf16[32,96,128]{2,1,0:T(8,128)(2,1)}, bf16[32,96,128]{2,1,0:T(8,128)(2,1)}, u32[]{:S(2)}, u32[]{:S(2)}) %collective-permute-start.10) | collective-permute-done | bytes 786464 | tf_op jit(solution)/shard_map/ppermute | solution.py:165
  94.6 6.0 %stack0.1 = (bf16[16,2,2,128,256]{4,3,2,1,0:T(8,128)(2,1)}, bf16[4,32,64,128]{3,2,1,0:T(8,128)(2,1)S(1)}, bf16[4,32,32,128]{3,2,1,0:T(8,128)(2,1)S(1)}) custom-call(s32[1]{0:T(128)} %bitcast.side_ref, s32[1]{0:T(128)} %bitcast.1.first_ref, s32[32]{0:T(128)S(1)} %reshape.55.mates_ref, f32[2,256,16]{2,1,0:T(8,128)S(1)} %bitcast.9, f32[32]{0:T(128)S(1)} %sqrt.3.norm_ref, ...), custom_call_target="tpu_custom_call" | custom-call | flops 5368709120 | bytes 8388608 | tf_op jit(solution)/shard_map/stack0/pallas_call | solution.py:139
  101.2 1.2 %collective-permute-done.13.refs_5_ = bf16[32,32,128]{2,1,0:T(8,128)(2,1)S(1)} collective-permute-done((bf16[32,32,128]{2,1,0:T(8,128)(2,1)S(1)}, bf16[32,32,128]{2,1,0:T(8,128)(2,1)S(1)}, u32[]{:S(2)}, u32[]{:S(2)}) %collective-permute-start.13) | collective-permute-done | bytes 262176 | tf_op jit(solution)/shard_map/ppermute | solution.py:165
  102.4 4.0 %stack1.1 = bf16[16,2,2,128,256]{4,3,2,1,0:T(8,128)(2,1)} custom-call(s32[1]{0:T(128)} %bitcast.side_ref, s32[1]{0:T(128)} %bitcast.1.first_ref, s32[32]{0:T(128)S(1)} %reshape.55.mates_ref, f32[2,256,16]{2,1,0:T(8,128)S(1)} %bitcast.10, f32[32]{0:T(128)S(1)} %sqrt.3.norm_ref, ...), custom_call_target="tpu_custom_call", output_to_operand_aliasing={{}: (11, {})} | custom-call | flops 5368709120 | bytes 8388608 | tf_op jit(solution)/shard_map/stack1/pallas_call | solution.py:139
  (34 shorter events, 3.1 us)
Async XLA Ops:
  0.0 20.4 %copy-start = (s32[2,64]{1,0:T(2,128)S(1)}, s32[2,64]{1,0:T(2,128)}, u32[]{:S(2)}) copy-start(s32[2,64]{1,0:T(2,128)} %param.5) | copy-start | bytes 1540
  0.0 1.6 %copy-start.1 = (bf16[1,128,32,2,128]{4,3,2,1,0:T(2,128)(2,1)S(1)}, bf16[1,128,32,2,128]{4,3,2,1,0:T(2,128)(2,1)}, u32[]{:S(2)}) copy-start(bf16[1,128,32,2,128]{4,3,2,1,0:T(2,128)(2,1)} %param.3) | copy-start | bytes 6291460
  1.6 16.6 %copy-start.3 = (s32[32,64]{1,0:T(8,128)S(1)}, s32[32,64]{1,0:T(8,128)}, u32[]{:S(2)}) copy-start(s32[32,64]{1,0:T(8,128)} %param.4) | copy-start | bytes 24580
  3.5 37.1 %all-to-all-start = ((bf16[32,2,64,128]{3,2,1,0:T(8,128)(2,1)}), bf16[32,2,64,128]{3,2,1,0:T(8,128)(2,1)S(1)}, u32[]{:S(2)}, u32[]{:S(2)}) async-start(bf16[32,2,64,128]{3,2,1,0:T(8,128)(2,1)} %get-tuple-element.25), calls=%async_computation | async-start | bytes 2097152 | tf_op jit(solution)/shard_map/all_to_all | solution.py:190
  15.4 25.2 %collective-permute-start = (bf16[32,96,128]{2,1,0:T(8,128)(2,1)S(1)}, bf16[32,96,128]{2,1,0:T(8,128)(2,1)S(1)}, u32[]{:S(2)}, u32[]{:S(2)}) collective-permute-start(bf16[32,96,128]{2,1,0:T(8,128)(2,1)S(1)} %get-tuple-element.26), channel_id=1, source_target_pairs={{0,130},{130,0},{2,128},{128,2},{1,131},{131,1},{3,129},{129,3},{4... | collective-permute-start | bytes 2359304 | tf_op jit(solution)/shard_map/ppermute | solution.py:171
  18.2 2.9 %collective-permute-start.3 = (s32[32,64]{1,0:T(8,128)S(1)}, s32[32,64]{1,0:T(8,128)S(1)}, u32[]{:S(2)}, u32[]{:S(2)}) collective-permute-start(s32[32,64]{1,0:T(8,128)S(1)} %copy-done.3), channel_id=1, source_target_pairs={{0,2},{2,0},{1,3},{3,1},{4,6},{6,4},{5,7},{7,5},{8,10},{10,8},{9,1... | collective-permute-start | bytes 24584 | tf_op jit(solution)/shard_map/ppermute | solution.py:168
  18.2 5.2 %collective-permute-start.2 = (s32[32,64]{1,0:T(8,128)S(1)}, s32[32,64]{1,0:T(8,128)S(1)}, u32[]{:S(2)}, u32[]{:S(2)}) collective-permute-start(s32[32,64]{1,0:T(8,128)S(1)} %copy-done.3), channel_id=1, source_target_pairs={{0,1},{1,0},{2,3},{3,2},{4,5},{5,4},{6,7},{7,6},{8,9},{9,8},{10,11... | collective-permute-start | bytes 24584 | tf_op jit(solution)/shard_map/ppermute | solution.py:165
  19.6 21.0 %collective-permute-start.1 = (bf16[32,32,128]{2,1,0:T(8,128)(2,1)S(1)}, bf16[32,32,128]{2,1,0:T(8,128)(2,1)}, u32[]{:S(2)}, u32[]{:S(2)}) collective-permute-start(bf16[32,32,128]{2,1,0:T(8,128)(2,1)S(1)} %get-tuple-element.27), channel_id=1, source_target_pairs={{0,130},{130,0},{2,128},{128,2},{1,131},{131,1},{3,129},{129,3},{4... | collective-permute-start | bytes 786440 | tf_op jit(solution)/shard_map/ppermute | solution.py:171
  21.1 2.9 %collective-permute-start.4 = (s32[32,64]{1,0:T(8,128)S(1)}, s32[32,64]{1,0:T(8,128)S(1)}, u32[]{:S(2)}, u32[]{:S(2)}) collective-permute-start(s32[32,64]{1,0:T(8,128)S(1)} %collective-permute-done.3), channel_id=1, source_target_pairs={{0,1},{1,0},{2,3},{3,2},{4,5},{5,4},{6,7},{7,6},{8,9},{9,8},{10,11... | collective-permute-start | bytes 24584 | tf_op jit(solution)/shard_map/ppermute | solution.py:165
  40.6 0.9 copy-start.2
  41.5 21.2 %collective-permute-start.6 = (bf16[32,2,64,128]{3,2,1,0:T(8,128)(2,1)S(1)}, bf16[32,2,64,128]{3,2,1,0:T(8,128)(2,1)S(1)}, u32[]{:S(2)}, u32[]{:S(2)}) collective-permute-start(bf16[32,2,64,128]{3,2,1,0:T(8,128)(2,1)S(1)} %all-to-all-done.refs_0_), channel_id=1, source_target_pairs={{0,2},{2,0},{1,3},{3,1},{4,6},{6,4},{5,7},{7,5},{8,10},{10,8},{9,1... | collective-permute-start | bytes 3145736 | tf_op jit(solution)/shard_map/ppermute | solution.py:168
  41.5 26.3 %all-to-all-start.1 = ((bf16[32,96,128]{2,1,0:T(8,128)(2,1)}), bf16[32,96,128]{2,1,0:T(8,128)(2,1)S(1)}, u32[]{:S(2)}, u32[]{:S(2)}) async-start(bf16[32,96,128]{2,1,0:T(8,128)(2,1)} %copy-done.2), calls=%async_computation.1 | async-start | bytes 1572864 | tf_op jit(solution)/shard_map/all_to_all | solution.py:195
  50.4 18.9 %collective-permute-start.5 = (bf16[32,2,64,128]{3,2,1,0:T(8,128)(2,1)S(1)}, bf16[32,2,64,128]{3,2,1,0:T(8,128)(2,1)}, u32[]{:S(2)}, u32[]{:S(2)}) collective-permute-start(bf16[32,2,64,128]{3,2,1,0:T(8,128)(2,1)S(1)} %all-to-all-done.refs_0_), channel_id=1, source_target_pairs={{0,1},{1,0},{2,3},{3,2},{4,5},{5,4},{6,7},{7,6},{8,9},{9,8},{10,11... | collective-permute-start | bytes 3145736 | tf_op jit(solution)/shard_map/ppermute | solution.py:165
  62.7 6.8 %collective-permute-start.7 = (bf16[32,2,64,128]{3,2,1,0:T(8,128)(2,1)S(1)}, bf16[32,2,64,128]{3,2,1,0:T(8,128)(2,1)}, u32[]{:S(2)}, u32[]{:S(2)}) collective-permute-start(bf16[32,2,64,128]{3,2,1,0:T(8,128)(2,1)S(1)} %collective-permute-done.6.refs_2_), channel_id=1, source_target_pairs={{0,1},{1,0},{2,3},{3,2},{4,5},{5,4},{6,7},{7,6},{8,9},{9,8},{10,11... | collective-permute-start | bytes 3145736 | tf_op jit(solution)/shard_map/ppermute | solution.py:165
  67.8 13.5 %collective-permute-start.9 = (bf16[32,96,128]{2,1,0:T(8,128)(2,1)S(1)}, bf16[32,96,128]{2,1,0:T(8,128)(2,1)}, u32[]{:S(2)}, u32[]{:S(2)}) collective-permute-start(bf16[32,96,128]{2,1,0:T(8,128)(2,1)S(1)} %all-to-all-done.1.refs_4_), channel_id=1, source_target_pairs={{0,2},{2,0},{1,3},{3,1},{4,6},{6,4},{5,7},{7,5},{8,10},{10,8},{9,1... | collective-permute-start | bytes 2359304 | tf_op jit(solution)/shard_map/ppermute | solution.py:168
  69.5 18.6 %all-to-all-start.2 = ((bf16[32,32,128]{2,1,0:T(8,128)(2,1)}), bf16[32,32,128]{2,1,0:T(8,128)(2,1)S(1)}, u32[]{:S(2)}, u32[]{:S(2)}) async-start(bf16[32,32,128]{2,1,0:T(8,128)(2,1)} %collective-permute-done.1), calls=%async_computation.2 | async-start | bytes 524288 | tf_op jit(solution)/shard_map/all_to_all | solution.py:198
  78.4 14.3 %collective-permute-start.8 = (bf16[32,96,128]{2,1,0:T(8,128)(2,1)S(1)}, bf16[32,96,128]{2,1,0:T(8,128)(2,1)}, u32[]{:S(2)}, u32[]{:S(2)}) collective-permute-start(bf16[32,96,128]{2,1,0:T(8,128)(2,1)S(1)} %all-to-all-done.1.refs_4_), channel_id=1, source_target_pairs={{0,1},{1,0},{2,3},{3,2},{4,5},{5,4},{6,7},{7,6},{8,9},{9,8},{10,11... | collective-permute-start | bytes 2359304 | tf_op jit(solution)/shard_map/ppermute | solution.py:165
  88.1 6.5 %collective-permute-start.10 = (bf16[32,96,128]{2,1,0:T(8,128)(2,1)}, bf16[32,96,128]{2,1,0:T(8,128)(2,1)}, u32[]{:S(2)}, u32[]{:S(2)}) collective-permute-start(bf16[32,96,128]{2,1,0:T(8,128)(2,1)} %collective-permute-done.9.refs_6_), channel_id=1, source_target_pairs={{0,1},{1,0},{2,3},{3,2},{4,5},{5,4},{6,7},{7,6},{8,9},{9,8},{10,11... | collective-permute-start | bytes 2359304 | tf_op jit(solution)/shard_map/ppermute | solution.py:165
  92.5 8.2 %collective-permute-start.12 = (bf16[32,32,128]{2,1,0:T(8,128)(2,1)S(1)}, bf16[32,32,128]{2,1,0:T(8,128)(2,1)S(1)}, u32[]{:S(2)}, u32[]{:S(2)}) collective-permute-start(bf16[32,32,128]{2,1,0:T(8,128)(2,1)S(1)} %all-to-all-done.2.refs_2_), channel_id=1, source_target_pairs={{0,2},{2,0},{1,3},{3,1},{4,6},{6,4},{5,7},{7,5},{8,10},{10,8},{9,1... | collective-permute-start | bytes 786440 | tf_op jit(solution)/shard_map/ppermute | solution.py:168
  92.5 8.7 %collective-permute-start.11 = (bf16[32,32,128]{2,1,0:T(8,128)(2,1)S(1)}, bf16[32,32,128]{2,1,0:T(8,128)(2,1)S(1)}, u32[]{:S(2)}, u32[]{:S(2)}) collective-permute-start(bf16[32,32,128]{2,1,0:T(8,128)(2,1)S(1)} %all-to-all-done.2.refs_2_), channel_id=1, source_target_pairs={{0,1},{1,0},{2,3},{3,2},{4,5},{5,4},{6,7},{7,6},{8,9},{9,8},{10,11... | collective-permute-start | bytes 786440 | tf_op jit(solution)/shard_map/ppermute | solution.py:165
  100.6 1.7 %collective-permute-start.13 = (bf16[32,32,128]{2,1,0:T(8,128)(2,1)S(1)}, bf16[32,32,128]{2,1,0:T(8,128)(2,1)S(1)}, u32[]{:S(2)}, u32[]{:S(2)}) collective-permute-start(bf16[32,32,128]{2,1,0:T(8,128)(2,1)S(1)} %collective-permute-done.12.refs_4_), channel_id=1, source_target_pairs={{0,1},{1,0},{2,3},{3,2},{4,5},{5,4},{6,7},{7,6},{8,9},{9,8},{10,11... | collective-permute-start | bytes 786440 | tf_op jit(solution)/shard_map/ppermute | solution.py:165

commit v4 on v3

--- a/solution.py
+++ b/solution.py
@@ -189,8 +189,8 @@
 
     near = shuffle(near)
     early, late = hand_on(early), hand_on(late)
-    near, early, late, wide, norm = after((near, early, late, wide, norm))
-    near_beside = along(near)
+    near, early, wide, norm = after((near, early, wide, norm))
+    near_beside, late = after((along(near), late))
     near = (near, across(near), near_beside, across(near_beside))
     early = shuffle(early)
     late, near = after((late, near))

time: 107 us -> 105 us (0.981)
  waiting for transfers between devices: 37.1 us -> 35.1 us
  starting transfers between devices: 53.4 us -> 54.6 us
    all_to_all x1, waiting for transfers between devices: 0.01 us -> 5.1 us  [per_device(): near = shuffle(near)]
    ppermute x4, waiting for transfers between devices: 10.1 us -> 6.74 us  [along(): return lax.ppermute(x, 'yl', swap_pairs)]
    all_to_all x1, waiting for transfers between devices: 0.76 us -> 3.15 us  [per_device(): early = shuffle(early)]
    all_to_all x1, waiting for transfers between devices: 6.75 us -> 4.47 us  [per_device(): late = shuffle(late)]
    ppermute x2, waiting for transfers between devices: 15.6 us -> 13.3 us  [hand_on(): return lax.ppermute(x, ('yh', 'yl'), [(0, 3), (3, 0), (1, 2), (2, 1)])]
    ppermute x8, waiting for transfers between devices: 3.83 us -> 2.34 us  [across(): return lax.ppermute(x, 'core', swap_pairs)]
    ppermute x4, starting transfers between devices: 1.47 us -> 2.77 us  [along(): return lax.ppermute(x, 'yl', swap_pairs)]
    ppermute x2, starting transfers between devices: 3.6 us -> 4.81 us  [hand_on(): return lax.ppermute(x, ('yh', 'yl'), [(0, 3), (3, 0), (1, 2), (2, 1)])]
  transfers between devices with their start and end apart: 17 -> 17, of which waited for: 9 -> 11; matrix products, arithmetic and copies ran while one was open for 1% -> 1% of each run, Pallas kernels for 6% -> 6%
where the time goes in v4:
time: 105 us
  starting transfers between devices  54.6 us (52%)
  waiting for transfers between devices  35.1 us (33%)
  Pallas kernels  11.9 us (11%)
  local copies, waits for them, and re-layouts  2.43 us (2%)
    ppermute x8, starting transfers between devices, across(): return lax.ppermute(x, 'core', swap_pairs)  18.2 us
    ppermute x2, waiting for transfers between devices, hand_on(): return lax.ppermute(x, ('yh', 'yl'), [(0, 3), (3, 0), (1, 2), (2, 1)])  13.3 us
    all_to_all x1, starting transfers between devices, per_device(): near = shuffle(near)  11.9 us
    pallas_call x2, Pallas kernels, stack(): pl.pallas_call(functools.partial(stack_kernel, which), out_shape=[jax.Sha...  10 us
    all_to_all x1, starting transfers between devices, per_device(): early = shuffle(early)  8.58 us
    all_to_all x1, starting transfers between devices, per_device(): late = shuffle(late)  8.34 us
    ppermute x4, waiting for transfers between devices, along(): return lax.ppermute(x, 'yl', swap_pairs)  6.74 us
    all_to_all x1, waiting for transfers between devices, per_device(): near = shuffle(near)  5.1 us
  transfers between devices with their start and end apart: 17, of which 11 were waited for; matrix products, arithmetic and copies ran while one was open for 1% of the time, Pallas kernels for 6%

profile of v4, /device:TPU:1, one launch (start us, length us, event | category | flops | bytes accessed | tf_op | source)
XLA Modules:
  0.0 104.7 jit_solution(2005874722586526261)
XLA Ops:
  0.0 1.6 %copy-done.1 = bf16[1,128,32,2,128]{4,3,2,1,0:T(2,128)(2,1)S(1)} copy-done((bf16[1,128,32,2,128]{4,3,2,1,0:T(2,128)(2,1)S(1)}, bf16[1,128,32,2,128]{4,3,2,1,0:T(2,128)(2,1)}, u32[]{:S(2)}) %copy-start.1) | copy-done | bytes 2097176
  1.6 1.9 %whiten.1 = (bf16[32,2,64,128]{3,2,1,0:T(8,128)(2,1)}, bf16[32,96,128]{2,1,0:T(8,128)(2,1)S(1)}, bf16[32,32,128]{2,1,0:T(8,128)(2,1)S(1)}) custom-call(s32[1]{0:T(128)} %bitcast.side_ref, bf16[128,64,128]{2,1,0:T(8,128)(2,1)S(1)} %bitcast.8), custom_call_target="tpu_custom_call" | custom-call | tf_op jit(solution)/shard_map/whiten/pallas_call | solution.py:52
  3.5 11.9 %all-to-all-start = ((bf16[32,2,64,128]{3,2,1,0:T(8,128)(2,1)}), bf16[32,2,64,128]{3,2,1,0:T(8,128)(2,1)S(1)}, u32[]{:S(2)}, u32[]{:S(2)}) async-start(bf16[32,2,64,128]{3,2,1,0:T(8,128)(2,1)} %get-tuple-element.26), calls=%async_computation | async-start | bytes 2097152 | tf_op jit(solution)/shard_map/all_to_all | solution.py:190
  15.4 2.8 %collective-permute-start = (bf16[32,96,128]{2,1,0:T(8,128)(2,1)S(1)}, bf16[32,96,128]{2,1,0:T(8,128)(2,1)S(1)}, u32[]{:S(2)}, u32[]{:S(2)}) collective-permute-start(bf16[32,96,128]{2,1,0:T(8,128)(2,1)S(1)} %get-tuple-element.27), channel_id=1, source_target_pairs={{0,130},{130,0},{2,128},{128,2},{1,131},{131,1},{3,129},{129,3},{4... | collective-permute-start | bytes 2359304 | tf_op jit(solution)/shard_map/ppermute | solution.py:171
  18.2 1.4 %collective-permute-start.1 = (s32[32,64]{1,0:T(8,128)S(1)}, s32[32,64]{1,0:T(8,128)S(1)}, u32[]{:S(2)}, u32[]{:S(2)}) collective-permute-start(s32[32,64]{1,0:T(8,128)S(1)} %copy-done.3), channel_id=1, source_target_pairs={{0,1},{1,0},{2,3},{3,2},{4,5},{5,4},{6,7},{7,6},{8,9},{9,8},{10,11... | collective-permute-start | bytes 24584 | tf_op jit(solution)/shard_map/ppermute | solution.py:165
  19.7 1.4 %collective-permute-done.2 = s32[32,64]{1,0:T(8,128)S(1)} collective-permute-done((s32[32,64]{1,0:T(8,128)S(1)}, s32[32,64]{1,0:T(8,128)S(1)}, u32[]{:S(2)}, u32[]{:S(2)}) %collective-permute-start.2) | collective-permute-done | bytes 8224 | tf_op jit(solution)/shard_map/ppermute | solution.py:168
  21.1 2.1 %collective-permute-start.3 = (s32[32,64]{1,0:T(8,128)S(1)}, s32[32,64]{1,0:T(8,128)S(1)}, u32[]{:S(2)}, u32[]{:S(2)}) collective-permute-start(s32[32,64]{1,0:T(8,128)S(1)} %collective-permute-done.2), channel_id=1, source_target_pairs={{0,1},{1,0},{2,3},{3,2},{4,5},{5,4},{6,7},{7,6},{8,9},{9,8},{10,11... | collective-permute-start | bytes 24584 | tf_op jit(solution)/shard_map/ppermute | solution.py:165
  25.0 9.9 %collective-permute-done = bf16[32,96,128]{2,1,0:T(8,128)(2,1)S(1)} collective-permute-done((bf16[32,96,128]{2,1,0:T(8,128)(2,1)S(1)}, bf16[32,96,128]{2,1,0:T(8,128)(2,1)S(1)}, u32[]{:S(2)}, u32[]{:S(2)}) %collective-permute-start) | collective-permute-done | bytes 786464 | tf_op jit(solution)/shard_map/ppermute | solution.py:171
  34.9 5.1 %all-to-all-done.refs_0_ = bf16[32,2,64,128]{3,2,1,0:T(8,128)(2,1)S(1)} async-done(((bf16[32,2,64,128]{3,2,1,0:T(8,128)(2,1)}), bf16[32,2,64,128]{3,2,1,0:T(8,128)(2,1)S(1)}, u32[]{:S(2)}, u32[]{:S(2)}) %all-to-all-start) | async-done | bytes 1048608 | tf_op jit(solution)/shard_map/all_to_all | solution.py:190
  40.0 1.3 %collective-permute-start.4 = (bf16[32,2,64,128]{3,2,1,0:T(8,128)(2,1)S(1)}, bf16[32,2,64,128]{3,2,1,0:T(8,128)(2,1)S(1)}, u32[]{:S(2)}, u32[]{:S(2)}) collective-permute-start(bf16[32,2,64,128]{3,2,1,0:T(8,128)(2,1)S(1)} %all-to-all-done.refs_0_), channel_id=1, source_target_pairs={{0,2},{2,0},{1,3},{3,1},{4,6},{6,4},{5,7},{7,5},{8,10},{10,8},{9,1... | collective-permute-start | bytes 3145736 | tf_op jit(solution)/shard_map/ppermute | solution.py:168
  41.3 8.6 %all-to-all-start.1 = ((bf16[32,96,128]{2,1,0:T(8,128)(2,1)}), bf16[32,96,128]{2,1,0:T(8,128)(2,1)S(1)}, u32[]{:S(2)}, u32[]{:S(2)}) async-start(bf16[32,96,128]{2,1,0:T(8,128)(2,1)} %copy-done.2), calls=%async_computation.1 | async-start | bytes 1572864 | tf_op jit(solution)/shard_map/all_to_all | solution.py:195
  49.9 2.0 %collective-permute-start.5 = (bf16[32,32,128]{2,1,0:T(8,128)(2,1)S(1)}, bf16[32,32,128]{2,1,0:T(8,128)(2,1)}, u32[]{:S(2)}, u32[]{:S(2)}) collective-permute-start(bf16[32,32,128]{2,1,0:T(8,128)(2,1)S(1)} %get-tuple-element.31), channel_id=1, source_target_pairs={{0,130},{130,0},{2,128},{128,2},{1,131},{131,1},{3,129},{129,3},{4... | collective-permute-start | bytes 786440 | tf_op jit(solution)/shard_map/ppermute | solution.py:171
  51.9 2.0 %collective-permute-start.6 = (bf16[32,2,64,128]{3,2,1,0:T(8,128)(2,1)S(1)}, bf16[32,2,64,128]{3,2,1,0:T(8,128)(2,1)}, u32[]{:S(2)}, u32[]{:S(2)}) collective-permute-start(bf16[32,2,64,128]{3,2,1,0:T(8,128)(2,1)S(1)} %all-to-all-done.refs_0_), channel_id=1, source_target_pairs={{0,1},{1,0},{2,3},{3,2},{4,5},{5,4},{6,7},{7,6},{8,9},{9,8},{10,11... | collective-permute-start | bytes 3145736 | tf_op jit(solution)/shard_map/ppermute | solution.py:165
  53.9 3.4 %collective-permute-done.5 = bf16[32,32,128]{2,1,0:T(8,128)(2,1)} collective-permute-done((bf16[32,32,128]{2,1,0:T(8,128)(2,1)S(1)}, bf16[32,32,128]{2,1,0:T(8,128)(2,1)}, u32[]{:S(2)}, u32[]{:S(2)}) %collective-permute-start.5) | collective-permute-done | bytes 262176 | tf_op jit(solution)/shard_map/ppermute | solution.py:171
  57.4 2.3 %collective-permute-done.4.refs_2_ = bf16[32,2,64,128]{3,2,1,0:T(8,128)(2,1)S(1)} collective-permute-done((bf16[32,2,64,128]{3,2,1,0:T(8,128)(2,1)S(1)}, bf16[32,2,64,128]{3,2,1,0:T(8,128)(2,1)S(1)}, u32[]{:S(2)}, u32[]{:S(2)}) %collective-permute-start.4) | collective-permute-done | bytes 1048608 | tf_op jit(solution)/shard_map/ppermute | solution.py:168
  59.7 5.9 %collective-permute-start.7 = (bf16[32,2,64,128]{3,2,1,0:T(8,128)(2,1)S(1)}, bf16[32,2,64,128]{3,2,1,0:T(8,128)(2,1)}, u32[]{:S(2)}, u32[]{:S(2)}) collective-permute-start(bf16[32,2,64,128]{3,2,1,0:T(8,128)(2,1)S(1)} %collective-permute-done.4.refs_2_), channel_id=1, source_target_pairs={{0,1},{1,0},{2,3},{3,2},{4,5},{5,4},{6,7},{7,6},{8,9},{9,8},{10,11... | collective-permute-start | bytes 3145736 | tf_op jit(solution)/shard_map/ppermute | solution.py:165
  65.6 3.1 %all-to-all-done.1.refs_4_ = bf16[32,96,128]{2,1,0:T(8,128)(2,1)S(1)} async-done(((bf16[32,96,128]{2,1,0:T(8,128)(2,1)}), bf16[32,96,128]{2,1,0:T(8,128)(2,1)S(1)}, u32[]{:S(2)}, u32[]{:S(2)}) %all-to-all-start.1) | async-done | bytes 786464 | tf_op jit(solution)/shard_map/all_to_all | solution.py:195
  68.9 8.3 %all-to-all-start.2 = ((bf16[32,32,128]{2,1,0:T(8,128)(2,1)}), bf16[32,32,128]{2,1,0:T(8,128)(2,1)S(1)}, u32[]{:S(2)}, u32[]{:S(2)}) async-start(bf16[32,32,128]{2,1,0:T(8,128)(2,1)} %collective-permute-done.5), calls=%async_computation.2 | async-start | bytes 524288 | tf_op jit(solution)/shard_map/all_to_all | solution.py:198
  77.3 2.2 %collective-permute-start.8 = (bf16[32,96,128]{2,1,0:T(8,128)(2,1)S(1)}, bf16[32,96,128]{2,1,0:T(8,128)(2,1)}, u32[]{:S(2)}, u32[]{:S(2)}) collective-permute-start(bf16[32,96,128]{2,1,0:T(8,128)(2,1)S(1)} %all-to-all-done.1.refs_4_), channel_id=1, source_target_pairs={{0,1},{1,0},{2,3},{3,2},{4,5},{5,4},{6,7},{7,6},{8,9},{9,8},{10,11... | collective-permute-start | bytes 2359304 | tf_op jit(solution)/shard_map/ppermute | solution.py:165
  79.5 3.0 %collective-permute-done.9.refs_6_ = bf16[32,96,128]{2,1,0:T(8,128)(2,1)} collective-permute-done((bf16[32,96,128]{2,1,0:T(8,128)(2,1)S(1)}, bf16[32,96,128]{2,1,0:T(8,128)(2,1)}, u32[]{:S(2)}, u32[]{:S(2)}) %collective-permute-start.9) | collective-permute-done | bytes 786464 | tf_op jit(solution)/shard_map/ppermute | solution.py:168
  82.5 4.5 %all-to-all-done.2.refs_2_ = bf16[32,32,128]{2,1,0:T(8,128)(2,1)S(1)} async-done(((bf16[32,32,128]{2,1,0:T(8,128)(2,1)}), bf16[32,32,128]{2,1,0:T(8,128)(2,1)S(1)}, u32[]{:S(2)}, u32[]{:S(2)}) %all-to-all-start.2) | async-done | bytes 262176 | tf_op jit(solution)/shard_map/all_to_all | solution.py:198
  86.9 3.8 %collective-permute-start.10 = (bf16[32,96,128]{2,1,0:T(8,128)(2,1)}, bf16[32,96,128]{2,1,0:T(8,128)(2,1)}, u32[]{:S(2)}, u32[]{:S(2)}) collective-permute-start(bf16[32,96,128]{2,1,0:T(8,128)(2,1)} %collective-permute-done.9.refs_6_), channel_id=1, source_target_pairs={{0,1},{1,0},{2,3},{3,2},{4,5},{5,4},{6,7},{7,6},{8,9},{9,8},{10,11... | collective-permute-start | bytes 2359304 | tf_op jit(solution)/shard_map/ppermute | solution.py:165
  92.9 6.0 %stack0.1 = (bf16[16,2,2,128,256]{4,3,2,1,0:T(8,128)(2,1)}, bf16[4,32,64,128]{3,2,1,0:T(8,128)(2,1)S(1)}, bf16[4,32,32,128]{3,2,1,0:T(8,128)(2,1)S(1)}) custom-call(s32[1]{0:T(128)} %bitcast.side_ref, s32[1]{0:T(128)} %bitcast.1.first_ref, s32[32]{0:T(128)S(1)} %reshape.55.mates_ref, f32[2,256,16]{2,1,0:T(8,128)S(1)} %bitcast.9, f32[32]{0:T(128)S(1)} %sqrt.3.norm_ref, ...), custom_call_target="tpu_custom_call" | custom-call | flops 5368709120 | bytes 8388608 | tf_op jit(solution)/shard_map/stack0/pallas_call | solution.py:139
  100.7 4.0 %stack1.1 = bf16[16,2,2,128,256]{4,3,2,1,0:T(8,128)(2,1)} custom-call(s32[1]{0:T(128)} %bitcast.side_ref, s32[1]{0:T(128)} %bitcast.1.first_ref, s32[32]{0:T(128)S(1)} %reshape.55.mates_ref, f32[2,256,16]{2,1,0:T(8,128)S(1)} %bitcast.10, f32[32]{0:T(128)S(1)} %sqrt.3.norm_ref, ...), custom_call_target="tpu_custom_call", output_to_operand_aliasing={{}: (11, {})} | custom-call | flops 5368709120 | bytes 8388608 | tf_op jit(solution)/shard_map/stack1/pallas_call | solution.py:139
  (34 shorter events, 6.0 us)
Async XLA Ops:
  0.0 19.6 %copy-start = (s32[2,64]{1,0:T(2,128)S(1)}, s32[2,64]{1,0:T(2,128)}, u32[]{:S(2)}) copy-start(s32[2,64]{1,0:T(2,128)} %param.5) | copy-start | bytes 1540
  0.0 1.6 %copy-start.1 = (bf16[1,128,32,2,128]{4,3,2,1,0:T(2,128)(2,1)S(1)}, bf16[1,128,32,2,128]{4,3,2,1,0:T(2,128)(2,1)}, u32[]{:S(2)}) copy-start(bf16[1,128,32,2,128]{4,3,2,1,0:T(2,128)(2,1)} %param.3) | copy-start | bytes 6291460
  1.6 16.6 %copy-start.3 = (s32[32,64]{1,0:T(8,128)S(1)}, s32[32,64]{1,0:T(8,128)}, u32[]{:S(2)}) copy-start(s32[32,64]{1,0:T(8,128)} %param.4) | copy-start | bytes 24580
  3.5 36.5 %all-to-all-start = ((bf16[32,2,64,128]{3,2,1,0:T(8,128)(2,1)}), bf16[32,2,64,128]{3,2,1,0:T(8,128)(2,1)S(1)}, u32[]{:S(2)}, u32[]{:S(2)}) async-start(bf16[32,2,64,128]{3,2,1,0:T(8,128)(2,1)} %get-tuple-element.26), calls=%async_computation | async-start | bytes 2097152 | tf_op jit(solution)/shard_map/all_to_all | solution.py:190
  15.4 19.5 %collective-permute-start = (bf16[32,96,128]{2,1,0:T(8,128)(2,1)S(1)}, bf16[32,96,128]{2,1,0:T(8,128)(2,1)S(1)}, u32[]{:S(2)}, u32[]{:S(2)}) collective-permute-start(bf16[32,96,128]{2,1,0:T(8,128)(2,1)S(1)} %get-tuple-element.27), channel_id=1, source_target_pairs={{0,130},{130,0},{2,128},{128,2},{1,131},{131,1},{3,129},{129,3},{4... | collective-permute-start | bytes 2359304 | tf_op jit(solution)/shard_map/ppermute | solution.py:171
  18.2 2.9 %collective-permute-start.2 = (s32[32,64]{1,0:T(8,128)S(1)}, s32[32,64]{1,0:T(8,128)S(1)}, u32[]{:S(2)}, u32[]{:S(2)}) collective-permute-start(s32[32,64]{1,0:T(8,128)S(1)} %copy-done.3), channel_id=1, source_target_pairs={{0,2},{2,0},{1,3},{3,1},{4,6},{6,4},{5,7},{7,5},{8,10},{10,8},{9,1... | collective-permute-start | bytes 24584 | tf_op jit(solution)/shard_map/ppermute | solution.py:168
  18.2 5.2 %collective-permute-start.1 = (s32[32,64]{1,0:T(8,128)S(1)}, s32[32,64]{1,0:T(8,128)S(1)}, u32[]{:S(2)}, u32[]{:S(2)}) collective-permute-start(s32[32,64]{1,0:T(8,128)S(1)} %copy-done.3), channel_id=1, source_target_pairs={{0,1},{1,0},{2,3},{3,2},{4,5},{5,4},{6,7},{7,6},{8,9},{9,8},{10,11... | collective-permute-start | bytes 24584 | tf_op jit(solution)/shard_map/ppermute | solution.py:165
  21.1 2.9 %collective-permute-start.3 = (s32[32,64]{1,0:T(8,128)S(1)}, s32[32,64]{1,0:T(8,128)S(1)}, u32[]{:S(2)}, u32[]{:S(2)}) collective-permute-start(s32[32,64]{1,0:T(8,128)S(1)} %collective-permute-done.2), channel_id=1, source_target_pairs={{0,1},{1,0},{2,3},{3,2},{4,5},{5,4},{6,7},{7,6},{8,9},{9,8},{10,11... | collective-permute-start | bytes 24584 | tf_op jit(solution)/shard_map/ppermute | solution.py:165
  34.9 5.1 %copy-start.2 = (bf16[32,96,128]{2,1,0:T(8,128)(2,1)}, bf16[32,96,128]{2,1,0:T(8,128)(2,1)S(1)}, u32[]{:S(2)}) copy-start(bf16[32,96,128]{2,1,0:T(8,128)(2,1)S(1)} %collective-permute-done) | copy-start | bytes 2359300
  40.0 19.7 %collective-permute-start.4 = (bf16[32,2,64,128]{3,2,1,0:T(8,128)(2,1)S(1)}, bf16[32,2,64,128]{3,2,1,0:T(8,128)(2,1)S(1)}, u32[]{:S(2)}, u32[]{:S(2)}) collective-permute-start(bf16[32,2,64,128]{3,2,1,0:T(8,128)(2,1)S(1)} %all-to-all-done.refs_0_), channel_id=1, source_target_pairs={{0,2},{2,0},{1,3},{3,1},{4,6},{6,4},{5,7},{7,5},{8,10},{10,8},{9,1... | collective-permute-start | bytes 3145736 | tf_op jit(solution)/shard_map/ppermute | solution.py:168
  41.3 27.4 %all-to-all-start.1 = ((bf16[32,96,128]{2,1,0:T(8,128)(2,1)}), bf16[32,96,128]{2,1,0:T(8,128)(2,1)S(1)}, u32[]{:S(2)}, u32[]{:S(2)}) async-start(bf16[32,96,128]{2,1,0:T(8,128)(2,1)} %copy-done.2), calls=%async_computation.1 | async-start | bytes 1572864 | tf_op jit(solution)/shard_map/all_to_all | solution.py:195
  49.9 7.5 %collective-permute-start.5 = (bf16[32,32,128]{2,1,0:T(8,128)(2,1)S(1)}, bf16[32,32,128]{2,1,0:T(8,128)(2,1)}, u32[]{:S(2)}, u32[]{:S(2)}) collective-permute-start(bf16[32,32,128]{2,1,0:T(8,128)(2,1)S(1)} %get-tuple-element.31), channel_id=1, source_target_pairs={{0,130},{130,0},{2,128},{128,2},{1,131},{131,1},{3,129},{129,3},{4... | collective-permute-start | bytes 786440 | tf_op jit(solution)/shard_map/ppermute | solution.py:171
  51.9 17.0 %collective-permute-start.6 = (bf16[32,2,64,128]{3,2,1,0:T(8,128)(2,1)S(1)}, bf16[32,2,64,128]{3,2,1,0:T(8,128)(2,1)}, u32[]{:S(2)}, u32[]{:S(2)}) collective-permute-start(bf16[32,2,64,128]{3,2,1,0:T(8,128)(2,1)S(1)} %all-to-all-done.refs_0_), channel_id=1, source_target_pairs={{0,1},{1,0},{2,3},{3,2},{4,5},{5,4},{6,7},{7,6},{8,9},{9,8},{10,11... | collective-permute-start | bytes 3145736 | tf_op jit(solution)/shard_map/ppermute | solution.py:165
  59.7 9.2 %collective-permute-start.7 = (bf16[32,2,64,128]{3,2,1,0:T(8,128)(2,1)S(1)}, bf16[32,2,64,128]{3,2,1,0:T(8,128)(2,1)}, u32[]{:S(2)}, u32[]{:S(2)}) collective-permute-start(bf16[32,2,64,128]{3,2,1,0:T(8,128)(2,1)S(1)} %collective-permute-done.4.refs_2_), channel_id=1, source_target_pairs={{0,1},{1,0},{2,3},{3,2},{4,5},{5,4},{6,7},{7,6},{8,9},{9,8},{10,11... | collective-permute-start | bytes 3145736 | tf_op jit(solution)/shard_map/ppermute | solution.py:165
  68.7 13.7 %collective-permute-start.9 = (bf16[32,96,128]{2,1,0:T(8,128)(2,1)S(1)}, bf16[32,96,128]{2,1,0:T(8,128)(2,1)}, u32[]{:S(2)}, u32[]{:S(2)}) collective-permute-start(bf16[32,96,128]{2,1,0:T(8,128)(2,1)S(1)} %all-to-all-done.1.refs_4_), channel_id=1, source_target_pairs={{0,2},{2,0},{1,3},{3,1},{4,6},{6,4},{5,7},{7,5},{8,10},{10,8},{9,1... | collective-permute-start | bytes 2359304 | tf_op jit(solution)/shard_map/ppermute | solution.py:168
  68.9 18.0 %all-to-all-start.2 = ((bf16[32,32,128]{2,1,0:T(8,128)(2,1)}), bf16[32,32,128]{2,1,0:T(8,128)(2,1)S(1)}, u32[]{:S(2)}, u32[]{:S(2)}) async-start(bf16[32,32,128]{2,1,0:T(8,128)(2,1)} %collective-permute-done.5), calls=%async_computation.2 | async-start | bytes 524288 | tf_op jit(solution)/shard_map/all_to_all | solution.py:198
  77.3 15.2 %collective-permute-start.8 = (bf16[32,96,128]{2,1,0:T(8,128)(2,1)S(1)}, bf16[32,96,128]{2,1,0:T(8,128)(2,1)}, u32[]{:S(2)}, u32[]{:S(2)}) collective-permute-start(bf16[32,96,128]{2,1,0:T(8,128)(2,1)S(1)} %all-to-all-done.1.refs_4_), channel_id=1, source_target_pairs={{0,1},{1,0},{2,3},{3,2},{4,5},{5,4},{6,7},{7,6},{8,9},{9,8},{10,11... | collective-permute-start | bytes 2359304 | tf_op jit(solution)/shard_map/ppermute | solution.py:165
  86.9 6.0 %collective-permute-start.10 = (bf16[32,96,128]{2,1,0:T(8,128)(2,1)}, bf16[32,96,128]{2,1,0:T(8,128)(2,1)}, u32[]{:S(2)}, u32[]{:S(2)}) collective-permute-start(bf16[32,96,128]{2,1,0:T(8,128)(2,1)} %collective-permute-done.9.refs_6_), channel_id=1, source_target_pairs={{0,1},{1,0},{2,3},{3,2},{4,5},{5,4},{6,7},{7,6},{8,9},{9,8},{10,11... | collective-permute-start | bytes 2359304 | tf_op jit(solution)/shard_map/ppermute | solution.py:165
  90.8 8.2 %collective-permute-start.12 = (bf16[32,32,128]{2,1,0:T(8,128)(2,1)S(1)}, bf16[32,32,128]{2,1,0:T(8,128)(2,1)S(1)}, u32[]{:S(2)}, u32[]{:S(2)}) collective-permute-start(bf16[32,32,128]{2,1,0:T(8,128)(2,1)S(1)} %all-to-all-done.2.refs_2_), channel_id=1, source_target_pairs={{0,2},{2,0},{1,3},{3,1},{4,6},{6,4},{5,7},{7,5},{8,10},{10,8},{9,1... | collective-permute-start | bytes 786440 | tf_op jit(solution)/shard_map/ppermute | solution.py:168
  92.1 7.4 %collective-permute-start.11 = (bf16[32,32,128]{2,1,0:T(8,128)(2,1)S(1)}, bf16[32,32,128]{2,1,0:T(8,128)(2,1)S(1)}, u32[]{:S(2)}, u32[]{:S(2)}) collective-permute-start(bf16[32,32,128]{2,1,0:T(8,128)(2,1)S(1)} %all-to-all-done.2.refs_2_), channel_id=1, source_target_pairs={{0,1},{1,0},{2,3},{3,2},{4,5},{5,4},{6,7},{7,6},{8,9},{9,8},{10,11... | collective-permute-start | bytes 786440 | tf_op jit(solution)/shard_map/ppermute | solution.py:165
  99.0 1.7 %collective-permute-start.13 = (bf16[32,32,128]{2,1,0:T(8,128)(2,1)S(1)}, bf16[32,32,128]{2,1,0:T(8,128)(2,1)S(1)}, u32[]{:S(2)}, u32[]{:S(2)}) collective-permute-start(bf16[32,32,128]{2,1,0:T(8,128)(2,1)S(1)} %collective-permute-done.12.refs_4_), channel_id=1, source_target_pairs={{0,1},{1,0},{2,3},{3,2},{4,5},{5,4},{6,7},{7,6},{8,9},{9,8},{10,11... | collective-permute-start | bytes 786440 | tf_op jit(solution)/shard_map/ppermute | solution.py:165

commit v5 on v4

--- a/solution.py
+++ b/solution.py
@@ -75,15 +75,24 @@
     chosen = norm_ref.shape[0] // rounds
     side = side_ref[0]
     if which == 0:
-        near, early, (out_ref, near_kept, early_kept, sems) = refs[:4], refs[4:8], refs[8:]
-        half, _, rows, width = near[0].shape
-        moves = [(near[t].at[:, 1], near_kept.at[t], sems.at[0, t]) for t in range(4)]
-        moves += [(early[t].at[:, pl.ds(rows, early_kept.shape[2])], early_kept.at[t], sems.at[1, t]) for t in range(4)]
+        near, early, (out_ref, near_kept, early_kept, held, sems) = refs[:4], refs[4:8], refs[8:]
+        half, some = early_kept.shape[1:3]
+        rows, width = held.shape[2:]
+        here, there = pl.ds(side * half, half), pl.ds((1 - side) * half, half)
+        now = [(near[t].at[:, 0], held.at[t, here], sems.at[0, t]) for t in range(4)]
+        now += [(early[t ^ 2].at[:, pl.ds(0, rows)], held.at[t, there], sems.at[1, t]) for t in range(4)]
+        later = [(near[t].at[:, 1], near_kept.at[t], sems.at[2, t]) for t in range(4)]
+        later += [(early[t].at[:, pl.ds(rows, some)], early_kept.at[t], sems.at[3, t]) for t in range(4)]
 
         @pl.when(pl.program_id(0) == 0)
-        def keep():
-            for move in moves:
+        def begin():
+            for move in now:
                 pltpu.make_async_copy(*move).start()
+            for move in now:
+                pltpu.make_async_copy(*move).wait()
+            for move in later:
+                pltpu.make_async_copy(*move).start()
+
     else:
         near_kept, early_kept, late, out_ref = refs[0], refs[1], refs[2:6], refs[-1]
         half, rows, width = near_kept.shape[1:]
@@ -94,7 +103,7 @@
         parts = []
         for t in range(4):
             if which == 0:
-                parts.append(jnp.where(mine, near[t][at, 0], early[t ^ 2][at, :rows]))
+                parts.append(held[t, b])
             else:
                 far = jnp.concatenate([early_kept[t ^ 2, at], late[t ^ 2][at]], axis=0)
                 parts.append(jnp.where(mine, near_kept[t, at], far))
@@ -121,7 +130,7 @@
 
         @pl.when(pl.program_id(0) == pl.num_programs(0) - 1)
         def kept():
-            for move in moves:
+            for move in later:
                 pltpu.make_async_copy(*move).wait()
 
 
@@ -131,18 +140,21 @@
     shapes = [(chosen, rounds, 2, width, 2 * width)]
     smem = pl.BlockSpec(memory_space=pltpu.SMEM)
     vmem = pl.BlockSpec(memory_space=pltpu.VMEM)
-    specs = [smem, smem, smem, pl.BlockSpec((1, rows, columns), lambda n: (n, 0, 0)), smem] + [vmem] * len(parts)
+    anywhere = pl.BlockSpec(memory_space=pl.ANY)
+    specs = [smem, smem, smem, pl.BlockSpec((1, rows, columns), lambda n: (n, 0, 0)), smem] + [vmem if which else anywhere] * len(parts)
+    scratch = []
     if which == 0:
         places, _, some = parts[0].shape[:3]
         shapes += [(4, places, some, width), (4, places, parts[4].shape[1] - some, width)]
+        scratch = [pltpu.VMEM((4, 2 * places, some, width), jnp.bfloat16), pltpu.SemaphoreType.DMA((4, 4))]
     more = () if into is None else (into,)
     return pl.pallas_call(
         functools.partial(stack_kernel, which),
         out_shape=[jax.ShapeDtypeStruct(shape, jnp.bfloat16) for shape in shapes],
         grid=(steps,),
-        in_specs=specs + [pl.BlockSpec(memory_space=pl.ANY)] * len(more),
+        in_specs=specs + [anywhere] * len(more),
         out_specs=[pl.BlockSpec((UNROLL, rounds, 1, width, 2 * width), lambda n: (n, 0, which, 0, 0))] + [vmem] * (len(shapes) - 1),
-        scratch_shapes=[] if which else [pltpu.SemaphoreType.DMA((2, 4))],
+        scratch_shapes=scratch,
         input_output_aliases={len(specs): 0} if more else {},
         compiler_params=pltpu.CompilerParams(vmem_limit_bytes=24 << 20),
         cost_estimate=pl.CostEstimate(flops=20 * chosen * rounds * 2 * width * rows * width, bytes_accessed=8 << 20, transcendentals=0),

time: 105 us -> 105 us (level)
  no operation moved by 1% of the time
where the time goes in v5:
time: 105 us
  starting transfers between devices  54.8 us (52%)
  waiting for transfers between devices  35.1 us (33%)
  Pallas kernels  11.7 us (11%)
  local copies, waits for them, and re-layouts  2.43 us (2%)
    ppermute x8, starting transfers between devices, across(): return lax.ppermute(x, 'core', swap_pairs)  18.4 us
    ppermute x2, waiting for transfers between devices, hand_on(): return lax.ppermute(x, ('yh', 'yl'), [(0, 3), (3, 0), (1, 2), (2, 1)])  13.3 us
    all_to_all x1, starting transfers between devices, per_device(): near = shuffle(near)  11.9 us
    pallas_call x2, Pallas kernels, stack(): pl.pallas_call(functools.partial(stack_kernel, which), out_shape=[jax.Sha...  9.81 us
    all_to_all x1, starting transfers between devices, per_device(): early = shuffle(early)  8.58 us
    all_to_all x1, starting transfers between devices, per_device(): late = shuffle(late)  8.34 us
    ppermute x4, waiting for transfers between devices, along(): return lax.ppermute(x, 'yl', swap_pairs)  6.75 us
    all_to_all x1, waiting for transfers between devices, per_device(): near = shuffle(near)  5.1 us
  transfers between devices with their start and end apart: 17, of which 11 were waited for; matrix products, arithmetic and copies ran while one was open for 1% of the time, Pallas kernels for 6%

profile of v5, /device:TPU:1, one launch (start us, length us, event | category | flops | bytes accessed | tf_op | source)
XLA Modules:
  0.0 104.7 jit_solution(12742522606561989536)
XLA Ops:
  0.0 1.6 %copy-done.1 = bf16[1,128,32,2,128]{4,3,2,1,0:T(2,128)(2,1)S(1)} copy-done((bf16[1,128,32,2,128]{4,3,2,1,0:T(2,128)(2,1)S(1)}, bf16[1,128,32,2,128]{4,3,2,1,0:T(2,128)(2,1)}, u32[]{:S(2)}) %copy-start.1) | copy-done | bytes 2097176
  1.6 1.9 %whiten.1 = (bf16[32,2,64,128]{3,2,1,0:T(8,128)(2,1)}, bf16[32,96,128]{2,1,0:T(8,128)(2,1)S(1)}, bf16[32,32,128]{2,1,0:T(8,128)(2,1)S(1)}) custom-call(s32[1]{0:T(128)} %bitcast.side_ref, bf16[128,64,128]{2,1,0:T(8,128)(2,1)S(1)} %bitcast.8), custom_call_target="tpu_custom_call" | custom-call | tf_op jit(solution)/shard_map/whiten/pallas_call | solution.py:52
  3.5 11.9 %all-to-all-start = ((bf16[32,2,64,128]{3,2,1,0:T(8,128)(2,1)}), bf16[32,2,64,128]{3,2,1,0:T(8,128)(2,1)S(1)}, u32[]{:S(2)}, u32[]{:S(2)}) async-start(bf16[32,2,64,128]{3,2,1,0:T(8,128)(2,1)} %get-tuple-element.26), calls=%async_computation | async-start | bytes 2097152 | tf_op jit(solution)/shard_map/all_to_all | solution.py:202
  15.4 2.8 %collective-permute-start = (bf16[32,96,128]{2,1,0:T(8,128)(2,1)S(1)}, bf16[32,96,128]{2,1,0:T(8,128)(2,1)S(1)}, u32[]{:S(2)}, u32[]{:S(2)}) collective-permute-start(bf16[32,96,128]{2,1,0:T(8,128)(2,1)S(1)} %get-tuple-element.27), channel_id=1, source_target_pairs={{0,130},{130,0},{2,128},{128,2},{1,131},{131,1},{3,129},{129,3},{4... | collective-permute-start | bytes 2359304 | tf_op jit(solution)/shard_map/ppermute | solution.py:183
  18.2 1.4 %collective-permute-start.1 = (s32[32,64]{1,0:T(8,128)S(1)}, s32[32,64]{1,0:T(8,128)S(1)}, u32[]{:S(2)}, u32[]{:S(2)}) collective-permute-start(s32[32,64]{1,0:T(8,128)S(1)} %copy-done.3), channel_id=1, source_target_pairs={{0,1},{1,0},{2,3},{3,2},{4,5},{5,4},{6,7},{7,6},{8,9},{9,8},{10,11... | collective-permute-start | bytes 24584 | tf_op jit(solution)/shard_map/ppermute | solution.py:177
  19.7 1.4 %collective-permute-done.2 = s32[32,64]{1,0:T(8,128)S(1)} collective-permute-done((s32[32,64]{1,0:T(8,128)S(1)}, s32[32,64]{1,0:T(8,128)S(1)}, u32[]{:S(2)}, u32[]{:S(2)}) %collective-permute-start.2) | collective-permute-done | bytes 8224 | tf_op jit(solution)/shard_map/ppermute | solution.py:180
  21.1 2.1 %collective-permute-start.3 = (s32[32,64]{1,0:T(8,128)S(1)}, s32[32,64]{1,0:T(8,128)S(1)}, u32[]{:S(2)}, u32[]{:S(2)}) collective-permute-start(s32[32,64]{1,0:T(8,128)S(1)} %collective-permute-done.2), channel_id=1, source_target_pairs={{0,1},{1,0},{2,3},{3,2},{4,5},{5,4},{6,7},{7,6},{8,9},{9,8},{10,11... | collective-permute-start | bytes 24584 | tf_op jit(solution)/shard_map/ppermute | solution.py:177
  25.0 9.9 %collective-permute-done = bf16[32,96,128]{2,1,0:T(8,128)(2,1)S(1)} collective-permute-done((bf16[32,96,128]{2,1,0:T(8,128)(2,1)S(1)}, bf16[32,96,128]{2,1,0:T(8,128)(2,1)S(1)}, u32[]{:S(2)}, u32[]{:S(2)}) %collective-permute-start) | collective-permute-done | bytes 786464 | tf_op jit(solution)/shard_map/ppermute | solution.py:183
  34.9 5.1 %all-to-all-done.refs_0_ = bf16[32,2,64,128]{3,2,1,0:T(8,128)(2,1)S(1)} async-done(((bf16[32,2,64,128]{3,2,1,0:T(8,128)(2,1)}), bf16[32,2,64,128]{3,2,1,0:T(8,128)(2,1)S(1)}, u32[]{:S(2)}, u32[]{:S(2)}) %all-to-all-start) | async-done | bytes 1048608 | tf_op jit(solution)/shard_map/all_to_all | solution.py:202
  40.0 1.3 %collective-permute-start.4 = (bf16[32,2,64,128]{3,2,1,0:T(8,128)(2,1)S(1)}, bf16[32,2,64,128]{3,2,1,0:T(8,128)(2,1)S(1)}, u32[]{:S(2)}, u32[]{:S(2)}) collective-permute-start(bf16[32,2,64,128]{3,2,1,0:T(8,128)(2,1)S(1)} %all-to-all-done.refs_0_), channel_id=1, source_target_pairs={{0,2},{2,0},{1,3},{3,1},{4,6},{6,4},{5,7},{7,5},{8,10},{10,8},{9,1... | collective-permute-start | bytes 3145736 | tf_op jit(solution)/shard_map/ppermute | solution.py:180
  41.3 8.6 %all-to-all-start.1 = ((bf16[32,96,128]{2,1,0:T(8,128)(2,1)}), bf16[32,96,128]{2,1,0:T(8,128)(2,1)S(1)}, u32[]{:S(2)}, u32[]{:S(2)}) async-start(bf16[32,96,128]{2,1,0:T(8,128)(2,1)} %copy-done.2), calls=%async_computation.1 | async-start | bytes 1572864 | tf_op jit(solution)/shard_map/all_to_all | solution.py:207
  49.9 2.0 %collective-permute-start.5 = (bf16[32,32,128]{2,1,0:T(8,128)(2,1)S(1)}, bf16[32,32,128]{2,1,0:T(8,128)(2,1)}, u32[]{:S(2)}, u32[]{:S(2)}) collective-permute-start(bf16[32,32,128]{2,1,0:T(8,128)(2,1)S(1)} %get-tuple-element.31), channel_id=1, source_target_pairs={{0,130},{130,0},{2,128},{128,2},{1,131},{131,1},{3,129},{129,3},{4... | collective-permute-start | bytes 786440 | tf_op jit(solution)/shard_map/ppermute | solution.py:183
  51.9 2.0 %collective-permute-start.6 = (bf16[32,2,64,128]{3,2,1,0:T(8,128)(2,1)S(1)}, bf16[32,2,64,128]{3,2,1,0:T(8,128)(2,1)}, u32[]{:S(2)}, u32[]{:S(2)}) collective-permute-start(bf16[32,2,64,128]{3,2,1,0:T(8,128)(2,1)S(1)} %all-to-all-done.refs_0_), channel_id=1, source_target_pairs={{0,1},{1,0},{2,3},{3,2},{4,5},{5,4},{6,7},{7,6},{8,9},{9,8},{10,11... | collective-permute-start | bytes 3145736 | tf_op jit(solution)/shard_map/ppermute | solution.py:177
  53.9 3.4 %collective-permute-done.5 = bf16[32,32,128]{2,1,0:T(8,128)(2,1)} collective-permute-done((bf16[32,32,128]{2,1,0:T(8,128)(2,1)S(1)}, bf16[32,32,128]{2,1,0:T(8,128)(2,1)}, u32[]{:S(2)}, u32[]{:S(2)}) %collective-permute-start.5) | collective-permute-done | bytes 262176 | tf_op jit(solution)/shard_map/ppermute | solution.py:183
  57.4 2.3 %collective-permute-done.4.refs_2_ = bf16[32,2,64,128]{3,2,1,0:T(8,128)(2,1)S(1)} collective-permute-done((bf16[32,2,64,128]{3,2,1,0:T(8,128)(2,1)S(1)}, bf16[32,2,64,128]{3,2,1,0:T(8,128)(2,1)S(1)}, u32[]{:S(2)}, u32[]{:S(2)}) %collective-permute-start.4) | collective-permute-done | bytes 1048608 | tf_op jit(solution)/shard_map/ppermute | solution.py:180
  59.7 5.9 %collective-permute-start.7 = (bf16[32,2,64,128]{3,2,1,0:T(8,128)(2,1)S(1)}, bf16[32,2,64,128]{3,2,1,0:T(8,128)(2,1)}, u32[]{:S(2)}, u32[]{:S(2)}) collective-permute-start(bf16[32,2,64,128]{3,2,1,0:T(8,128)(2,1)S(1)} %collective-permute-done.4.refs_2_), channel_id=1, source_target_pairs={{0,1},{1,0},{2,3},{3,2},{4,5},{5,4},{6,7},{7,6},{8,9},{9,8},{10,11... | collective-permute-start | bytes 3145736 | tf_op jit(solution)/shard_map/ppermute | solution.py:177
  65.6 3.1 %all-to-all-done.1.refs_4_ = bf16[32,96,128]{2,1,0:T(8,128)(2,1)S(1)} async-done(((bf16[32,96,128]{2,1,0:T(8,128)(2,1)}), bf16[32,96,128]{2,1,0:T(8,128)(2,1)S(1)}, u32[]{:S(2)}, u32[]{:S(2)}) %all-to-all-start.1) | async-done | bytes 786464 | tf_op jit(solution)/shard_map/all_to_all | solution.py:207
  68.9 8.3 %all-to-all-start.2 = ((bf16[32,32,128]{2,1,0:T(8,128)(2,1)}), bf16[32,32,128]{2,1,0:T(8,128)(2,1)S(1)}, u32[]{:S(2)}, u32[]{:S(2)}) async-start(bf16[32,32,128]{2,1,0:T(8,128)(2,1)} %collective-permute-done.5), calls=%async_computation.2 | async-start | bytes 524288 | tf_op jit(solution)/shard_map/all_to_all | solution.py:210
  77.3 2.2 %collective-permute-start.8 = (bf16[32,96,128]{2,1,0:T(8,128)(2,1)S(1)}, bf16[32,96,128]{2,1,0:T(8,128)(2,1)}, u32[]{:S(2)}, u32[]{:S(2)}) collective-permute-start(bf16[32,96,128]{2,1,0:T(8,128)(2,1)S(1)} %all-to-all-done.1.refs_4_), channel_id=1, source_target_pairs={{0,1},{1,0},{2,3},{3,2},{4,5},{5,4},{6,7},{7,6},{8,9},{9,8},{10,11... | collective-permute-start | bytes 2359304 | tf_op jit(solution)/shard_map/ppermute | solution.py:177
  79.5 3.0 %collective-permute-done.9.refs_6_ = bf16[32,96,128]{2,1,0:T(8,128)(2,1)} collective-permute-done((bf16[32,96,128]{2,1,0:T(8,128)(2,1)S(1)}, bf16[32,96,128]{2,1,0:T(8,128)(2,1)}, u32[]{:S(2)}, u32[]{:S(2)}) %collective-permute-start.9) | collective-permute-done | bytes 786464 | tf_op jit(solution)/shard_map/ppermute | solution.py:180
  82.5 4.5 %all-to-all-done.2.refs_2_ = bf16[32,32,128]{2,1,0:T(8,128)(2,1)S(1)} async-done(((bf16[32,32,128]{2,1,0:T(8,128)(2,1)}), bf16[32,32,128]{2,1,0:T(8,128)(2,1)S(1)}, u32[]{:S(2)}, u32[]{:S(2)}) %all-to-all-start.2) | async-done | bytes 262176 | tf_op jit(solution)/shard_map/all_to_all | solution.py:210
  86.9 3.8 %collective-permute-start.10 = (bf16[32,96,128]{2,1,0:T(8,128)(2,1)}, bf16[32,96,128]{2,1,0:T(8,128)(2,1)}, u32[]{:S(2)}, u32[]{:S(2)}) collective-permute-start(bf16[32,96,128]{2,1,0:T(8,128)(2,1)} %collective-permute-done.9.refs_6_), channel_id=1, source_target_pairs={{0,1},{1,0},{2,3},{3,2},{4,5},{5,4},{6,7},{7,6},{8,9},{9,8},{10,11... | collective-permute-start | bytes 2359304 | tf_op jit(solution)/shard_map/ppermute | solution.py:177
  92.9 5.8 %stack0.1 = (bf16[16,2,2,128,256]{4,3,2,1,0:T(8,128)(2,1)}, bf16[4,32,64,128]{3,2,1,0:T(8,128)(2,1)S(1)}, bf16[4,32,32,128]{3,2,1,0:T(8,128)(2,1)S(1)}) custom-call(s32[1]{0:T(128)} %bitcast.side_ref, s32[1]{0:T(128)} %bitcast.1.first_ref, s32[32]{0:T(128)S(1)} %reshape.55.mates_ref, f32[2,256,16]{2,1,0:T(8,128)S(1)} %bitcast.9, f32[32]{0:T(128)S(1)} %sqrt.3.norm_ref, ...), custom_call_target="tpu_custom_call" | custom-call | flops 5368709120 | bytes 8388608 | tf_op jit(solution)/shard_map/stack0/pallas_call | solution.py:151
  100.7 4.0 %stack1.1 = bf16[16,2,2,128,256]{4,3,2,1,0:T(8,128)(2,1)} custom-call(s32[1]{0:T(128)} %bitcast.side_ref, s32[1]{0:T(128)} %bitcast.1.first_ref, s32[32]{0:T(128)S(1)} %reshape.55.mates_ref, f32[2,256,16]{2,1,0:T(8,128)S(1)} %bitcast.10, f32[32]{0:T(128)S(1)} %sqrt.3.norm_ref, ...), custom_call_target="tpu_custom_call", output_to_operand_aliasing={{}: (11, {})} | custom-call | flops 5368709120 | bytes 8388608 | tf_op jit(solution)/shard_map/stack1/pallas_call | solution.py:151
  (34 shorter events, 6.3 us)
Async XLA Ops:
  0.0 19.6 %copy-start = (s32[2,64]{1,0:T(2,128)S(1)}, s32[2,64]{1,0:T(2,128)}, u32[]{:S(2)}) copy-start(s32[2,64]{1,0:T(2,128)} %param.5) | copy-start | bytes 1540
  0.0 1.6 %copy-start.1 = (bf16[1,128,32,2,128]{4,3,2,1,0:T(2,128)(2,1)S(1)}, bf16[1,128,32,2,128]{4,3,2,1,0:T(2,128)(2,1)}, u32[]{:S(2)}) copy-start(bf16[1,128,32,2,128]{4,3,2,1,0:T(2,128)(2,1)} %param.3) | copy-start | bytes 6291460
  1.6 16.6 %copy-start.3 = (s32[32,64]{1,0:T(8,128)S(1)}, s32[32,64]{1,0:T(8,128)}, u32[]{:S(2)}) copy-start(s32[32,64]{1,0:T(8,128)} %param.4) | copy-start | bytes 24580
  3.5 36.5 %all-to-all-start = ((bf16[32,2,64,128]{3,2,1,0:T(8,128)(2,1)}), bf16[32,2,64,128]{3,2,1,0:T(8,128)(2,1)S(1)}, u32[]{:S(2)}, u32[]{:S(2)}) async-start(bf16[32,2,64,128]{3,2,1,0:T(8,128)(2,1)} %get-tuple-element.26), calls=%async_computation | async-start | bytes 2097152 | tf_op jit(solution)/shard_map/all_to_all | solution.py:202
  15.4 19.5 %collective-permute-start = (bf16[32,96,128]{2,1,0:T(8,128)(2,1)S(1)}, bf16[32,96,128]{2,1,0:T(8,128)(2,1)S(1)}, u32[]{:S(2)}, u32[]{:S(2)}) collective-permute-start(bf16[32,96,128]{2,1,0:T(8,128)(2,1)S(1)} %get-tuple-element.27), channel_id=1, source_target_pairs={{0,130},{130,0},{2,128},{128,2},{1,131},{131,1},{3,129},{129,3},{4... | collective-permute-start | bytes 2359304 | tf_op jit(solution)/shard_map/ppermute | solution.py:183
  18.2 2.9 %collective-permute-start.2 = (s32[32,64]{1,0:T(8,128)S(1)}, s32[32,64]{1,0:T(8,128)S(1)}, u32[]{:S(2)}, u32[]{:S(2)}) collective-permute-start(s32[32,64]{1,0:T(8,128)S(1)} %copy-done.3), channel_id=1, source_target_pairs={{0,2},{2,0},{1,3},{3,1},{4,6},{6,4},{5,7},{7,5},{8,10},{10,8},{9,1... | collective-permute-start | bytes 24584 | tf_op jit(solution)/shard_map/ppermute | solution.py:180
  18.2 5.2 %collective-permute-start.1 = (s32[32,64]{1,0:T(8,128)S(1)}, s32[32,64]{1,0:T(8,128)S(1)}, u32[]{:S(2)}, u32[]{:S(2)}) collective-permute-start(s32[32,64]{1,0:T(8,128)S(1)} %copy-done.3), channel_id=1, source_target_pairs={{0,1},{1,0},{2,3},{3,2},{4,5},{5,4},{6,7},{7,6},{8,9},{9,8},{10,11... | collective-permute-start | bytes 24584 | tf_op jit(solution)/shard_map/ppermute | solution.py:177
  21.1 2.9 %collective-permute-start.3 = (s32[32,64]{1,0:T(8,128)S(1)}, s32[32,64]{1,0:T(8,128)S(1)}, u32[]{:S(2)}, u32[]{:S(2)}) collective-permute-start(s32[32,64]{1,0:T(8,128)S(1)} %collective-permute-done.2), channel_id=1, source_target_pairs={{0,1},{1,0},{2,3},{3,2},{4,5},{5,4},{6,7},{7,6},{8,9},{9,8},{10,11... | collective-permute-start | bytes 24584 | tf_op jit(solution)/shard_map/ppermute | solution.py:177
  34.9 5.1 %copy-start.2 = (bf16[32,96,128]{2,1,0:T(8,128)(2,1)}, bf16[32,96,128]{2,1,0:T(8,128)(2,1)S(1)}, u32[]{:S(2)}) copy-start(bf16[32,96,128]{2,1,0:T(8,128)(2,1)S(1)} %collective-permute-done) | copy-start | bytes 2359300
  40.0 19.7 %collective-permute-start.4 = (bf16[32,2,64,128]{3,2,1,0:T(8,128)(2,1)S(1)}, bf16[32,2,64,128]{3,2,1,0:T(8,128)(2,1)S(1)}, u32[]{:S(2)}, u32[]{:S(2)}) collective-permute-start(bf16[32,2,64,128]{3,2,1,0:T(8,128)(2,1)S(1)} %all-to-all-done.refs_0_), channel_id=1, source_target_pairs={{0,2},{2,0},{1,3},{3,1},{4,6},{6,4},{5,7},{7,5},{8,10},{10,8},{9,1... | collective-permute-start | bytes 3145736 | tf_op jit(solution)/shard_map/ppermute | solution.py:180
  41.3 27.4 %all-to-all-start.1 = ((bf16[32,96,128]{2,1,0:T(8,128)(2,1)}), bf16[32,96,128]{2,1,0:T(8,128)(2,1)S(1)}, u32[]{:S(2)}, u32[]{:S(2)}) async-start(bf16[32,96,128]{2,1,0:T(8,128)(2,1)} %copy-done.2), calls=%async_computation.1 | async-start | bytes 1572864 | tf_op jit(solution)/shard_map/all_to_all | solution.py:207
  49.9 7.5 %collective-permute-start.5 = (bf16[32,32,128]{2,1,0:T(8,128)(2,1)S(1)}, bf16[32,32,128]{2,1,0:T(8,128)(2,1)}, u32[]{:S(2)}, u32[]{:S(2)}) collective-permute-start(bf16[32,32,128]{2,1,0:T(8,128)(2,1)S(1)} %get-tuple-element.31), channel_id=1, source_target_pairs={{0,130},{130,0},{2,128},{128,2},{1,131},{131,1},{3,129},{129,3},{4... | collective-permute-start | bytes 786440 | tf_op jit(solution)/shard_map/ppermute | solution.py:183
  51.9 17.0 %collective-permute-start.6 = (bf16[32,2,64,128]{3,2,1,0:T(8,128)(2,1)S(1)}, bf16[32,2,64,128]{3,2,1,0:T(8,128)(2,1)}, u32[]{:S(2)}, u32[]{:S(2)}) collective-permute-start(bf16[32,2,64,128]{3,2,1,0:T(8,128)(2,1)S(1)} %all-to-all-done.refs_0_), channel_id=1, source_target_pairs={{0,1},{1,0},{2,3},{3,2},{4,5},{5,4},{6,7},{7,6},{8,9},{9,8},{10,11... | collective-permute-start | bytes 3145736 | tf_op jit(solution)/shard_map/ppermute | solution.py:177
  59.7 9.2 %collective-permute-start.7 = (bf16[32,2,64,128]{3,2,1,0:T(8,128)(2,1)S(1)}, bf16[32,2,64,128]{3,2,1,0:T(8,128)(2,1)}, u32[]{:S(2)}, u32[]{:S(2)}) collective-permute-start(bf16[32,2,64,128]{3,2,1,0:T(8,128)(2,1)S(1)} %collective-permute-done.4.refs_2_), channel_id=1, source_target_pairs={{0,1},{1,0},{2,3},{3,2},{4,5},{5,4},{6,7},{7,6},{8,9},{9,8},{10,11... | collective-permute-start | bytes 3145736 | tf_op jit(solution)/shard_map/ppermute | solution.py:177
  68.7 13.7 %collective-permute-start.9 = (bf16[32,96,128]{2,1,0:T(8,128)(2,1)S(1)}, bf16[32,96,128]{2,1,0:T(8,128)(2,1)}, u32[]{:S(2)}, u32[]{:S(2)}) collective-permute-start(bf16[32,96,128]{2,1,0:T(8,128)(2,1)S(1)} %all-to-all-done.1.refs_4_), channel_id=1, source_target_pairs={{0,2},{2,0},{1,3},{3,1},{4,6},{6,4},{5,7},{7,5},{8,10},{10,8},{9,1... | collective-permute-start | bytes 2359304 | tf_op jit(solution)/shard_map/ppermute | solution.py:180
  68.9 18.0 %all-to-all-start.2 = ((bf16[32,32,128]{2,1,0:T(8,128)(2,1)}), bf16[32,32,128]{2,1,0:T(8,128)(2,1)S(1)}, u32[]{:S(2)}, u32[]{:S(2)}) async-start(bf16[32,32,128]{2,1,0:T(8,128)(2,1)} %collective-permute-done.5), calls=%async_computation.2 | async-start | bytes 524288 | tf_op jit(solution)/shard_map/all_to_all | solution.py:210
  77.3 15.2 %collective-permute-start.8 = (bf16[32,96,128]{2,1,0:T(8,128)(2,1)S(1)}, bf16[32,96,128]{2,1,0:T(8,128)(2,1)}, u32[]{:S(2)}, u32[]{:S(2)}) collective-permute-start(bf16[32,96,128]{2,1,0:T(8,128)(2,1)S(1)} %all-to-all-done.1.refs_4_), channel_id=1, source_target_pairs={{0,1},{1,0},{2,3},{3,2},{4,5},{5,4},{6,7},{7,6},{8,9},{9,8},{10,11... | collective-permute-start | bytes 2359304 | tf_op jit(solution)/shard_map/ppermute | solution.py:177
  86.9 6.0 %collective-permute-start.10 = (bf16[32,96,128]{2,1,0:T(8,128)(2,1)}, bf16[32,96,128]{2,1,0:T(8,128)(2,1)}, u32[]{:S(2)}, u32[]{:S(2)}) collective-permute-start(bf16[32,96,128]{2,1,0:T(8,128)(2,1)} %collective-permute-done.9.refs_6_), channel_id=1, source_target_pairs={{0,1},{1,0},{2,3},{3,2},{4,5},{5,4},{6,7},{7,6},{8,9},{9,8},{10,11... | collective-permute-start | bytes 2359304 | tf_op jit(solution)/shard_map/ppermute | solution.py:177
  90.8 7.9 %collective-permute-start.12 = (bf16[32,32,128]{2,1,0:T(8,128)(2,1)S(1)}, bf16[32,32,128]{2,1,0:T(8,128)(2,1)S(1)}, u32[]{:S(2)}, u32[]{:S(2)}) collective-permute-start(bf16[32,32,128]{2,1,0:T(8,128)(2,1)S(1)} %all-to-all-done.2.refs_2_), channel_id=1, source_target_pairs={{0,2},{2,0},{1,3},{3,1},{4,6},{6,4},{5,7},{7,5},{8,10},{10,8},{9,1... | collective-permute-start | bytes 786440 | tf_op jit(solution)/shard_map/ppermute | solution.py:180
  92.1 7.4 %collective-permute-start.11 = (bf16[32,32,128]{2,1,0:T(8,128)(2,1)S(1)}, bf16[32,32,128]{2,1,0:T(8,128)(2,1)S(1)}, u32[]{:S(2)}, u32[]{:S(2)}) collective-permute-start(bf16[32,32,128]{2,1,0:T(8,128)(2,1)S(1)} %all-to-all-done.2.refs_2_), channel_id=1, source_target_pairs={{0,1},{1,0},{2,3},{3,2},{4,5},{5,4},{6,7},{7,6},{8,9},{9,8},{10,11... | collective-permute-start | bytes 786440 | tf_op jit(solution)/shard_map/ppermute | solution.py:177
  98.8 1.9 %collective-permute-start.13 = (bf16[32,32,128]{2,1,0:T(8,128)(2,1)S(1)}, bf16[32,32,128]{2,1,0:T(8,128)(2,1)S(1)}, u32[]{:S(2)}, u32[]{:S(2)}) collective-permute-start(bf16[32,32,128]{2,1,0:T(8,128)(2,1)S(1)} %collective-permute-done.12.refs_4_), channel_id=1, source_target_pairs={{0,1},{1,0},{2,3},{3,2},{4,5},{5,4},{6,7},{7,6},{8,9},{9,8},{10,11... | collective-permute-start | bytes 786440 | tf_op jit(solution)/shard_map/ppermute | solution.py:177

commit v6 on v5

--- a/solution.py
+++ b/solution.py
@@ -12,32 +12,63 @@
 UNROLL = 8
 
 
-def whiten_kernel(side_ref, x_ref, near_ref, early_ref, late_ref):
-    bins, rows, width = x_ref.shape
+def near_kernel(side_ref, x_ref, near_ref, scale_ref, held, near, in_sems, out_sems):
+    bins, rows, width = held.shape
     half = bins // 2
-    more = early_ref.shape[1] - rows
     step = 4
+    slabs, parts = in_sems.shape[0], out_sems.shape[0]
+    slab, part = bins // slabs, half // 2 // parts
+    loads = [pltpu.make_async_copy(x_ref.at[pl.ds(i * slab, slab)], held.at[pl.ds(i * slab, slab)], in_sems.at[i]) for i in range(slabs)]
+    for load in loads:
+        load.start()
 
     def add(i, total):
         for j in range(step):
-            values = x_ref[i * step + j].astype(jnp.float32)
+            values = held[i * step + j].astype(jnp.float32)
             total = total + values * values
         return total
 
-    total = lax.fori_loop(0, bins // step, add, jnp.zeros((rows, width), jnp.float32))
+    total = jnp.zeros((rows, width), jnp.float32)
+    for i, load in enumerate(loads):
+        load.wait()
+        total = lax.fori_loop(i * slab // step, (i + 1) * slab // step, add, total)
     first = lax.broadcasted_iota(jnp.int32, (rows, width), 0) % 2 == 0
     other = jnp.where(first, pltpu.roll(total, rows - 1, 0), pltpu.roll(total, 1, 0))
     scale = lax.rsqrt((total + other) / bins + EPS)
-    near = side_ref[0] * half
-    far = half - near
+    scale_ref[...] = scale
+    here = side_ref[0] * half
+
+    def put(i, carry):
+        for j in range(step):
+            for which in range(2):
+                at = i * step + j
+                near[at, which] = (held[here + 2 * at + which].astype(jnp.float32) * scale).astype(near.dtype)
+        return carry
+
+    stores = []
+    for i in range(parts):
+        lax.fori_loop(i * part // step, (i + 1) * part // step, put, 0)
+        places = pl.ds(i * part, part)
+        stores.append(pltpu.make_async_copy(near.at[places], near_ref.at[places], out_sems.at[i]))
+        stores[-1].start()
+    for store in stores:
+        store.wait()
+
+
+def far_kernel(side_ref, x_ref, scale_ref, early_ref, late_ref, held, sem):
+    half, rows, width = held.shape
+    more = early_ref.shape[1] - rows
+    step = 4
+    load = pltpu.make_async_copy(x_ref.at[pl.ds((1 - side_ref[0]) * half, half)], held, sem)
+    load.start()
+    load.wait()
+    scale = scale_ref[...]
 
     def put(i, carry):
         for j in range(step):
             at = i * step + j
-            for which in range(2):
-                near_ref[at, which] = (x_ref[near + 2 * at + which].astype(jnp.float32) * scale).astype(near_ref.dtype)
-            early_ref[at, :rows] = (x_ref[far + 2 * at].astype(jnp.float32) * scale).astype(early_ref.dtype)
-            odd = (x_ref[far + 2 * at + 1].astype(jnp.float32) * scale).astype(early_ref.dtype)
+            early_ref[at, :rows] = (held[2 * at].astype(jnp.float32) * scale).astype(early_ref.dtype)
+            odd = (held[2 * at + 1].astype(jnp.float32) * scale).astype(early_ref.dtype)
             early_ref[at, rows:] = odd[:more]
             late_ref[at] = odd[more:]
         return carry
@@ -48,18 +79,35 @@
 def whiten(side, spectra):
     bins, rows, width = spectra.shape
     places = bins // 4
+    smem = pl.BlockSpec(memory_space=pltpu.SMEM)
     vmem = pl.BlockSpec(memory_space=pltpu.VMEM)
-    return pl.pallas_call(
-        whiten_kernel,
-        out_shape=[
-            jax.ShapeDtypeStruct(shape, spectra.dtype)
-            for shape in ((places, 2, rows, width), (places, rows + rows // 2, width), (places, rows // 2, width))
+    params = pltpu.CompilerParams(vmem_limit_bytes=16 << 20)
+    near, scale = pl.pallas_call(
+        near_kernel,
+        out_shape=[jax.ShapeDtypeStruct((places, 2, rows, width), spectra.dtype), jax.ShapeDtypeStruct((rows, width), jnp.float32)],
+        in_specs=[smem, pl.BlockSpec(memory_space=pl.ANY)],
+        out_specs=[pl.BlockSpec(memory_space=pl.ANY), vmem],
+        scratch_shapes=[
+            pltpu.VMEM(spectra.shape, spectra.dtype),
+            pltpu.VMEM((places, 2, rows, width), spectra.dtype),
+            pltpu.SemaphoreType.DMA((8,)),
+            pltpu.SemaphoreType.DMA((4,)),
         ],
-        in_specs=[pl.BlockSpec(memory_space=pltpu.SMEM), vmem],
-        out_specs=[vmem] * 3,
-        compiler_params=pltpu.CompilerParams(vmem_limit_bytes=16 << 20),
-        name="whiten",
+        compiler_params=pltpu.CompilerParams(vmem_limit_bytes=61 << 20),
+        name="whiten_near",
     )(side, spectra)
+    shapes = ((places, rows + rows // 2, width), (places, rows // 2, width))
+    early, late = pl.pallas_call(
+        far_kernel,
+        out_shape=[jax.ShapeDtypeStruct(shape, spectra.dtype) for shape in shapes],
+        in_specs=[smem, pl.BlockSpec(memory_space=pl.ANY), vmem],
+        out_specs=[vmem] * 2,
+        scratch_shapes=[pltpu.VMEM((bins // 2, rows, width), spectra.dtype), pltpu.SemaphoreType.DMA],
+        compiler_params=params,
+        cost_estimate=pl.CostEstimate(flops=0, bytes_accessed=4 << 20, transcendentals=0),
+        name="whiten_far",
+    )(side, spectra, scale)
+    return near, early, late
 
 
 def turn_matrix(rows):

time: 105 us -> 105 us (level)
  Pallas kernels: 11.7 us -> 13.5 us
  waiting for transfers between devices: 35.1 us -> 33.6 us
    pallas_call x1 -> x2, Pallas kernels: 1.9 us -> 3.74 us  [the longest x1 3.46 us: whiten(): pl.pallas_call(near_kernel, out_shape=[jax.ShapeDtypeStruct((places, 2, r...]
    all_to_all x1, waiting for transfers between devices: 5.1 us -> 3.31 us  [per_device(): near = shuffle(near)]
  transfers between devices with their start and end apart: 17 -> 17, of which waited for: 11 -> 12; matrix products, arithmetic and copies ran while one was open for 1% -> 1% of each run, Pallas kernels for 6% -> 6%
where the time goes in v6:
time: 105 us
  starting transfers between devices  54.7 us (52%)
  waiting for transfers between devices  33.6 us (32%)
  Pallas kernels  13.5 us (13%)
  local copies, waits for them, and re-layouts  2.27 us (2%)
    ppermute x8, starting transfers between devices, across(): return lax.ppermute(x, 'core', swap_pairs)  18.3 us
    ppermute x2, waiting for transfers between devices, hand_on(): return lax.ppermute(x, ('yh', 'yl'), [(0, 3), (3, 0), (1, 2), (2, 1)])  13.6 us
    all_to_all x1, starting transfers between devices, per_device(): near = shuffle(near)  12 us
    pallas_call x2, Pallas kernels, stack(): pl.pallas_call(functools.partial(stack_kernel, which), out_shape=[jax.Sha...  9.72 us
    all_to_all x1, starting transfers between devices, per_device(): early = shuffle(early)  8.58 us
    all_to_all x1, starting transfers between devices, per_device(): late = shuffle(late)  8.34 us
    ppermute x4, waiting for transfers between devices, along(): return lax.ppermute(x, 'yl', swap_pairs)  7.04 us
    ppermute x2, starting transfers between devices, hand_on(): return lax.ppermute(x, ('yh', 'yl'), [(0, 3), (3, 0), (1, 2), (2, 1)])  4.72 us
  transfers between devices with their start and end apart: 17, of which 12 were waited for; matrix products, arithmetic and copies ran while one was open for 1% of the time, Pallas kernels for 6%

profile of v6, /device:TPU:1, one launch (start us, length us, event | category | flops | bytes accessed | tf_op | source)
XLA Modules:
  0.0 104.8 jit_solution(7591704832513395545)
XLA Ops:
  0.0 3.5 %whiten_near.1 = (bf16[32,2,64,128]{3,2,1,0:T(8,128)(2,1)}, f32[64,128]{1,0:T(8,128)}) custom-call(s32[1]{0:T(128)} %bitcast.side_ref, bf16[128,64,128]{2,1,0:T(8,128)(2,1)} %bitcast.8), custom_call_target="tpu_custom_call" | custom-call | tf_op jit(solution)/shard_map/whiten_near/pallas_call | solution.py:85
  3.5 12.0 %all-to-all-start = ((bf16[32,2,64,128]{3,2,1,0:T(8,128)(2,1)}), bf16[32,2,64,128]{3,2,1,0:T(8,128)(2,1)}, u32[]{:S(2)}, u32[]{:S(2)}) async-start(bf16[32,2,64,128]{3,2,1,0:T(8,128)(2,1)} %get-tuple-element.27), calls=%async_computation | async-start | bytes 2097152 | tf_op jit(solution)/shard_map/all_to_all | solution.py:250
  17.3 2.7 %collective-permute-start = (bf16[32,96,128]{2,1,0:T(8,128)(2,1)S(1)}, bf16[32,96,128]{2,1,0:T(8,128)(2,1)}, u32[]{:S(2)}, u32[]{:S(2)}) collective-permute-start(bf16[32,96,128]{2,1,0:T(8,128)(2,1)S(1)} %get-tuple-element.29), channel_id=1, source_target_pairs={{0,130},{130,0},{2,128},{128,2},{1,131},{131,1},{3,129},{129,3},{4... | collective-permute-start | bytes 2359304 | tf_op jit(solution)/shard_map/ppermute | solution.py:231
  20.0 1.4 %collective-permute-start.1 = (s32[32,64]{1,0:T(8,128)S(1)}, s32[32,64]{1,0:T(8,128)S(1)}, u32[]{:S(2)}, u32[]{:S(2)}) collective-permute-start(s32[32,64]{1,0:T(8,128)S(1)} %copy-done.4), channel_id=1, source_target_pairs={{0,1},{1,0},{2,3},{3,2},{4,5},{5,4},{6,7},{7,6},{8,9},{9,8},{10,11... | collective-permute-start | bytes 24584 | tf_op jit(solution)/shard_map/ppermute | solution.py:225
  21.4 1.5 %collective-permute-done.2 = s32[32,64]{1,0:T(8,128)S(1)} collective-permute-done((s32[32,64]{1,0:T(8,128)S(1)}, s32[32,64]{1,0:T(8,128)S(1)}, u32[]{:S(2)}, u32[]{:S(2)}) %collective-permute-start.2) | collective-permute-done | bytes 8224 | tf_op jit(solution)/shard_map/ppermute | solution.py:228
  23.0 2.0 %collective-permute-start.3 = (s32[32,64]{1,0:T(8,128)S(1)}, s32[32,64]{1,0:T(8,128)S(1)}, u32[]{:S(2)}, u32[]{:S(2)}) collective-permute-start(s32[32,64]{1,0:T(8,128)S(1)} %collective-permute-done.2), channel_id=1, source_target_pairs={{0,1},{1,0},{2,3},{3,2},{4,5},{5,4},{6,7},{7,6},{8,9},{9,8},{10,11... | collective-permute-start | bytes 24584 | tf_op jit(solution)/shard_map/ppermute | solution.py:225
  26.8 10.0 %collective-permute-done = bf16[32,96,128]{2,1,0:T(8,128)(2,1)} collective-permute-done((bf16[32,96,128]{2,1,0:T(8,128)(2,1)S(1)}, bf16[32,96,128]{2,1,0:T(8,128)(2,1)}, u32[]{:S(2)}, u32[]{:S(2)}) %collective-permute-start) | collective-permute-done | bytes 786464 | tf_op jit(solution)/shard_map/ppermute | solution.py:231
  36.8 3.3 %all-to-all-done.refs_0_ = bf16[32,2,64,128]{3,2,1,0:T(8,128)(2,1)} async-done(((bf16[32,2,64,128]{3,2,1,0:T(8,128)(2,1)}), bf16[32,2,64,128]{3,2,1,0:T(8,128)(2,1)}, u32[]{:S(2)}, u32[]{:S(2)}) %all-to-all-start) | async-done | bytes 1048608 | tf_op jit(solution)/shard_map/all_to_all | solution.py:250
  40.1 1.3 %collective-permute-start.4 = (bf16[32,2,64,128]{3,2,1,0:T(8,128)(2,1)}, bf16[32,2,64,128]{3,2,1,0:T(8,128)(2,1)S(1)}, u32[]{:S(2)}, u32[]{:S(2)}) collective-permute-start(bf16[32,2,64,128]{3,2,1,0:T(8,128)(2,1)} %all-to-all-done.refs_0_), channel_id=1, source_target_pairs={{0,2},{2,0},{1,3},{3,1},{4,6},{6,4},{5,7},{7,5},{8,10},{10,8},{9,1... | collective-permute-start | bytes 3145736 | tf_op jit(solution)/shard_map/ppermute | solution.py:228
  41.4 8.6 %all-to-all-start.1 = ((bf16[32,96,128]{2,1,0:T(8,128)(2,1)}), bf16[32,96,128]{2,1,0:T(8,128)(2,1)S(1)}, u32[]{:S(2)}, u32[]{:S(2)}) async-start(bf16[32,96,128]{2,1,0:T(8,128)(2,1)} %collective-permute-done), calls=%async_computation.1 | async-start | bytes 1572864 | tf_op jit(solution)/shard_map/all_to_all | solution.py:255
  50.0 2.0 %collective-permute-start.5 = (bf16[32,32,128]{2,1,0:T(8,128)(2,1)}, bf16[32,32,128]{2,1,0:T(8,128)(2,1)}, u32[]{:S(2)}, u32[]{:S(2)}) collective-permute-start(bf16[32,32,128]{2,1,0:T(8,128)(2,1)} %copy-done.3), channel_id=1, source_target_pairs={{0,130},{130,0},{2,128},{128,2},{1,131},{131,1},{3,129},{129,3},{4... | collective-permute-start | bytes 786440 | tf_op jit(solution)/shard_map/ppermute | solution.py:231
  52.0 2.0 %collective-permute-start.6 = (bf16[32,2,64,128]{3,2,1,0:T(8,128)(2,1)}, bf16[32,2,64,128]{3,2,1,0:T(8,128)(2,1)}, u32[]{:S(2)}, u32[]{:S(2)}) collective-permute-start(bf16[32,2,64,128]{3,2,1,0:T(8,128)(2,1)} %all-to-all-done.refs_0_), channel_id=1, source_target_pairs={{0,1},{1,0},{2,3},{3,2},{4,5},{5,4},{6,7},{7,6},{8,9},{9,8},{10,11... | collective-permute-start | bytes 3145736 | tf_op jit(solution)/shard_map/ppermute | solution.py:225
  54.0 3.7 %collective-permute-done.5 = bf16[32,32,128]{2,1,0:T(8,128)(2,1)} collective-permute-done((bf16[32,32,128]{2,1,0:T(8,128)(2,1)}, bf16[32,32,128]{2,1,0:T(8,128)(2,1)}, u32[]{:S(2)}, u32[]{:S(2)}) %collective-permute-start.5) | collective-permute-done | bytes 262176 | tf_op jit(solution)/shard_map/ppermute | solution.py:231
  57.7 2.3 %collective-permute-done.4.refs_2_ = bf16[32,2,64,128]{3,2,1,0:T(8,128)(2,1)S(1)} collective-permute-done((bf16[32,2,64,128]{3,2,1,0:T(8,128)(2,1)}, bf16[32,2,64,128]{3,2,1,0:T(8,128)(2,1)S(1)}, u32[]{:S(2)}, u32[]{:S(2)}) %collective-permute-start.4) | collective-permute-done | bytes 1048608 | tf_op jit(solution)/shard_map/ppermute | solution.py:228
  60.0 5.9 %collective-permute-start.7 = (bf16[32,2,64,128]{3,2,1,0:T(8,128)(2,1)S(1)}, bf16[32,2,64,128]{3,2,1,0:T(8,128)(2,1)}, u32[]{:S(2)}, u32[]{:S(2)}) collective-permute-start(bf16[32,2,64,128]{3,2,1,0:T(8,128)(2,1)S(1)} %collective-permute-done.4.refs_2_), channel_id=1, source_target_pairs={{0,1},{1,0},{2,3},{3,2},{4,5},{5,4},{6,7},{7,6},{8,9},{9,8},{10,11... | collective-permute-start | bytes 3145736 | tf_op jit(solution)/shard_map/ppermute | solution.py:225
  65.9 2.9 %all-to-all-done.1.refs_4_ = bf16[32,96,128]{2,1,0:T(8,128)(2,1)S(1)} async-done(((bf16[32,96,128]{2,1,0:T(8,128)(2,1)}), bf16[32,96,128]{2,1,0:T(8,128)(2,1)S(1)}, u32[]{:S(2)}, u32[]{:S(2)}) %all-to-all-start.1) | async-done | bytes 786464 | tf_op jit(solution)/shard_map/all_to_all | solution.py:255
  69.0 8.3 %all-to-all-start.2 = ((bf16[32,32,128]{2,1,0:T(8,128)(2,1)}), bf16[32,32,128]{2,1,0:T(8,128)(2,1)S(1)}, u32[]{:S(2)}, u32[]{:S(2)}) async-start(bf16[32,32,128]{2,1,0:T(8,128)(2,1)} %collective-permute-done.5), calls=%async_computation.2 | async-start | bytes 524288 | tf_op jit(solution)/shard_map/all_to_all | solution.py:258
  77.4 2.2 %collective-permute-start.8 = (bf16[32,96,128]{2,1,0:T(8,128)(2,1)S(1)}, bf16[32,96,128]{2,1,0:T(8,128)(2,1)}, u32[]{:S(2)}, u32[]{:S(2)}) collective-permute-start(bf16[32,96,128]{2,1,0:T(8,128)(2,1)S(1)} %all-to-all-done.1.refs_4_), channel_id=1, source_target_pairs={{0,1},{1,0},{2,3},{3,2},{4,5},{5,4},{6,7},{7,6},{8,9},{9,8},{10,11... | collective-permute-start | bytes 2359304 | tf_op jit(solution)/shard_map/ppermute | solution.py:225
  79.6 2.9 %collective-permute-done.9.refs_6_ = bf16[32,96,128]{2,1,0:T(8,128)(2,1)S(1)} collective-permute-done((bf16[32,96,128]{2,1,0:T(8,128)(2,1)S(1)}, bf16[32,96,128]{2,1,0:T(8,128)(2,1)S(1)}, u32[]{:S(2)}, u32[]{:S(2)}) %collective-permute-start.9) | collective-permute-done | bytes 786464 | tf_op jit(solution)/shard_map/ppermute | solution.py:228
  82.5 4.6 %all-to-all-done.2.refs_2_ = bf16[32,32,128]{2,1,0:T(8,128)(2,1)S(1)} async-done(((bf16[32,32,128]{2,1,0:T(8,128)(2,1)}), bf16[32,32,128]{2,1,0:T(8,128)(2,1)S(1)}, u32[]{:S(2)}, u32[]{:S(2)}) %all-to-all-start.2) | async-done | bytes 262176 | tf_op jit(solution)/shard_map/all_to_all | solution.py:258
  87.0 3.8 %collective-permute-start.10 = (bf16[32,96,128]{2,1,0:T(8,128)(2,1)S(1)}, bf16[32,96,128]{2,1,0:T(8,128)(2,1)}, u32[]{:S(2)}, u32[]{:S(2)}) collective-permute-start(bf16[32,96,128]{2,1,0:T(8,128)(2,1)S(1)} %collective-permute-done.9.refs_6_), channel_id=1, source_target_pairs={{0,1},{1,0},{2,3},{3,2},{4,5},{5,4},{6,7},{7,6},{8,9},{9,8},{10,11... | collective-permute-start | bytes 2359304 | tf_op jit(solution)/shard_map/ppermute | solution.py:225
  90.9 1.3 %collective-permute-start.12 = (bf16[32,32,128]{2,1,0:T(8,128)(2,1)S(1)}, bf16[32,32,128]{2,1,0:T(8,128)(2,1)S(1)}, u32[]{:S(2)}, u32[]{:S(2)}) collective-permute-start(bf16[32,32,128]{2,1,0:T(8,128)(2,1)S(1)} %all-to-all-done.2.refs_2_), channel_id=1, source_target_pairs={{0,2},{2,0},{1,3},{3,1},{4,6},{6,4},{5,7},{7,5},{8,10},{10,8},{9,1... | collective-permute-start | bytes 786440 | tf_op jit(solution)/shard_map/ppermute | solution.py:228
  92.8 5.7 %stack0.1 = (bf16[16,2,2,128,256]{4,3,2,1,0:T(8,128)(2,1)}, bf16[4,32,64,128]{3,2,1,0:T(8,128)(2,1)S(1)}, bf16[4,32,32,128]{3,2,1,0:T(8,128)(2,1)S(1)}) custom-call(s32[1]{0:T(128)} %bitcast.side_ref, s32[1]{0:T(128)} %bitcast.1.first_ref, s32[32]{0:T(128)S(1)} %reshape.55.mates_ref, f32[2,256,16]{2,1,0:T(8,128)S(1)} %bitcast.10, f32[32]{0:T(128)S(1)} %sqrt.3.norm_ref, ...), custom_call_target="tpu_custom_call" | custom-call | flops 5368709120 | bytes 8388608 | tf_op jit(solution)/shard_map/stack0/pallas_call | solution.py:199
  100.8 4.0 %stack1.1 = bf16[16,2,2,128,256]{4,3,2,1,0:T(8,128)(2,1)} custom-call(s32[1]{0:T(128)} %bitcast.side_ref, s32[1]{0:T(128)} %bitcast.1.first_ref, s32[32]{0:T(128)S(1)} %reshape.55.mates_ref, f32[2,256,16]{2,1,0:T(8,128)S(1)} %bitcast.11, f32[32]{0:T(128)S(1)} %sqrt.3.norm_ref, ...), custom_call_target="tpu_custom_call", output_to_operand_aliasing={{}: (11, {})} | custom-call | flops 5368709120 | bytes 8388608 | tf_op jit(solution)/shard_map/stack1/pallas_call | solution.py:199
  (37 shorter events, 6.8 us)
Async XLA Ops:
  0.0 21.4 %copy-start = (s32[2,64]{1,0:T(2,128)S(1)}, s32[2,64]{1,0:T(2,128)}, u32[]{:S(2)}) copy-start(s32[2,64]{1,0:T(2,128)} %param.5) | copy-start | bytes 1540
  0.0 15.5 %copy-start.1 = (bf16[1,128,32,2,128]{4,3,2,1,0:T(2,128)(2,1)S(1)}, bf16[1,128,32,2,128]{4,3,2,1,0:T(2,128)(2,1)}, u32[]{:S(2)}) copy-start(bf16[1,128,32,2,128]{4,3,2,1,0:T(2,128)(2,1)} %param.3) | copy-start | bytes 6291460
  0.0 20.0 %copy-start.4 = (s32[32,64]{1,0:T(8,128)S(1)}, s32[32,64]{1,0:T(8,128)}, u32[]{:S(2)}) copy-start(s32[32,64]{1,0:T(8,128)} %param.4) | copy-start | bytes 24580
  3.5 36.6 %all-to-all-start = ((bf16[32,2,64,128]{3,2,1,0:T(8,128)(2,1)}), bf16[32,2,64,128]{3,2,1,0:T(8,128)(2,1)}, u32[]{:S(2)}, u32[]{:S(2)}) async-start(bf16[32,2,64,128]{3,2,1,0:T(8,128)(2,1)} %get-tuple-element.27), calls=%async_computation | async-start | bytes 2097152 | tf_op jit(solution)/shard_map/all_to_all | solution.py:250
  15.5 0.8 copy-start.2
  16.6 0.7 copy-start.3
  17.3 19.5 %collective-permute-start = (bf16[32,96,128]{2,1,0:T(8,128)(2,1)S(1)}, bf16[32,96,128]{2,1,0:T(8,128)(2,1)}, u32[]{:S(2)}, u32[]{:S(2)}) collective-permute-start(bf16[32,96,128]{2,1,0:T(8,128)(2,1)S(1)} %get-tuple-element.29), channel_id=1, source_target_pairs={{0,130},{130,0},{2,128},{128,2},{1,131},{131,1},{3,129},{129,3},{4... | collective-permute-start | bytes 2359304 | tf_op jit(solution)/shard_map/ppermute | solution.py:231
  20.0 3.0 %collective-permute-start.2 = (s32[32,64]{1,0:T(8,128)S(1)}, s32[32,64]{1,0:T(8,128)S(1)}, u32[]{:S(2)}, u32[]{:S(2)}) collective-permute-start(s32[32,64]{1,0:T(8,128)S(1)} %copy-done.4), channel_id=1, source_target_pairs={{0,2},{2,0},{1,3},{3,1},{4,6},{6,4},{5,7},{7,5},{8,10},{10,8},{9,1... | collective-permute-start | bytes 24584 | tf_op jit(solution)/shard_map/ppermute | solution.py:228
  20.0 5.2 %collective-permute-start.1 = (s32[32,64]{1,0:T(8,128)S(1)}, s32[32,64]{1,0:T(8,128)S(1)}, u32[]{:S(2)}, u32[]{:S(2)}) collective-permute-start(s32[32,64]{1,0:T(8,128)S(1)} %copy-done.4), channel_id=1, source_target_pairs={{0,1},{1,0},{2,3},{3,2},{4,5},{5,4},{6,7},{7,6},{8,9},{9,8},{10,11... | collective-permute-start | bytes 24584 | tf_op jit(solution)/shard_map/ppermute | solution.py:225
  23.0 2.8 %collective-permute-start.3 = (s32[32,64]{1,0:T(8,128)S(1)}, s32[32,64]{1,0:T(8,128)S(1)}, u32[]{:S(2)}, u32[]{:S(2)}) collective-permute-start(s32[32,64]{1,0:T(8,128)S(1)} %collective-permute-done.2), channel_id=1, source_target_pairs={{0,1},{1,0},{2,3},{3,2},{4,5},{5,4},{6,7},{7,6},{8,9},{9,8},{10,11... | collective-permute-start | bytes 24584 | tf_op jit(solution)/shard_map/ppermute | solution.py:225
  40.1 19.9 %collective-permute-start.4 = (bf16[32,2,64,128]{3,2,1,0:T(8,128)(2,1)}, bf16[32,2,64,128]{3,2,1,0:T(8,128)(2,1)S(1)}, u32[]{:S(2)}, u32[]{:S(2)}) collective-permute-start(bf16[32,2,64,128]{3,2,1,0:T(8,128)(2,1)} %all-to-all-done.refs_0_), channel_id=1, source_target_pairs={{0,2},{2,0},{1,3},{3,1},{4,6},{6,4},{5,7},{7,5},{8,10},{10,8},{9,1... | collective-permute-start | bytes 3145736 | tf_op jit(solution)/shard_map/ppermute | solution.py:228
  41.4 27.4 %all-to-all-start.1 = ((bf16[32,96,128]{2,1,0:T(8,128)(2,1)}), bf16[32,96,128]{2,1,0:T(8,128)(2,1)S(1)}, u32[]{:S(2)}, u32[]{:S(2)}) async-start(bf16[32,96,128]{2,1,0:T(8,128)(2,1)} %collective-permute-done), calls=%async_computation.1 | async-start | bytes 1572864 | tf_op jit(solution)/shard_map/all_to_all | solution.py:255
  50.0 7.7 %collective-permute-start.5 = (bf16[32,32,128]{2,1,0:T(8,128)(2,1)}, bf16[32,32,128]{2,1,0:T(8,128)(2,1)}, u32[]{:S(2)}, u32[]{:S(2)}) collective-permute-start(bf16[32,32,128]{2,1,0:T(8,128)(2,1)} %copy-done.3), channel_id=1, source_target_pairs={{0,130},{130,0},{2,128},{128,2},{1,131},{131,1},{3,129},{129,3},{4... | collective-permute-start | bytes 786440 | tf_op jit(solution)/shard_map/ppermute | solution.py:231
  52.0 17.0 %collective-permute-start.6 = (bf16[32,2,64,128]{3,2,1,0:T(8,128)(2,1)}, bf16[32,2,64,128]{3,2,1,0:T(8,128)(2,1)}, u32[]{:S(2)}, u32[]{:S(2)}) collective-permute-start(bf16[32,2,64,128]{3,2,1,0:T(8,128)(2,1)} %all-to-all-done.refs_0_), channel_id=1, source_target_pairs={{0,1},{1,0},{2,3},{3,2},{4,5},{5,4},{6,7},{7,6},{8,9},{9,8},{10,11... | collective-permute-start | bytes 3145736 | tf_op jit(solution)/shard_map/ppermute | solution.py:225
  60.0 9.0 %collective-permute-start.7 = (bf16[32,2,64,128]{3,2,1,0:T(8,128)(2,1)S(1)}, bf16[32,2,64,128]{3,2,1,0:T(8,128)(2,1)}, u32[]{:S(2)}, u32[]{:S(2)}) collective-permute-start(bf16[32,2,64,128]{3,2,1,0:T(8,128)(2,1)S(1)} %collective-permute-done.4.refs_2_), channel_id=1, source_target_pairs={{0,1},{1,0},{2,3},{3,2},{4,5},{5,4},{6,7},{7,6},{8,9},{9,8},{10,11... | collective-permute-start | bytes 3145736 | tf_op jit(solution)/shard_map/ppermute | solution.py:225
  68.8 13.6 %collective-permute-start.9 = (bf16[32,96,128]{2,1,0:T(8,128)(2,1)S(1)}, bf16[32,96,128]{2,1,0:T(8,128)(2,1)S(1)}, u32[]{:S(2)}, u32[]{:S(2)}) collective-permute-start(bf16[32,96,128]{2,1,0:T(8,128)(2,1)S(1)} %all-to-all-done.1.refs_4_), channel_id=1, source_target_pairs={{0,2},{2,0},{1,3},{3,1},{4,6},{6,4},{5,7},{7,5},{8,10},{10,8},{9,1... | collective-permute-start | bytes 2359304 | tf_op jit(solution)/shard_map/ppermute | solution.py:228
  69.0 18.0 %all-to-all-start.2 = ((bf16[32,32,128]{2,1,0:T(8,128)(2,1)}), bf16[32,32,128]{2,1,0:T(8,128)(2,1)S(1)}, u32[]{:S(2)}, u32[]{:S(2)}) async-start(bf16[32,32,128]{2,1,0:T(8,128)(2,1)} %collective-permute-done.5), calls=%async_computation.2 | async-start | bytes 524288 | tf_op jit(solution)/shard_map/all_to_all | solution.py:258
  77.4 15.2 %collective-permute-start.8 = (bf16[32,96,128]{2,1,0:T(8,128)(2,1)S(1)}, bf16[32,96,128]{2,1,0:T(8,128)(2,1)}, u32[]{:S(2)}, u32[]{:S(2)}) collective-permute-start(bf16[32,96,128]{2,1,0:T(8,128)(2,1)S(1)} %all-to-all-done.1.refs_4_), channel_id=1, source_target_pairs={{0,1},{1,0},{2,3},{3,2},{4,5},{5,4},{6,7},{7,6},{8,9},{9,8},{10,11... | collective-permute-start | bytes 2359304 | tf_op jit(solution)/shard_map/ppermute | solution.py:225
  87.0 5.8 %collective-permute-start.10 = (bf16[32,96,128]{2,1,0:T(8,128)(2,1)S(1)}, bf16[32,96,128]{2,1,0:T(8,128)(2,1)}, u32[]{:S(2)}, u32[]{:S(2)}) collective-permute-start(bf16[32,96,128]{2,1,0:T(8,128)(2,1)S(1)} %collective-permute-done.9.refs_6_), channel_id=1, source_target_pairs={{0,1},{1,0},{2,3},{3,2},{4,5},{5,4},{6,7},{7,6},{8,9},{9,8},{10,11... | collective-permute-start | bytes 2359304 | tf_op jit(solution)/shard_map/ppermute | solution.py:225
  90.9 7.9 %collective-permute-start.12 = (bf16[32,32,128]{2,1,0:T(8,128)(2,1)S(1)}, bf16[32,32,128]{2,1,0:T(8,128)(2,1)S(1)}, u32[]{:S(2)}, u32[]{:S(2)}) collective-permute-start(bf16[32,32,128]{2,1,0:T(8,128)(2,1)S(1)} %all-to-all-done.2.refs_2_), channel_id=1, source_target_pairs={{0,2},{2,0},{1,3},{3,1},{4,6},{6,4},{5,7},{7,5},{8,10},{10,8},{9,1... | collective-permute-start | bytes 786440 | tf_op jit(solution)/shard_map/ppermute | solution.py:228
  92.2 7.4 %collective-permute-start.11 = (bf16[32,32,128]{2,1,0:T(8,128)(2,1)S(1)}, bf16[32,32,128]{2,1,0:T(8,128)(2,1)S(1)}, u32[]{:S(2)}, u32[]{:S(2)}) collective-permute-start(bf16[32,32,128]{2,1,0:T(8,128)(2,1)S(1)} %all-to-all-done.2.refs_2_), channel_id=1, source_target_pairs={{0,1},{1,0},{2,3},{3,2},{4,5},{5,4},{6,7},{7,6},{8,9},{9,8},{10,11... | collective-permute-start | bytes 786440 | tf_op jit(solution)/shard_map/ppermute | solution.py:225
  98.9 1.9 %collective-permute-start.13 = (bf16[32,32,128]{2,1,0:T(8,128)(2,1)S(1)}, bf16[32,32,128]{2,1,0:T(8,128)(2,1)S(1)}, u32[]{:S(2)}, u32[]{:S(2)}) collective-permute-start(bf16[32,32,128]{2,1,0:T(8,128)(2,1)S(1)} %collective-permute-done.12.refs_4_), channel_id=1, source_target_pairs={{0,1},{1,0},{2,3},{3,2},{4,5},{5,4},{6,7},{7,6},{8,9},{9,8},{10,11... | collective-permute-start | bytes 786440 | tf_op jit(solution)/shard_map/ppermute | solution.py:225
